TPU v7x, 128 devices: a whole 4x4x4 slice. The times are simulated.
128 devices in a mesh: lat: 16 (over z, x), lon: 8 (over y, core).
Axes of the slice: x: 4, y: 4, z: 4, core: 2. Of those that a mesh axis runs over, the one named last changes fastest.
Arguments:
- grid: bfloat16 [128, 512, 512], P('lat', 'lon'), may hold values from -6 to 6
- mesh_nodes: bfloat16 [16, 8, 256, 512], P('lat', 'lon'), may hold values from -6 to 6
- grid_cot: bfloat16 [128, 512, 512], P('lat', 'lon'), may hold values from -6 to 6
- enc_send: bfloat16 [512, 512], replicated, may hold values from -0.25 to 0.25
- enc_recv: bfloat16 [512, 512], replicated, may hold values from -0.25 to 0.25
- enc_out: bfloat16 [512, 512], replicated, may hold values from -0.25 to 0.25
- dec_send: bfloat16 [512, 512], replicated, may hold values from -0.25 to 0.25
- dec_recv: bfloat16 [512, 512], replicated, may hold values from -0.25 to 0.25
- dec_out: bfloat16 [512, 512], replicated, may hold values from -0.25 to 0.25
- enc_src: int32 [16, 8, 256, 32], P('lat', 'lon'), may hold values from 0 to 65535, as said below
- enc_live: int32 [16, 8, 256, 32], P('lat', 'lon'), may hold values from 0 to 1, as said below
- dec_src: int32 [3, 128, 512], P(None, 'lat', 'lon'), may hold values from 0 to 32767, as said below
Outputs:
- grid_new: bfloat16 [128, 512, 512], P('lat', 'lon')
- grid_grad: bfloat16 [128, 512, 512], P('lat', 'lon')
- mesh_grad: bfloat16 [16, 8, 256, 512], P('lat', 'lon')
- enc_send_grad: float32 [512, 512], replicated
- enc_recv_grad: float32 [512, 512], replicated
- enc_out_grad: float32 [512, 512], replicated
- dec_send_grad: float32 [512, 512], replicated
- dec_recv_grad: float32 [512, 512], replicated
- dec_out_grad: float32 [512, 512], replicated
Inputs may be any that keep to these rules, and one draw needn't show every extreme that they name: `enc_src`: every sender named by the mesh nodes of block (a, b), padded slots included, lies in grid rows a * 8 - 4 to (a + 1) * 8 + 3 and, cyclically, columns b * 64 - 4 to (b + 1) * 64 + 3; these bounds are reached. `enc_live`: the live slots of a mesh node are its first ones, 2 to 32 of them; some node has all 32. `dec_src`: the block (a, b) of every sender of a grid node is at most one block from the node's own block in latitude and, cyclically, in longitude; offsets of one are reached both ways.
All inputs are finite; a program needn't handle non-finite values.
Results may differ from a plain program's by a relative error of at most 0.013.
Values may be sent and summed in bfloat16 or wider, within the bound.
No kernel may reach another device: no remote copies, remote signals or barrier semaphores. Data moves between devices by JAX's collectives and lax.ppermute only.
A program may use at most 192 MiB of HBM per device.

v0:
```python
import jax
import jax.numpy as jnp
from jax import lax
from jax.experimental import pallas as pl
from jax.experimental.pallas import tpu as pltpu
from jax.sharding import PartitionSpec as P

REACH = 4
NORM_EPSILON = 1e-05
BF = jnp.bfloat16
F32 = jnp.float32
VMEM_LIMIT = 56 * 1024 * 1024
ENC_TILE = 32
ENC_CHUNK = 4
STRIP = 16
DEC_TILE = 256


def dot(a, b):
    return jnp.dot(a, b, preferred_element_type=F32)


def dot_nt(a, b):
    return lax.dot_general(a, b, (((1,), (1,)), ((), ())), preferred_element_type=F32)


def dot_tn(a, b):
    return lax.dot_general(a, b, (((0,), (0,)), ((), ())), preferred_element_type=F32)


def sigma(v):
    return 0.5 * jnp.tanh(0.5 * v) + 0.5


def normalise(message):
    centred = message - jnp.mean(message, axis=-1, keepdims=True)
    factor = lax.rsqrt(jnp.mean(centred * centred, axis=-1, keepdims=True) + NORM_EPSILON)
    return centred, factor


def one_hot(index, places):
    return jnp.where(index == places, BF(1.0), BF(0.0))


def places_of(shape, dim):
    return lax.broadcasted_iota(jnp.int32, shape, dim).astype(jnp.int16)


def staggered(stages, count):
    for i in range(count + len(stages) - 1):
        for d in range(len(stages) - 1, -1, -1):
            if 0 <= i - d < count:
                stages[d](i - d)


def kernel_params():
    return pltpu.CompilerParams(vmem_limit_bytes=VMEM_LIMIT)


def whole(shape):
    return pl.BlockSpec(shape, lambda t: (0,) * len(shape))


def rows_of(count, width):
    return pl.BlockSpec((count, width), lambda t: (t, 0))


def enc_forward_kernel(
    idx_ref, count_ref, mesh_ref, own_ref, high_ref, low_ref, left_ref, right_ref,
    send_ref, recv_ref, out_ref, dec_send_ref,
    new_ref, moved_ref, slope_ref, hidden_ref, normed_ref, scale_ref,
    band, onehot, received_all,
):
    step = pl.program_id(0)
    tile, degree = idx_ref.shape
    width = mesh_ref.shape[1]
    band_rows = band.shape[0]
    own = pl.ds(pl.multiple_of(step * tile, tile), tile)

    @pl.when(step == 0)
    def _():
        received_all[...] = dot(mesh_ref[...], recv_ref[...])
        at = 0
        for piece in (own_ref, high_ref, low_ref, left_ref, right_ref):
            count = piece.shape[0]
            band[at : at + count, :] = dot(piece[...], send_ref[...]).astype(BF)
            at += count

    places = places_of((tile, band_rows), 1)
    index = idx_ref[...].astype(jnp.int16)
    received = received_all[own, :]
    lane = lax.broadcasted_iota(jnp.int32, (tile, degree), 1)
    rows = ENC_CHUNK * tile
    state = {"total": jnp.zeros((tile, width), F32), "scales": jnp.zeros((tile, degree), F32)}
    held = {}

    def place(c):
        for k in range(c * ENC_CHUNK, (c + 1) * ENC_CHUNK):
            onehot[k * tile : (k + 1) * tile, :] = one_hot(index[:, k : k + 1], places)

    def gather(c):
        held["gathered", c] = dot(onehot[c * rows : (c + 1) * rows, :], band[...])

    def activate(c):
        before = held.pop(("gathered", c)).reshape(ENC_CHUNK, tile, width) + received[None]
        sig = sigma(before)
        silu = before * sig
        part = slice(c * rows, (c + 1) * rows)
        slope_ref[part, :] = (sig + silu * (1.0 - sig)).reshape(rows, width).astype(BF)
        hidden = silu.reshape(rows, width).astype(BF)
        hidden_ref[part, :] = hidden
        held["hidden", c] = hidden

    def project(c):
        held["message", c] = dot(held.pop(("hidden", c)), out_ref[...])

    def norm(c):
        centred, factor = normalise(held.pop(("message", c)))
        normed = (centred * factor).reshape(ENC_CHUNK, tile, width)
        normed_ref[c * rows : (c + 1) * rows, :] = normed.reshape(rows, width).astype(BF)
        factor = factor.reshape(ENC_CHUNK, tile, 1)
        for j in range(ENC_CHUNK):
            k = c * ENC_CHUNK + j
            live = jnp.where(count_ref[...] > k, 1.0, 0.0)
            state["total"] = state["total"] + normed[j] * live
            state["scales"] = jnp.where(lane == k, factor[j] * live, state["scales"])

    staggered([place, gather, activate, project, norm], degree // ENC_CHUNK)
    scale_ref[...] = state["scales"]
    nodes = mesh_ref[own, :].astype(F32)
    new_ref[own, :] = (nodes + degree ** (-0.5) * state["total"]).astype(BF)

    @pl.when(step == pl.num_programs(0) - 1)
    def _():
        moved_ref[...] = dot(new_ref[...], dec_send_ref[...]).astype(BF)


def enc_forward(idx, counts, mesh_rows, pieces, enc_send, enc_recv, enc_out, dec_send):
    nodes, degree = idx.shape
    width = mesh_rows.shape[1]
    tile = ENC_TILE
    edges = tile * degree
    band_rows = sum(p.shape[0] for p in pieces)
    square = whole((width, width))
    return pl.pallas_call(
        enc_forward_kernel,
        name="enc_forward",
        grid=(nodes // tile,),
        in_specs=[rows_of(tile, degree), rows_of(tile, 1), whole((nodes, width))]
        + [whole(p.shape) for p in pieces]
        + [square] * 4,
        out_specs=[
            whole((nodes, width)), whole((nodes, width)),
            rows_of(edges, width), rows_of(edges, width), rows_of(edges, width), rows_of(tile, degree),
        ],
        out_shape=[
            jax.ShapeDtypeStruct((nodes, width), BF),
            jax.ShapeDtypeStruct((nodes, width), BF),
            jax.ShapeDtypeStruct((nodes * degree, width), BF),
            jax.ShapeDtypeStruct((nodes * degree, width), BF),
            jax.ShapeDtypeStruct((nodes * degree, width), BF),
            jax.ShapeDtypeStruct((nodes, degree), F32),
        ],
        scratch_shapes=[
            pltpu.VMEM((band_rows, width), BF),
            pltpu.VMEM((edges, band_rows), BF),
            pltpu.VMEM((nodes, width), F32),
        ],
        compiler_params=kernel_params(),
    )(idx, counts, mesh_rows, *pieces, enc_send, enc_recv, enc_out, dec_send)


def enc_between_kernel(normed_ref, out_ref, *refs):
    refs[-1][...] = dot_nt(normed_ref[...], out_ref[...]).astype(BF)


def enc_between(normed, enc_out, first, count, rows, done=None):
    width = normed.shape[1]
    per_edge = pl.BlockSpec((rows, width), lambda t: (t + first, 0))
    share = count * rows * width
    kept = () if done is None else (done,)
    return pl.pallas_call(
        enc_between_kernel,
        name="enc_between",
        grid=(count,),
        in_specs=[per_edge, whole((width, width))] + [pl.BlockSpec(memory_space=pl.ANY)] * len(kept),
        out_specs=per_edge,
        out_shape=jax.ShapeDtypeStruct(normed.shape, BF),
        input_output_aliases={2: 0} if kept else {},
        compiler_params=kernel_params(),
        cost_estimate=pl.CostEstimate(flops=2 * share * width, bytes_accessed=4 * share, transcendentals=0),
    )(normed, enc_out, *kept)


def decoder_kernel(
    idx_ref, idx_row_ref, grid_ref, cot_ref, centre_ref, left_ref, right_ref,
    recv_ref, out_ref,
    new_ref, hidden_ref, message_cot_ref, before_cot_ref, received_cot_ref, left_tot_ref, right_tot_ref,
    onehot, onehot_t, received_all, new_all, received_cot_all,
):
    nodes, width = grid_ref.shape
    degree = idx_ref.shape[1]
    third = centre_ref.shape[0]
    tile = DEC_TILE
    parts = nodes // tile
    index = idx_ref[...].astype(jnp.int16)
    places = places_of((tile, 3 * third), 1)
    held = {}

    received_all[...] = dot(grid_ref[...], recv_ref[...])

    def spot(i):
        h, j = divmod(i, degree)
        return j, slice(h * tile, (h + 1) * tile), slice(i * tile, (i + 1) * tile)

    def place(i):
        j, at, edges = spot(i)
        onehot[edges, :] = one_hot(index[at, j : j + 1], places)

    def gather(i):
        j, at, edges = spot(i)
        gathered = dot(onehot[edges, :third], centre_ref[...])
        gathered = gathered + dot(onehot[edges, third : 2 * third], left_ref[...])
        held["gathered", i] = gathered + dot(onehot[edges, 2 * third :], right_ref[...])

    def activate(i):
        j, at, edges = spot(i)
        before = held.pop(("gathered", i)) + received_all[at, :]
        sig = sigma(before)
        silu = before * sig
        hidden = silu.astype(BF)
        hidden_ref[edges, :] = hidden
        held["slope", i] = sig + silu * (1.0 - sig)
        held["message", i] = dot(hidden, out_ref[...])

    def norm(i):
        j, at, edges = spot(i)
        centred, factor = normalise(held.pop(("message", i)))
        normed = centred * factor
        cot = cot_ref[at, :].astype(F32)
        level = cot - jnp.mean(cot, axis=-1, keepdims=True)
        along = jnp.mean(cot * normed, axis=-1, keepdims=True)
        message_cot = (factor * (level - normed * along)).astype(BF)
        message_cot_ref[edges, :] = message_cot
        held["hidden_cot", i] = dot_nt(message_cot, out_ref[...])
        if j == 0:
            new_all[at, :] = grid_ref[at, :].astype(F32) + normed
        else:
            new_all[at, :] += normed

    def back(i):
        j, at, edges = spot(i)
        before_cot = held.pop(("hidden_cot", i)) * held.pop(("slope", i))
        before_cot_ref[edges, :] = before_cot.astype(BF)
        if j == 0:
            received_cot_all[at, :] = before_cot
        else:
            received_cot_all[at, :] += before_cot
        rows = lax.broadcasted_iota(jnp.int32, (2 * third, tile), 0) + third
        picks = jnp.broadcast_to(idx_row_ref[j : j + 1, at], (16, tile)).astype(jnp.int16)[:1]
        onehot_t[:, edges] = one_hot(picks, rows.astype(jnp.int16))

    staggered([place, gather, activate, norm, back], degree * parts)
    left_tot_ref[...] = dot(onehot_t[:third, :], before_cot_ref[...]).astype(BF)
    new_ref[...] = new_all[...].astype(BF)
    right_tot_ref[...] = dot(onehot_t[third:, :], before_cot_ref[...]).astype(BF)
    received_cot_ref[...] = received_cot_all[...].astype(BF)


def decoder(idx, idx_rows, grid_rows, cot_rows, centre, left, right, dec_recv, dec_out):
    nodes, width = grid_rows.shape
    degree = idx.shape[1]
    third = centre.shape[0]
    edge_shape = jax.ShapeDtypeStruct((degree * nodes, width), BF)
    node_shape = jax.ShapeDtypeStruct((nodes, width), BF)
    side_shape = jax.ShapeDtypeStruct((third, width), BF)
    return pl.pallas_call(
        decoder_kernel,
        name="decoder",
        out_shape=[node_shape, edge_shape, edge_shape, edge_shape, node_shape, side_shape, side_shape],
        scratch_shapes=[
            pltpu.VMEM((degree * nodes, 3 * third), BF),
            pltpu.VMEM((2 * third, degree * nodes), BF),
            pltpu.VMEM((nodes, width), F32),
            pltpu.VMEM((nodes, width), F32),
            pltpu.VMEM((nodes, width), F32),
        ],
        compiler_params=kernel_params(),
    )(idx, idx_rows, grid_rows, cot_rows, centre, left, right, dec_recv, dec_out)


def decoder_rest_kernel(
    idx_row_ref, grid_ref, cot_ref, hidden_ref, message_cot_ref, before_cot_ref, received_cot_ref, recv_ref,
    part_ref, out_grad_ref, recv_grad_ref, centre_tot_ref,
    onehot_t,
):
    third, width = centre_tot_ref.shape
    degree, nodes = idx_row_ref.shape
    tile = DEC_TILE
    rows = places_of((third, tile), 0)
    for i in range(degree * nodes // tile):
        h, j = divmod(i, degree)
        picks = jnp.broadcast_to(idx_row_ref[j : j + 1, h * tile : (h + 1) * tile], (16, tile))
        onehot_t[:, i * tile : (i + 1) * tile] = one_hot(picks.astype(jnp.int16)[:1], rows)
    centre_tot_ref[...] = dot(onehot_t[...], before_cot_ref[...]).astype(BF)
    out_grad_ref[...] = dot_tn(hidden_ref[...], message_cot_ref[...]).astype(BF)
    received_cot = received_cot_ref[...]
    recv_grad_ref[...] = dot_tn(grid_ref[...], received_cot).astype(BF)
    part_ref[...] = cot_ref[...].astype(F32) + dot_nt(received_cot, recv_ref[...])


def decoder_rest(idx_rows, grid_rows, cot_rows, hidden, message_cot, before_cot, received_cot, dec_recv, third):
    degree, nodes = idx_rows.shape
    width = hidden.shape[1]
    return pl.pallas_call(
        decoder_rest_kernel,
        name="decoder_rest",
        out_shape=[
            jax.ShapeDtypeStruct((nodes, width), F32),
            jax.ShapeDtypeStruct((width, width), BF),
            jax.ShapeDtypeStruct((width, width), BF),
            jax.ShapeDtypeStruct((third, width), BF),
        ],
        scratch_shapes=[pltpu.VMEM((third, degree * nodes), BF)],
        compiler_params=kernel_params(),
        cost_estimate=pl.CostEstimate(
            flops=2 * degree * nodes * width * (third + 2 * width), bytes_accessed=8 * degree * nodes * width,
            transcendentals=0,
        ),
    )(idx_rows, grid_rows, cot_rows, hidden, message_cot, before_cot, received_cot, dec_recv)


def enc_backward_kernel(
    idx_row_ref, scale_ref, mesh_ref, moved_cot_ref, normed_ref, turned_ref, slope_ref, hidden_ref,
    own_ref, high_ref, low_ref, left_ref, right_ref,
    dec_send_ref, recv_ref, out_ref,
    mesh_grad_ref, band_cot_ref, grads_ref,
    onehot_t0, onehot_t1, cot0, cot1, message_cot, totals, out_acc, node_cot, levels, turned_level, received_cot,
):
    step = pl.program_id(0)
    nodes, width = mesh_ref.shape
    edges = normed_ref.shape[0]
    band_rows = totals.shape[0]
    tiles = pl.num_programs(0) - 1
    tile = ENC_TILE
    degree = edges // tile
    scaling = degree ** (-0.5)
    cots = (cot0, cot1)
    onehots = (onehot_t0, onehot_t1)

    @pl.when(step == 0)
    def _():
        totals[...] = jnp.zeros_like(totals)
        cot = dot_nt(moved_cot_ref[...], dec_send_ref[...])
        node_cot[...] = cot
        spread = scaling * cot
        level = spread - jnp.mean(spread, axis=-1, keepdims=True)
        levels[...] = level
        turned_level[...] = dot_nt(level.astype(BF), out_ref[...])
        out_acc[...] = jnp.zeros_like(out_acc)

    def scatter(slot, n):
        half = width // 2
        at = slice(n * half, (n + 1) * half)
        totals[:, at] += dot(onehots[slot][...], cots[slot][:, at])

    def edge_part(slot, beside):
        strips = tile // STRIP
        total = [jnp.zeros((STRIP, width), F32)] * strips
        scales = scale_ref[...]
        for n in range(2):
            if beside is not None:
                scatter(beside, n)
            for k in range(n * degree // 2, (n + 1) * degree // 2):
                for i in range(strips):
                    at = slice(k * tile + i * STRIP, k * tile + (i + 1) * STRIP)
                    mine = pl.ds(pl.multiple_of(step * tile + i * STRIP, STRIP), STRIP)
                    spread = scaling * node_cot[mine, :]
                    normed = normed_ref[at, :].astype(F32)
                    along = jnp.mean(spread * normed, axis=-1, keepdims=True)
                    scale = scales[i * STRIP : (i + 1) * STRIP, k : k + 1]
                    message_cot[at, :] = (scale * (levels[mine, :] - along * normed)).astype(BF)
                    turned = scale * (turned_level[mine, :] - along * turned_ref[at, :].astype(F32))
                    before_cot = slope_ref[at, :].astype(F32) * turned
                    total[i] = total[i] + before_cot
                    cots[slot][at, :] = before_cot.astype(BF)
            part = slice(n * edges // 2, (n + 1) * edges // 2)
            out_acc[...] += dot_tn(hidden_ref[part, :], message_cot[part, :])
        places = places_of((band_rows, edges), 0)
        spot = jnp.broadcast_to(idx_row_ref[0], (16, edges)).astype(jnp.int16)[:1]
        onehots[slot][...] = one_hot(spot, places)
        received_cot[pl.ds(pl.multiple_of(step * tile, tile), tile), :] = jnp.concatenate(total, axis=0).astype(BF)

    @pl.when(step == 0)
    def _():
        edge_part(0, None)

    for parity in range(2):
        @pl.when((step > 0) & (step < tiles) & (step % 2 == parity))
        def _():
            edge_part(parity, 1 - parity)

    @pl.when(step == tiles)
    def _():
        scatter(1, 0)
        scatter(1, 1)
        grads_ref[width : 2 * width, :] = dot_tn(mesh_ref[...], received_cot[...]).astype(BF)
        grads_ref[2 * width :, :] = out_acc[...].astype(BF)
        mesh_grad_ref[...] = (node_cot[...] + dot_nt(received_cot[...], recv_ref[...])).astype(BF)
        band_cot_ref[...] = totals[...].astype(BF)
        at = 0
        send_grad = jnp.zeros((width, width), F32)
        for piece in (own_ref, high_ref, low_ref, left_ref, right_ref):
            count = piece.shape[0]
            send_grad = send_grad + dot_tn(piece[...], band_cot_ref[at : at + count, :])
            at += count
        grads_ref[:width, :] = send_grad.astype(BF)


def enc_backward(idx_rows, scale, mesh_rows, moved_cot, normed, turned, slope, hidden, pieces, dec_send, enc_recv, enc_out):
    nodes, width = mesh_rows.shape
    degree = scale.shape[1]
    tile = ENC_TILE
    tiles = nodes // tile
    assert tiles % 2 == 0
    edges = normed.shape[0] // tiles
    band_rows = sum(p.shape[0] for p in pieces)
    square = whole((width, width))
    last = tiles - 1
    per_node = whole((nodes, width))
    per_edge = pl.BlockSpec((edges, width), lambda t: (jnp.minimum(t, last), 0))
    return pl.pallas_call(
        enc_backward_kernel,
        name="enc_backward",
        grid=(tiles + 1,),
        in_specs=[
            pl.BlockSpec((1, 1, edges), lambda t: (jnp.minimum(t, last), 0, 0)),
            pl.BlockSpec((tile, degree), lambda t: (jnp.minimum(t, last), 0)),
        ]
        + [per_node] * 2
        + [per_edge] * 4
        + [whole(p.shape) for p in pieces]
        + [square] * 3,
        out_specs=[per_node, whole((band_rows, width)), whole((3 * width, width))],
        out_shape=[
            jax.ShapeDtypeStruct((nodes, width), BF),
            jax.ShapeDtypeStruct((band_rows, width), BF),
            jax.ShapeDtypeStruct((3 * width, width), BF),
        ],
        scratch_shapes=[
            pltpu.VMEM((band_rows, edges), BF),
            pltpu.VMEM((band_rows, edges), BF),
            pltpu.VMEM((edges, width), BF),
            pltpu.VMEM((edges, width), BF),
            pltpu.VMEM((edges, width), BF),
            pltpu.VMEM((band_rows, width), F32),
            pltpu.VMEM((width, width), F32),
            pltpu.VMEM((nodes, width), F32),
            pltpu.VMEM((nodes, width), F32),
            pltpu.VMEM((nodes, width), F32),
            pltpu.VMEM((nodes, width), BF),
        ],
        compiler_params=kernel_params(),
    )(idx_rows, scale, mesh_rows, moved_cot, normed, turned, slope, hidden, *pieces, dec_send, enc_recv, enc_out)


def to_lon(shard, by):
    count = lax.axis_size("lon")
    return lax.ppermute(shard, "lon", [(i, (i + by) % count) for i in range(count)])


def to_lat(shard, by):
    count = lax.axis_size("lat")
    return lax.ppermute(shard, "lat", [(i, i + by) for i in range(count) if 0 <= i + by < count])


def core_swap(array):
    return lax.ppermute(array, "lon", [(i, i ^ 1) for i in range(lax.axis_size("lon"))])


def across_chips(parts):
    count = lax.axis_size("lat") * lax.axis_size("lon")
    alike = [[i for i in range(count) if i % 2 == c] for c in range(2)]
    return lax.all_to_all(parts, ("lat", "lon"), 0, 0, axis_index_groups=alike, tiled=True)


def on_device(
    grid, mesh_nodes, grid_cot, enc_send, enc_recv, enc_out, dec_send, dec_recv, dec_out,
    enc_src, enc_live, dec_src,
):
    lat_cells, lon_cells, width = grid.shape
    slots, degree = enc_src.shape[2:]
    lat_index = lax.axis_index("lat")
    lon_index = lax.axis_index("lon")
    lon_count = lax.axis_size("lon")
    lon_total = lon_cells * lon_count
    cells = lat_cells * lon_cells
    edge_rows = REACH * lon_cells
    tall = lat_cells + 2 * REACH

    grid_rows = grid.reshape(cells, width)
    mesh_rows = mesh_nodes.reshape(slots, width)
    high = to_lat(grid_rows[:edge_rows], -1)
    low = to_lat(grid_rows[cells - edge_rows :], 1)
    inner = jnp.concatenate([grid_rows, high, low], axis=0).reshape(tall, lon_cells, width)
    left = to_lon(inner[:, lon_cells - REACH :].reshape(tall * REACH, width), 1)
    right = to_lon(inner[:, :REACH].reshape(tall * REACH, width), -1)
    pieces = (grid_rows, high, low, left, right)

    source = enc_src.reshape(slots, degree)
    row = (source // lon_total - lat_index * lat_cells) % tall
    col = (source % lon_total - lon_index * lon_cells + REACH) % lon_total - REACH
    inner_rows = tall * lon_cells
    enc_idx = jnp.where(
        col < 0,
        inner_rows + row * REACH + col + REACH,
        jnp.where(
            col >= lon_cells,
            inner_rows + tall * REACH + row * REACH + col - lon_cells,
            row * lon_cells + col,
        ),
    )
    tiles = slots // ENC_TILE
    enc_idx_rows = enc_idx.reshape(tiles, ENC_TILE, degree).transpose(0, 2, 1)
    enc_idx_rows = enc_idx_rows.reshape(tiles, 1, ENC_TILE * degree)
    counts = jnp.sum(enc_live.reshape(slots, degree), axis=1, keepdims=True)

    picks = dec_src.reshape(3, cells)
    owner = picks // slots
    owner_lat = (owner // lon_count - lat_index) % 3
    owner_lon = (owner % lon_count - lon_index + lon_count) % lon_count
    owner_lon = jnp.where(owner_lon == lon_count - 1, 1, owner_lon * 2)
    dec_idx_rows = (owner_lon * 3 + owner_lat) * slots + picks % slots

    mesh_new, moved, slope, hidden, normed, scale = enc_forward(
        enc_idx, counts, mesh_rows, pieces, enc_send, enc_recv, enc_out, dec_send
    )

    above = to_lat(moved, -1)
    below = to_lat(moved, 1)
    half = slots * degree // 2
    block = half // 4
    part = enc_between(normed, enc_out, 0, 4, block)
    centre = jnp.concatenate([moved, above, below], axis=0)
    centre, part = lax.optimization_barrier((centre, part))
    west = to_lon(centre, 1)
    east = to_lon(centre, -1)
    turned = enc_between(normed, enc_out, 4, 4, block, part)
    west, east, turned = lax.optimization_barrier((west, east, turned))
    cot_rows = grid_cot.reshape(cells, width)
    grid_new, dec_hidden, dec_message_cot, dec_before_cot, dec_received_cot, west_tot, east_tot = decoder(
        dec_idx_rows.T, dec_idx_rows, grid_rows, cot_rows, centre, west, east, dec_recv, dec_out
    )
    from_east = to_lon(west_tot, -1)
    from_west = to_lon(east_tot, 1)
    grid_part, dec_out_grad, dec_recv_grad, centre_tot = decoder_rest(
        dec_idx_rows, grid_rows, cot_rows, dec_hidden, dec_message_cot, dec_before_cot, dec_received_cot,
        dec_recv, 3 * slots,
    )
    column = centre_tot.astype(F32) + from_east.astype(F32) + from_west.astype(F32)
    from_below = to_lat(column[slots : 2 * slots].astype(BF), 1)
    from_above = to_lat(column[2 * slots :].astype(BF), -1)
    moved_cot = column[:slots] + from_below.astype(F32) + from_above.astype(F32)
    moved_cot = moved_cot.astype(BF)
    dec_send_grad = dot_tn(mesh_new, moved_cot).astype(BF)

    mesh_grad, band_cot, enc_stack = enc_backward(
        enc_idx_rows, scale, mesh_rows, moved_cot, normed, turned, slope, hidden, pieces, dec_send, enc_recv, enc_out
    )
    dec_stack = jnp.concatenate([dec_send_grad, dec_recv_grad, dec_out_grad], axis=0)

    side = tall * REACH
    from_right = to_lon(band_cot[inner_rows : inner_rows + side], -1)
    from_left = to_lon(band_cot[inner_rows + side :], 1)

    leads = lon_index % 2 == 0
    chips = lax.axis_size("lat") * lon_count // 2
    swapped = core_swap(jnp.where(leads, dec_stack, enc_stack))
    kept = jnp.where(leads, enc_stack, dec_stack).astype(F32) + swapped.astype(F32)
    kept = kept.astype(BF).reshape(chips, 3 * width // chips, width)
    kept, from_right, from_left = lax.optimization_barrier((kept, from_right, from_left))

    inner_cot = band_cot[:inner_rows].astype(F32).reshape(tall, lon_cells, width)
    inner_cot = inner_cot.at[:, lon_cells - REACH :].add(from_right.astype(F32).reshape(tall, REACH, width))
    inner_cot = inner_cot.at[:, :REACH].add(from_left.astype(F32).reshape(tall, REACH, width))
    inner_cot = inner_cot.reshape(inner_rows, width)
    from_low = to_lat(inner_cot[cells : cells + edge_rows].astype(BF), 1)
    from_high = to_lat(inner_cot[cells + edge_rows :].astype(BF), -1)

    mine = jnp.sum(across_chips(kept).astype(F32), axis=0).astype(BF)
    mine, from_low, from_high = lax.optimization_barrier((mine, from_low, from_high))
    ours = across_chips(jnp.broadcast_to(mine[None], kept.shape)).reshape(3 * width, width)
    theirs = core_swap(ours)
    enc_grads = jnp.where(leads, ours, theirs).astype(F32)
    dec_grads = jnp.where(leads, theirs, ours).astype(F32)

    sent_cot = inner_cot[:cells] + jnp.concatenate([from_low, from_high], axis=0).astype(F32)
    grid_grad = (grid_part + dot_nt(sent_cot.astype(BF), enc_send)).astype(BF)

    return (
        grid_new.reshape(grid.shape),
        grid_grad.reshape(grid.shape),
        mesh_grad.reshape(mesh_nodes.shape),
        enc_grads[:width],
        enc_grads[width : 2 * width],
        enc_grads[2 * width :],
        dec_grads[:width],
        dec_grads[width : 2 * width],
        dec_grads[2 * width :],
    )


def solution(mesh):
    node = P("lat", "lon", None)
    block = P("lat", "lon", None, None)
    placed = (
        node, block, node, P(), P(), P(), P(), P(), P(), block, block, P(None, "lat", "lon"),
    )
    return jax.shard_map(
        on_device,
        mesh=mesh,
        in_specs=placed,
        out_specs=(node, node, block, P(), P(), P(), P(), P(), P()),
        check_vma=False,
    )
```

profile of v0, /device:TPU:1, one launch (start us, length us, event | category | flops | bytes accessed | tf_op | source)
XLA Modules:
  0.0 240.3 jit_solution(8652696969355463990)
XLA Ops:
  1.8 1.3 collective-permute-start
  3.1 4.6 %collective-permute-start.1 = (bf16[256,512]{1,0:T(8,128)(2,1)S(1)}, bf16[256,512]{1,0:T(8,128)(2,1)S(1)}, u32[]{:S(2)}, u32[]{:S(2)}) collective-permute-start(bf16[256,512]{1,0:T(8,128)(2,1)S(1)} %bitcast.65), channel_id=1, source_target_pairs={{0,8},{8,16},{16,24},{24,32},{32,40},{40,48},{48,56},{56,64},{64,7... | collective-permute-start | bytes 786440 | tf_op jit(solution)/shard_map/ppermute | solution.py:474
  8.6 2.7 %collective-permute-done.high_ref = bf16[256,512]{1,0:T(8,128)(2,1)S(1)} collective-permute-done((bf16[256,512]{1,0:T(8,128)(2,1)S(1)}, bf16[256,512]{1,0:T(8,128)(2,1)S(1)}, u32[]{:S(2)}, u32[]{:S(2)}) %collective-permute-start) | collective-permute-done | bytes 262176 | tf_op jit(solution)/shard_map/ppermute | solution.py:474
  12.3 3.5 %collective-permute-start.2 = (bf16[64,512]{1,0:T(8,128)(2,1)S(1)}, bf16[64,512]{1,0:T(8,128)(2,1)S(1)}, u32[]{:S(2)}, u32[]{:S(2)}) collective-permute-start(bf16[64,512]{1,0:T(8,128)(2,1)S(1)} %reshape.154), channel_id=1, source_target_pairs={{0,1},{1,2},{2,3},{3,4},{4,5},{5,6},{6,7},{7,0},{8,9},{9,10},{10,1... | collective-permute-start | bytes 196616 | tf_op jit(solution)/shard_map/ppermute | solution.py:469
  17.6 1.9 collective-permute-done.3.right_ref
  20.1 28.0 %enc_forward.1 = (bf16[256,512]{1,0:T(8,128)(2,1)}, bf16[256,512]{1,0:T(8,128)(2,1)}, bf16[8192,512]{1,0:T(8,128)(2,1)}, bf16[8192,512]{1,0:T(8,128)(2,1)}, bf16...) custom-call(s32[256,32]{1,0:T(8,128)} %select_select_fusion.idx_ref, s32[256,1]{1,0:T(8,128)} %copy.29.count_ref, ...), custom_call_target="tpu_custom_call" | custom-call | tf_op jit(solution)/shard_map/enc_forward/pallas_call | solution.py:145
  48.1 1.3 collective-permute-start.4
  49.4 4.9 %collective-permute-start.5 = (bf16[256,512]{1,0:T(8,128)(2,1)}, bf16[256,512]{1,0:T(8,128)(2,1)S(1)}, u32[]{:S(2)}, u32[]{:S(2)}) collective-permute-start(bf16[256,512]{1,0:T(8,128)(2,1)} %get-tuple-element.64), channel_id=1, source_target_pairs={{0,8},{8,16},{16,24},{24,32},{32,40},{40,48},{48,56},{56,64},{64,7... | collective-permute-start | bytes 786440 | tf_op jit(solution)/shard_map/ppermute | solution.py:474
  54.4 6.3 %enc_between.2.refs_0_ = bf16[8192,512]{1,0:T(8,128)(2,1)} custom-call(bf16[8192,512]{1,0:T(8,128)(2,1)} %get-tuple-element.65.normed_ref, bf16[512,512]{1,0:T(8,128)(2,1)} %out_ref.9), custom_call_target="tpu_custom_call" | custom-call | flops 2147483648 | bytes 8388608 | tf_op jit(solution)/shard_map/enc_between/pallas_call | solution.py:182
  63.1 6.3 %enc_between.3.turned_ref = bf16[8192,512]{1,0:T(8,128)(2,1)} custom-call(bf16[8192,512]{1,0:T(8,128)(2,1)} %get-tuple-element.65.normed_ref, bf16[512,512]{1,0:T(8,128)(2,1)} %out_ref.9, bf16[8192,512]{1,0:T(8,128)(2,1)} %enc_between.2.refs_0_), custom_call_target="tpu_custom_call", output_to_operand_aliasing={{}: (2, {})} | custom-call | flops 2147483648 | bytes 8388608 | tf_op jit(solution)/shard_map/enc_between/pallas_call | solution.py:182
  70.0 2.8 %collective-permute-done.7.right_ref = bf16[768,512]{1,0:T(8,128)(2,1)S(1)} collective-permute-done((bf16[768,512]{1,0:T(8,128)(2,1)S(1)}, bf16[768,512]{1,0:T(8,128)(2,1)S(1)}, u32[]{:S(2)}, u32[]{:S(2)}) %collective-permute-start.7) | collective-permute-done | bytes 786464 | tf_op jit(solution)/shard_map/ppermute | solution.py:469
  73.7 12.7 %decoder.1 = (bf16[512,512]{1,0:T(8,128)(2,1)}, bf16[1536,512]{1,0:T(8,128)(2,1)}, bf16[1536,512]{1,0:T(8,128)(2,1)}, bf16[1536,512]{1,0:T(8,128)(2,1)}, bf16[51...) custom-call(s32[512,3]{1,0:T(8,128)} %copy.30.idx_ref, s32[3,512]{1,0:T(4,128)} %fusion.30.idx_row_ref, ...), custom_call_target="tpu_custom_call" | custom-call | tf_op jit(solution)/shard_map/decoder/pallas_call | solution.py:277
  88.1 6.7 %decoder_rest.1 = (f32[512,512]{1,0:T(8,128)}, bf16[512,512]{1,0:T(8,128)(2,1)}, bf16[512,512]{1,0:T(8,128)(2,1)}, bf16[768,512]{1,0:T(8,128)(2,1)}) custom-call(s32[3,512]{1,0:T(4,128)} %fusion.30.idx_row_ref, bf16[512,512]{1,0:T(8,128)(2,1)} %bitcast.54, bf16[512,512]{1,0:T(8,128)(2,1)} %bitcast.63, bf16[1536,512]{1,0:T(8,128)(2,1)} %get-tuple-element.71.hidden_ref, ...), custom_call_target="tpu_custom_call" | custom-call | flops 2818572288 | bytes 6291456 | tf_op jit(solution)/shard_map/decoder_rest/pallas_call | solution.py:315
  94.8 3.5 %collective-permute-done.8 = bf16[768,512]{1,0:T(8,128)(2,1)S(1)} collective-permute-done((bf16[768,512]{1,0:T(8,128)(2,1)}, bf16[768,512]{1,0:T(8,128)(2,1)S(1)}, u32[]{:S(2)}, u32[]{:S(2)}) %collective-permute-start.8) | collective-permute-done | bytes 786464 | tf_op jit(solution)/shard_map/ppermute | solution.py:469
  98.3 1.5 fusion.34
  99.8 3.9 %collective-permute-start.10 = (bf16[256,512]{1,0:T(8,128)(2,1)S(1)}, bf16[256,512]{1,0:T(8,128)(2,1)S(1)}, u32[]{:S(2)}, u32[]{:S(2)}) collective-permute-start(bf16[256,512]{1,0:T(8,128)(2,1)S(1)} %get-tuple-element.111), channel_id=1, source_target_pairs={{0,8},{8,16},{16,24},{24,32},{32,40},{40,48},{48,56},{56,64},{64,7... | collective-permute-start | bytes 786440 | tf_op jit(solution)/shard_map/ppermute | solution.py:474
  103.7 1.5 collective-permute-start.11
  107.0 4.4 %collective-permute-done.11 = bf16[256,512]{1,0:T(8,128)(2,1)S(1)} collective-permute-done((bf16[256,512]{1,0:T(8,128)(2,1)S(1)}, bf16[256,512]{1,0:T(8,128)(2,1)S(1)}, u32[]{:S(2)}, u32[]{:S(2)}) %collective-permute-start.11) | collective-permute-done | bytes 262176 | tf_op jit(solution)/shard_map/ppermute | solution.py:474
  112.2 34.0 %enc_backward.1 = (bf16[256,512]{1,0:T(8,128)(2,1)}, bf16[1152,512]{1,0:T(8,128)(2,1)}, bf16[1536,512]{1,0:T(8,128)(2,1)}) custom-call(s32[8,1,1024]{2,1,0:T(1,128)} %reshape.158.idx_row_ref, f32[256,32]{1,0:T(8,128)} %get-tuple-element.76.scale_ref, bf16[256,512]{1,0:T(8,128)(2,1)} %bitcast.61, bf16[256,512]{1,0:T(8,128)(2,1)} %copy-done.3, ...), custom_call_target="tpu_custom_call" | custom-call | tf_op jit(solution)/shard_map/enc_backward/pallas_call | solution.py:432
  146.3 2.0 broadcast_select_fusion
  148.3 4.7 %collective-permute-start.12 = (bf16[1536,512]{1,0:T(8,128)(2,1)S(1)}, bf16[1536,512]{1,0:T(8,128)(2,1)S(1)}, u32[]{:S(2)}, u32[]{:S(2)}) collective-permute-start(bf16[1536,512]{1,0:T(8,128)(2,1)S(1)} %broadcast_select_fusion), channel_id=1, source_target_pairs={{0,1},{1,0},{2,3},{3,2},{4,5},{5,4},{6,7},{7,6},{8,9},{9,8},{10,11... | collective-permute-start | bytes 4718600 | tf_op jit(solution)/shard_map/ppermute | solution.py:478
  153.4 1.3 collective-permute-start.14
  156.0 1.8 add_convert_fusion
  157.8 18.4 %all-to-all-start = ((bf16[64,24,512]{2,1,0:T(8,128)(2,1)}), bf16[64,24,512]{2,1,0:T(8,128)(2,1)}, u32[]{:S(2)}, u32[]{:S(2)}) async-start(bf16[64,24,512]{2,1,0:T(8,128)(2,1)} %bitcast.13), calls=%async_computation | async-start | bytes 3145728 | tf_op jit(solution)/shard_map/all_to_all | solution.py:484
  176.9 2.9 %collective-permute-start.15 = (bf16[256,512]{1,0:T(8,128)(2,1)S(1)}, bf16[256,512]{1,0:T(8,128)(2,1)S(1)}, u32[]{:S(2)}, u32[]{:S(2)}) collective-permute-start(bf16[256,512]{1,0:T(8,128)(2,1)S(1)} %bitcast.68), channel_id=1, source_target_pairs={{0,8},{8,16},{16,24},{24,32},{32,40},{40,48},{48,56},{56,64},{64,7... | collective-permute-start | bytes 786440 | tf_op jit(solution)/shard_map/ppermute | solution.py:474
  179.8 1.3 collective-permute-start.16
  181.1 17.7 %all-to-all-done = bf16[64,24,512]{2,1,0:T(8,128)(2,1)} async-done(((bf16[64,24,512]{2,1,0:T(8,128)(2,1)}), bf16[64,24,512]{2,1,0:T(8,128)(2,1)}, u32[]{:S(2)}, u32[]{:S(2)}) %all-to-all-start) | async-done | bytes 1572896 | tf_op jit(solution)/shard_map/all_to_all | solution.py:484
  198.8 1.7 reduce_sum.22
  200.6 30.1 %all_to_all.10 = bf16[64,24,512]{2,1,0:T(8,128)(2,1)S(1)} all-to-all(bf16[64,24,512]{2,1,0:T(8,128)(2,1)S(1)} %broadcast_in_dim.12), channel_id=1, replica_groups={{0,2,4,6,8,10,12,14,16,18,20,22,24,26,28,30,32,34,36,38,40,42,44,46,48,..., dimensions={0} | all-to-all | bytes 3145728 | tf_op jit(solution)/shard_map/all_to_all | solution.py:484
  230.6 3.4 %collective-permute-start.17 = (bf16[1536,512]{1,0:T(8,128)(2,1)S(1)}, bf16[1536,512]{1,0:T(8,128)(2,1)S(1)}, u32[]{:S(2)}, u32[]{:S(2)}) collective-permute-start(bf16[1536,512]{1,0:T(8,128)(2,1)S(1)} %bitcast.57), channel_id=1, source_target_pairs={{0,1},{1,0},{2,3},{3,2},{4,5},{5,4},{6,7},{7,6},{8,9},{9,8},{10,11... | collective-permute-start | bytes 4718600 | tf_op jit(solution)/shard_map/ppermute | solution.py:478
  235.5 1.3 fusion
  237.6 2.7 %fusion.35 = (f32[512,512]{1,0:T(8,128)}, f32[512,512]{1,0:T(8,128)}, f32[512,512]{1,0:T(8,128)}, f32[512,512]{1,0:T(8,128)}, f32[512,512]{1,0:T(8,128)}, /*index=5*/f32[512,512]{1,0:T(8,128)}) fusion(f32[1536,512]{1,0:T(8,128)S(1)} %get-tuple-element.100, f32[1536,512]{1,0:T(8,128)S(1)} %get-tuple-element.101), kind=kLoop, calls=%fused_computation.92 | loop fusion | bytes 12582912 | tf_op jit(solution)/shard_map/slice | solution.py:609
  (92 shorter events, 18.5 us)
Async XLA Ops:
  0.6 11.5 %copy-start = (bf16[8,64,512]{2,1,0:T(8,128)(2,1)S(1)}, bf16[8,64,512]{2,1,0:T(8,128)(2,1)}, u32[]{:S(2)}) copy-start(bf16[8,64,512]{2,1,0:T(8,128)(2,1)} %param.16) | copy-start | bytes 1572868
  1.8 15.0 %copy-start.18 = (s32[1,1,256,32]{2,3,1,0:T(8,128)S(1)}, s32[1,1,256,32]{2,3,1,0:T(8,128)}, u32[]{:S(2)}) copy-start(s32[1,1,256,32]{2,3,1,0:T(8,128)} %param.26) | copy-start | bytes 98308
  1.8 9.5 %collective-permute-start = (bf16[256,512]{1,0:T(8,128)(2,1)S(1)}, bf16[256,512]{1,0:T(8,128)(2,1)S(1)}, u32[]{:S(2)}, u32[]{:S(2)}) collective-permute-start(bf16[256,512]{1,0:T(8,128)(2,1)S(1)} %bitcast.66), channel_id=1, source_target_pairs={{8,0},{16,8},{24,16},{32,24},{40,32},{48,40},{56,48},{64,56},{72,6... | collective-permute-start | bytes 786440 | tf_op jit(solution)/shard_map/ppermute | solution.py:474
  3.1 9.0 %collective-permute-start.1 = (bf16[256,512]{1,0:T(8,128)(2,1)S(1)}, bf16[256,512]{1,0:T(8,128)(2,1)S(1)}, u32[]{:S(2)}, u32[]{:S(2)}) collective-permute-start(bf16[256,512]{1,0:T(8,128)(2,1)S(1)} %bitcast.65), channel_id=1, source_target_pairs={{0,8},{8,16},{16,24},{24,32},{32,40},{40,48},{48,56},{56,64},{64,7... | collective-permute-start | bytes 786440 | tf_op jit(solution)/shard_map/ppermute | solution.py:474
  11.3 8.2 %copy-start.4 = (bf16[256,512]{1,0:T(8,128)(2,1)}, bf16[256,512]{1,0:T(8,128)(2,1)S(1)}, u32[]{:S(2)}) copy-start(bf16[256,512]{1,0:T(8,128)(2,1)S(1)} %collective-permute-done.high_ref) | copy-start | bytes 786436
  12.1 7.4 %copy-start.5 = (bf16[256,512]{1,0:T(8,128)(2,1)}, bf16[256,512]{1,0:T(8,128)(2,1)S(1)}, u32[]{:S(2)}) copy-start(bf16[256,512]{1,0:T(8,128)(2,1)S(1)} %collective-permute-done.1.low_ref) | copy-start | bytes 786436
  12.3 5.3 %collective-permute-start.2 = (bf16[64,512]{1,0:T(8,128)(2,1)S(1)}, bf16[64,512]{1,0:T(8,128)(2,1)S(1)}, u32[]{:S(2)}, u32[]{:S(2)}) collective-permute-start(bf16[64,512]{1,0:T(8,128)(2,1)S(1)} %reshape.154), channel_id=1, source_target_pairs={{0,1},{1,2},{2,3},{3,4},{4,5},{5,6},{6,7},{7,0},{8,9},{9,10},{10,1... | collective-permute-start | bytes 196616 | tf_op jit(solution)/shard_map/ppermute | solution.py:469
  15.8 3.7 %collective-permute-start.3 = (bf16[64,512]{1,0:T(8,128)(2,1)S(1)}, bf16[64,512]{1,0:T(8,128)(2,1)S(1)}, u32[]{:S(2)}, u32[]{:S(2)}) collective-permute-start(bf16[64,512]{1,0:T(8,128)(2,1)S(1)} %reshape.155), channel_id=1, source_target_pairs={{0,7},{1,0},{2,1},{3,2},{4,3},{5,4},{6,5},{7,6},{8,15},{9,8},{10,9... | collective-permute-start | bytes 196616 | tf_op jit(solution)/shard_map/ppermute | solution.py:469
  48.1 12.6 %collective-permute-start.4 = (bf16[256,512]{1,0:T(8,128)(2,1)}, bf16[256,512]{1,0:T(8,128)(2,1)S(1)}, u32[]{:S(2)}, u32[]{:S(2)}) collective-permute-start(bf16[256,512]{1,0:T(8,128)(2,1)} %get-tuple-element.64), channel_id=1, source_target_pairs={{8,0},{16,8},{24,16},{32,24},{40,32},{48,40},{56,48},{64,56},{72,6... | collective-permute-start | bytes 786440 | tf_op jit(solution)/shard_map/ppermute | solution.py:474
  49.4 11.3 %collective-permute-start.5 = (bf16[256,512]{1,0:T(8,128)(2,1)}, bf16[256,512]{1,0:T(8,128)(2,1)S(1)}, u32[]{:S(2)}, u32[]{:S(2)}) collective-permute-start(bf16[256,512]{1,0:T(8,128)(2,1)} %get-tuple-element.64), channel_id=1, source_target_pairs={{0,8},{8,16},{16,24},{24,32},{32,40},{40,48},{48,56},{56,64},{64,7... | collective-permute-start | bytes 786440 | tf_op jit(solution)/shard_map/ppermute | solution.py:474
  54.4 6.4 %copy-start.16 = (bf16[256,512]{1,0:T(8,128)(2,1)S(1)}, bf16[256,512]{1,0:T(8,128)(2,1)}, u32[]{:S(2)}) copy-start(bf16[256,512]{1,0:T(8,128)(2,1)} %get-tuple-element.64) | copy-start | bytes 786436
  60.8 8.6 %copy-start.2 = (bf16[768,512]{1,0:T(8,128)(2,1)}, bf16[768,512]{1,0:T(8,128)(2,1)S(1)}, u32[]{:S(2)}) copy-start(bf16[768,512]{1,0:T(8,128)(2,1)S(1)} %pad_maximum_fusion.2.centre_ref) | copy-start | bytes 2359300
  60.8 9.2 %collective-permute-start.6 = (bf16[768,512]{1,0:T(8,128)(2,1)S(1)}, bf16[768,512]{1,0:T(8,128)(2,1)S(1)}, u32[]{:S(2)}, u32[]{:S(2)}) collective-permute-start(bf16[768,512]{1,0:T(8,128)(2,1)S(1)} %pad_maximum_fusion.2.centre_ref), channel_id=1, source_target_pairs={{0,1},{1,2},{2,3},{3,4},{4,5},{5,6},{6,7},{7,0},{8,9},{9,10},{10,1... | collective-permute-start | bytes 2359304 | tf_op jit(solution)/shard_map/ppermute | solution.py:469
  61.1 11.7 %collective-permute-start.7 = (bf16[768,512]{1,0:T(8,128)(2,1)S(1)}, bf16[768,512]{1,0:T(8,128)(2,1)S(1)}, u32[]{:S(2)}, u32[]{:S(2)}) collective-permute-start(bf16[768,512]{1,0:T(8,128)(2,1)S(1)} %pad_maximum_fusion.2.centre_ref), channel_id=1, source_target_pairs={{0,7},{1,0},{2,1},{3,2},{4,3},{5,4},{6,5},{7,6},{8,15},{9,8},{10,9... | collective-permute-start | bytes 2359304 | tf_op jit(solution)/shard_map/ppermute | solution.py:469
  70.0 2.8 %copy-start.11 = (bf16[768,512]{1,0:T(8,128)(2,1)}, bf16[768,512]{1,0:T(8,128)(2,1)S(1)}, u32[]{:S(2)}) copy-start(bf16[768,512]{1,0:T(8,128)(2,1)S(1)} %collective-permute-done.6.left_ref) | copy-start | bytes 2359300
  86.4 11.9 %collective-permute-start.8 = (bf16[768,512]{1,0:T(8,128)(2,1)}, bf16[768,512]{1,0:T(8,128)(2,1)S(1)}, u32[]{:S(2)}, u32[]{:S(2)}) collective-permute-start(bf16[768,512]{1,0:T(8,128)(2,1)} %get-tuple-element.78), channel_id=1, source_target_pairs={{0,7},{1,0},{2,1},{3,2},{4,3},{5,4},{6,5},{7,6},{8,15},{9,8},{10,9... | collective-permute-start | bytes 2359304 | tf_op jit(solution)/shard_map/ppermute | solution.py:469
  87.5 10.8 %collective-permute-start.9 = (bf16[768,512]{1,0:T(8,128)(2,1)}, bf16[768,512]{1,0:T(8,128)(2,1)S(1)}, u32[]{:S(2)}, u32[]{:S(2)}) collective-permute-start(bf16[768,512]{1,0:T(8,128)(2,1)} %get-tuple-element.79), channel_id=1, source_target_pairs={{0,1},{1,2},{2,3},{3,4},{4,5},{5,6},{6,7},{7,0},{8,9},{9,10},{10,1... | collective-permute-start | bytes 2359304 | tf_op jit(solution)/shard_map/ppermute | solution.py:469
  98.3 7.0 %copy-start.17 = (s32[1,1,256,32]{2,3,1,0:T(8,128)S(1)}, s32[1,1,256,32]{2,3,1,0:T(8,128)}, u32[]{:S(2)}) copy-start(s32[1,1,256,32]{2,3,1,0:T(8,128)} %param.25) | copy-start | bytes 98308
  99.8 11.8 %copy-start.15 = (bf16[256,512]{1,0:T(8,128)(2,1)S(1)}, bf16[256,512]{1,0:T(8,128)(2,1)}, u32[]{:S(2)}) copy-start(bf16[256,512]{1,0:T(8,128)(2,1)} %get-tuple-element.85) | copy-start | bytes 786436
  99.8 7.2 %collective-permute-start.10 = (bf16[256,512]{1,0:T(8,128)(2,1)S(1)}, bf16[256,512]{1,0:T(8,128)(2,1)S(1)}, u32[]{:S(2)}, u32[]{:S(2)}) collective-permute-start(bf16[256,512]{1,0:T(8,128)(2,1)S(1)} %get-tuple-element.111), channel_id=1, source_target_pairs={{0,8},{8,16},{16,24},{24,32},{32,40},{40,48},{48,56},{56,64},{64,7... | collective-permute-start | bytes 786440 | tf_op jit(solution)/shard_map/ppermute | solution.py:474
  103.7 7.7 %collective-permute-start.11 = (bf16[256,512]{1,0:T(8,128)(2,1)S(1)}, bf16[256,512]{1,0:T(8,128)(2,1)S(1)}, u32[]{:S(2)}, u32[]{:S(2)}) collective-permute-start(bf16[256,512]{1,0:T(8,128)(2,1)S(1)} %get-tuple-element.112), channel_id=1, source_target_pairs={{8,0},{16,8},{24,16},{32,24},{40,32},{48,40},{56,48},{64,56},{72,6... | collective-permute-start | bytes 786440 | tf_op jit(solution)/shard_map/ppermute | solution.py:474
  112.2 34.0 %copy-start.6 = (bf16[512,512]{1,0:T(8,128)(2,1)S(1)}, bf16[512,512]{1,0:T(8,128)(2,1)}, u32[]{:S(2)}) copy-start(bf16[512,512]{1,0:T(8,128)(2,1)} %get-tuple-element.87) | copy-start | bytes 1572868
  112.2 34.0 %copy-start.7 = (bf16[512,512]{1,0:T(8,128)(2,1)S(1)}, bf16[512,512]{1,0:T(8,128)(2,1)}, u32[]{:S(2)}) copy-start(bf16[512,512]{1,0:T(8,128)(2,1)} %get-tuple-element.86) | copy-start | bytes 1572868
  146.2 6.7 %copy-start.9 = (bf16[1152,512]{1,0:T(8,128)(2,1)S(1)}, bf16[1152,512]{1,0:T(8,128)(2,1)}, u32[]{:S(2)}) copy-start(bf16[1152,512]{1,0:T(8,128)(2,1)} %get-tuple-element.83) | copy-start | bytes 3538948
  146.3 9.7 %copy-start.1 = (bf16[1536,512]{1,0:T(8,128)(2,1)S(1)}, bf16[1536,512]{1,0:T(8,128)(2,1)}, u32[]{:S(2)}) copy-start(bf16[1536,512]{1,0:T(8,128)(2,1)} %get-tuple-element.84) | copy-start | bytes 4718596
  148.3 7.7 %collective-permute-start.12 = (bf16[1536,512]{1,0:T(8,128)(2,1)S(1)}, bf16[1536,512]{1,0:T(8,128)(2,1)S(1)}, u32[]{:S(2)}, u32[]{:S(2)}) collective-permute-start(bf16[1536,512]{1,0:T(8,128)(2,1)S(1)} %broadcast_select_fusion), channel_id=1, source_target_pairs={{0,1},{1,0},{2,3},{3,2},{4,5},{5,4},{6,7},{7,6},{8,9},{9,8},{10,11... | collective-permute-start | bytes 4718600 | tf_op jit(solution)/shard_map/ppermute | solution.py:478
  152.9 4.8 %collective-permute-start.13 = (bf16[64,512]{1,0:T(8,128)(2,1)S(1)}, bf16[64,512]{1,0:T(8,128)(2,1)S(1)}, u32[]{:S(2)}, u32[]{:S(2)}) collective-permute-start(bf16[64,512]{1,0:T(8,128)(2,1)S(1)} %get-tuple-element.106), channel_id=1, source_target_pairs={{0,7},{1,0},{2,1},{3,2},{4,3},{5,4},{6,5},{7,6},{8,15},{9,8},{10,9... | collective-permute-start | bytes 196616 | tf_op jit(solution)/shard_map/ppermute | solution.py:469
  153.4 4.4 %collective-permute-start.14 = (bf16[64,512]{1,0:T(8,128)(2,1)S(1)}, bf16[64,512]{1,0:T(8,128)(2,1)S(1)}, u32[]{:S(2)}, u32[]{:S(2)}) collective-permute-start(bf16[64,512]{1,0:T(8,128)(2,1)S(1)} %get-tuple-element.105), channel_id=1, source_target_pairs={{0,1},{1,2},{2,3},{3,4},{4,5},{5,6},{6,7},{7,0},{8,9},{9,10},{10,1... | collective-permute-start | bytes 196616 | tf_op jit(solution)/shard_map/ppermute | solution.py:469
  157.8 41.0 %all-to-all-start = ((bf16[64,24,512]{2,1,0:T(8,128)(2,1)}), bf16[64,24,512]{2,1,0:T(8,128)(2,1)}, u32[]{:S(2)}, u32[]{:S(2)}) async-start(bf16[64,24,512]{2,1,0:T(8,128)(2,1)} %bitcast.13), calls=%async_computation | async-start | bytes 3145728 | tf_op jit(solution)/shard_map/all_to_all | solution.py:484
  176.9 23.5 %collective-permute-start.15 = (bf16[256,512]{1,0:T(8,128)(2,1)S(1)}, bf16[256,512]{1,0:T(8,128)(2,1)S(1)}, u32[]{:S(2)}, u32[]{:S(2)}) collective-permute-start(bf16[256,512]{1,0:T(8,128)(2,1)S(1)} %bitcast.68), channel_id=1, source_target_pairs={{0,8},{8,16},{16,24},{24,32},{32,40},{40,48},{48,56},{56,64},{64,7... | collective-permute-start | bytes 786440 | tf_op jit(solution)/shard_map/ppermute | solution.py:474
  179.8 20.6 %collective-permute-start.16 = (bf16[256,512]{1,0:T(8,128)(2,1)S(1)}, bf16[256,512]{1,0:T(8,128)(2,1)S(1)}, u32[]{:S(2)}, u32[]{:S(2)}) collective-permute-start(bf16[256,512]{1,0:T(8,128)(2,1)S(1)} %bitcast.67), channel_id=1, source_target_pairs={{8,0},{16,8},{24,16},{32,24},{40,32},{48,40},{56,48},{64,56},{72,6... | collective-permute-start | bytes 786440 | tf_op jit(solution)/shard_map/ppermute | solution.py:474
  230.6 6.5 %collective-permute-start.17 = (bf16[1536,512]{1,0:T(8,128)(2,1)S(1)}, bf16[1536,512]{1,0:T(8,128)(2,1)S(1)}, u32[]{:S(2)}, u32[]{:S(2)}) collective-permute-start(bf16[1536,512]{1,0:T(8,128)(2,1)S(1)} %bitcast.57), channel_id=1, source_target_pairs={{0,1},{1,0},{2,3},{3,2},{4,5},{5,4},{6,7},{7,6},{8,9},{9,8},{10,11... | collective-permute-start | bytes 4718600 | tf_op jit(solution)/shard_map/ppermute | solution.py:478
  (7 other events, 7.3 us)
where the time goes:
time: 241 us; the launch traced here: 240 us
  Pallas kernels  94 us (39%)
  starting transfers between devices  55.6 us (23%)
  waiting for transfers between devices  36.7 us (15%)
  blocking collectives  30.1 us (12%)
  local copies, waits for them, and re-layouts  11 us (5%)
  other arithmetic  10.4 us (4%)
    pallas_call x1, Pallas kernels, enc_backward(): pl.pallas_call(enc_backward_kernel, name='enc_backward', grid=(tiles + 1,...  34 us
    all_to_all x1, blocking collectives, across_chips(): lax.all_to_all(parts, ('lat', 'lon'), 0, 0, axis_index_groups=alike, tile...  30.1 us
    pallas_call x1, Pallas kernels, enc_forward(): pl.pallas_call(enc_forward_kernel, name='enc_forward', grid=(nodes // til...  28 us
    ppermute x8, starting transfers between devices, to_lat(): lax.ppermute(shard, 'lat', [(i, i + by) for i in range(count) if 0 <= i +...  21.7 us
    all_to_all x1, starting transfers between devices, across_chips(): lax.all_to_all(parts, ('lat', 'lon'), 0, 0, axis_index_groups=alike, tile...  18.4 us
    all_to_all x1, waiting for transfers between devices, across_chips(): lax.all_to_all(parts, ('lat', 'lon'), 0, 0, axis_index_groups=alike, tile...  17.7 us
    pallas_call x1, Pallas kernels, decoder(): pl.pallas_call(decoder_kernel, name='decoder', out_shape=[node_shape, edg...  12.7 us
    pallas_call x2, Pallas kernels, enc_between(): pl.pallas_call(enc_between_kernel, name='enc_between', grid=(count,), in_...  12.6 us
  transfers between devices with their start and end apart: 19, of which 11 were waited for; matrix products, arithmetic and copies ran while one was open for 5% of the time, Pallas kernels for 8%

commit v1 on v0

--- a/solution.py
+++ b/solution.py
@@ -9,7 +9,7 @@
 NORM_EPSILON = 1e-05
 BF = jnp.bfloat16
 F32 = jnp.float32
-VMEM_LIMIT = 56 * 1024 * 1024
+MIB = 1024 * 1024
 ENC_TILE = 32
 ENC_CHUNK = 4
 STRIP = 16
@@ -53,8 +53,8 @@
                 stages[d](i - d)
 
 
-def kernel_params():
-    return pltpu.CompilerParams(vmem_limit_bytes=VMEM_LIMIT)
+def kernel_params(mib):
+    return pltpu.CompilerParams(vmem_limit_bytes=mib * MIB)
 
 
 def whole(shape):
@@ -166,7 +166,7 @@
             pltpu.VMEM((edges, band_rows), BF),
             pltpu.VMEM((nodes, width), F32),
         ],
-        compiler_params=kernel_params(),
+        compiler_params=kernel_params(26),
     )(idx, counts, mesh_rows, *pieces, enc_send, enc_recv, enc_out, dec_send)
 
 
@@ -187,7 +187,7 @@
         out_specs=per_edge,
         out_shape=jax.ShapeDtypeStruct(normed.shape, BF),
         input_output_aliases={2: 0} if kept else {},
-        compiler_params=kernel_params(),
+        compiler_params=kernel_params(12),
         cost_estimate=pl.CostEstimate(flops=2 * share * width, bytes_accessed=4 * share, transcendentals=0),
     )(normed, enc_out, *kept)
 
@@ -285,7 +285,7 @@
             pltpu.VMEM((nodes, width), F32),
             pltpu.VMEM((nodes, width), F32),
         ],
-        compiler_params=kernel_params(),
+        compiler_params=kernel_params(36),
     )(idx, idx_rows, grid_rows, cot_rows, centre, left, right, dec_recv, dec_out)
 
 
@@ -322,7 +322,7 @@
             jax.ShapeDtypeStruct((third, width), BF),
         ],
         scratch_shapes=[pltpu.VMEM((third, degree * nodes), BF)],
-        compiler_params=kernel_params(),
+        compiler_params=kernel_params(20),
         cost_estimate=pl.CostEstimate(
             flops=2 * degree * nodes * width * (third + 2 * width), bytes_accessed=8 * degree * nodes * width,
             transcendentals=0,
@@ -460,7 +460,7 @@
             pltpu.VMEM((nodes, width), F32),
             pltpu.VMEM((nodes, width), BF),
         ],
-        compiler_params=kernel_params(),
+        compiler_params=kernel_params(40),
     )(idx_rows, scale, mesh_rows, moved_cot, normed, turned, slope, hidden, *pieces, dec_send, enc_recv, enc_out)
 
 

time: 241 us -> 247 us (1.025)
  local copies, waits for them, and re-layouts: 11 us -> 37.2 us
  Pallas kernels: 94 us -> 76.6 us
  waiting for transfers between devices: 36.7 us -> 30.5 us
    unnamed x41 -> x65, local copies, waits for them, and re-layouts: 4.06 us -> 25.1 us
    pallas_call x2, Pallas kernels: 12.6 us -> 5.98 us  [enc_between(): pl.pallas_call(enc_between_kernel, name='enc_between', grid=(count,), in_...]
    ppermute x8, waiting for transfers between devices: 8.64 us -> 4.15 us  [to_lat(): lax.ppermute(shard, 'lat', [(i, i + by) for i in range(count) if 0 <= i +...]
    pallas_call x1, Pallas kernels: 6.7 us -> 2.73 us  [decoder_rest(): pl.pallas_call(decoder_rest_kernel, name='decoder_rest', out_shape=[jax.S...]
    pallas_call x1, Pallas kernels: 34 us -> 31.4 us  [enc_backward(): pl.pallas_call(enc_backward_kernel, name='enc_backward', grid=(tiles + 1,...]
    all_to_all x1, starting transfers between devices: 18.4 us -> 15.8 us  [across_chips(): lax.all_to_all(parts, ('lat', 'lon'), 0, 0, axis_index_groups=alike, tile...]
  transfers between devices with their start and end apart: 19 -> 19, of which waited for: 11 -> 8; matrix products, arithmetic and copies ran while one was open for 5% -> 7% of each run, Pallas kernels for 8% -> 4%
where the time goes in v1:
time: 247 us; the launch traced here: 246 us
  Pallas kernels  76.6 us (31%)
  starting transfers between devices  55.6 us (23%)
  local copies, waits for them, and re-layouts  37.2 us (15%)
  waiting for transfers between devices  30.5 us (12%)
  blocking collectives  30 us (12%)
  other arithmetic  11.9 us (5%)
  matrix products  2.54 us (1%)
    pallas_call x1, Pallas kernels, enc_backward(): pl.pallas_call(enc_backward_kernel, name='enc_backward', grid=(tiles + 1,...  31.4 us
    all_to_all x1, blocking collectives, across_chips(): lax.all_to_all(parts, ('lat', 'lon'), 0, 0, axis_index_groups=alike, tile...  30 us
    pallas_call x1, Pallas kernels, enc_forward(): pl.pallas_call(enc_forward_kernel, name='enc_forward', grid=(nodes // til...  25.6 us
    unnamed x65, local copies, waits for them, and re-layouts  25.1 us
    ppermute x8, starting transfers between devices, to_lat(): lax.ppermute(shard, 'lat', [(i, i + by) for i in range(count) if 0 <= i +...  22.1 us
    all_to_all x1, waiting for transfers between devices, across_chips(): lax.all_to_all(parts, ('lat', 'lon'), 0, 0, axis_index_groups=alike, tile...  17.3 us
    all_to_all x1, starting transfers between devices, across_chips(): lax.all_to_all(parts, ('lat', 'lon'), 0, 0, axis_index_groups=alike, tile...  15.8 us
    pallas_call x1, Pallas kernels, decoder(): pl.pallas_call(decoder_kernel, name='decoder', out_shape=[node_shape, edg...  10.9 us
  transfers between devices with their start and end apart: 19, of which 8 were waited for; matrix products, arithmetic and copies ran while one was open for 7% of the time, Pallas kernels for 4%

profile of v1, /device:TPU:1, one launch (start us, length us, event | category | flops | bytes accessed | tf_op | source)
XLA Modules:
  0.0 245.5 jit_solution(13687704637184562200)
XLA Ops:
  0.7 1.9 fusion.41
  3.8 4.6 %collective-permute-start.1 = (bf16[256,512]{1,0:T(8,128)(2,1)}, bf16[256,512]{1,0:T(8,128)(2,1)S(1)}, u32[]{:S(2)}, u32[]{:S(2)}) collective-permute-start(bf16[256,512]{1,0:T(8,128)(2,1)} %bitcast.7), channel_id=1, source_target_pairs={{0,8},{8,16},{16,24},{24,32},{32,40},{40,48},{48,56},{56,64},{64,7... | collective-permute-start | bytes 786440 | tf_op jit(solution)/shard_map/ppermute | solution.py:474
  10.0 2.2 collective-permute-done.high_ref
  14.0 3.5 %collective-permute-start.2 = (bf16[64,512]{1,0:T(8,128)(2,1)}, bf16[64,512]{1,0:T(8,128)(2,1)}, u32[]{:S(2)}, u32[]{:S(2)}) collective-permute-start(bf16[64,512]{1,0:T(8,128)(2,1)} %reshape.154), channel_id=1, source_target_pairs={{0,1},{1,2},{2,3},{3,4},{4,5},{5,6},{6,7},{7,0},{8,9},{9,10},{10,1... | collective-permute-start | bytes 196616 | tf_op jit(solution)/shard_map/ppermute | solution.py:469
  23.1 25.6 %enc_forward.1 = (bf16[256,512]{1,0:T(8,128)(2,1)S(1)}, bf16[256,512]{1,0:T(8,128)(2,1)S(1)}, bf16[8192,512]{1,0:T(8,128)(2,1)S(1)}, bf16[8192,512]{1,0:T(8,128)...) custom-call(s32[256,32]{1,0:T(8,128)S(1)} %select_select_fusion.idx_ref, s32[256,1]{1,0:T(8,128)S(1)} %copy-done.26, ...), custom_call_target="tpu_custom_call" | custom-call | tf_op jit(solution)/shard_map/enc_forward/pallas_call | solution.py:145
  51.3 4.8 %collective-permute-start.5 = (bf16[256,512]{1,0:T(8,128)(2,1)S(1)}, bf16[256,512]{1,0:T(8,128)(2,1)S(1)}, u32[]{:S(2)}, u32[]{:S(2)}) collective-permute-start(bf16[256,512]{1,0:T(8,128)(2,1)S(1)} %get-tuple-element.64), channel_id=1, source_target_pairs={{0,8},{8,16},{16,24},{24,32},{32,40},{40,48},{48,56},{56,64},{64,7... | collective-permute-start | bytes 786440 | tf_op jit(solution)/shard_map/ppermute | solution.py:474
  56.1 3.4 %copy-done = bf16[8192,512]{1,0:T(8,128)(2,1)S(1)} copy-done((bf16[8192,512]{1,0:T(8,128)(2,1)S(1)}, bf16[8192,512]{1,0:T(8,128)(2,1)}, u32[]{:S(2)}) %copy-start) | copy-done | bytes 8388632
  59.5 3.0 %enc_between.2.refs_0_ = bf16[8192,512]{1,0:T(8,128)(2,1)S(1)} custom-call(bf16[8192,512]{1,0:T(8,128)(2,1)S(1)} %copy-done, bf16[512,512]{1,0:T(8,128)(2,1)S(1)} %copy-done.7), custom_call_target="tpu_custom_call" | custom-call | flops 2147483648 | bytes 8388608 | tf_op jit(solution)/shard_map/enc_between/pallas_call | solution.py:182
  62.5 3.3 %copy-done.3 = bf16[8192,512]{1,0:T(8,128)(2,1)} copy-done((bf16[8192,512]{1,0:T(8,128)(2,1)}, bf16[8192,512]{1,0:T(8,128)(2,1)S(1)}, u32[]{:S(2)}) %copy-start.3) | copy-done | bytes 8388632
  67.8 3.4 %copy-done.1 = bf16[8192,512]{1,0:T(8,128)(2,1)S(1)} copy-done((bf16[8192,512]{1,0:T(8,128)(2,1)S(1)}, bf16[8192,512]{1,0:T(8,128)(2,1)}, u32[]{:S(2)}) %copy-start.1) | copy-done | bytes 8388632
  71.1 3.4 %copy-done.4 = bf16[8192,512]{1,0:T(8,128)(2,1)S(1)} copy-done((bf16[8192,512]{1,0:T(8,128)(2,1)S(1)}, bf16[8192,512]{1,0:T(8,128)(2,1)}, u32[]{:S(2)}) %copy-start.4) | copy-done | bytes 8388632
  74.5 3.0 %enc_between.3.turned_ref = bf16[8192,512]{1,0:T(8,128)(2,1)S(1)} custom-call(bf16[8192,512]{1,0:T(8,128)(2,1)S(1)} %copy-done.1, bf16[512,512]{1,0:T(8,128)(2,1)S(1)} %copy-done.7, bf16[8192,512]{1,0:T(8,128)(2,1)S(1)} %copy-done.4), custom_call_target="tpu_custom_call", output_to_operand_aliasing={{}: (2, {})} | custom-call | flops 2147483648 | bytes 8388608 | tf_op jit(solution)/shard_map/enc_between/pallas_call | solution.py:182
  77.5 3.3 %copy-done.5 = bf16[8192,512]{1,0:T(8,128)(2,1)} copy-done((bf16[8192,512]{1,0:T(8,128)(2,1)}, bf16[8192,512]{1,0:T(8,128)(2,1)S(1)}, u32[]{:S(2)}) %copy-start.5) | copy-done | bytes 8388632
  80.8 10.9 %decoder.1 = (bf16[512,512]{1,0:T(8,128)(2,1)}, bf16[1536,512]{1,0:T(8,128)(2,1)S(1)}, bf16[1536,512]{1,0:T(8,128)(2,1)S(1)}, bf16[1536,512]{1,0:T(8,128)(2,1)S(...) custom-call(s32[512,3]{1,0:T(8,128)S(1)} %copy-done.20, ...), custom_call_target="tpu_custom_call" | custom-call | tf_op jit(solution)/shard_map/decoder/pallas_call | solution.py:277
  91.8 2.8 %collective-permute-start.8 = (bf16[768,512]{1,0:T(8,128)(2,1)S(1)}, bf16[768,512]{1,0:T(8,128)(2,1)S(1)}, u32[]{:S(2)}, u32[]{:S(2)}) collective-permute-start(bf16[768,512]{1,0:T(8,128)(2,1)S(1)} %get-tuple-element.78), channel_id=1, source_target_pairs={{0,7},{1,0},{2,1},{3,2},{4,3},{5,4},{6,5},{7,6},{8,15},{9,8},{10,9... | collective-permute-start | bytes 2359304 | tf_op jit(solution)/shard_map/ppermute | solution.py:469
  94.5 2.7 %decoder_rest.1 = (f32[512,512]{1,0:T(8,128)S(1)}, bf16[512,512]{1,0:T(8,128)(2,1)S(1)}, bf16[512,512]{1,0:T(8,128)(2,1)S(1)}, bf16[768,512]{1,0:T(8,128)(2,1)S(1)}) custom-call(s32[3,512]{1,0:T(4,128)S(1)} %fusion.30.idx_row_ref, bf16[512,512]{1,0:T(8,128)(2,1)S(1)} %bitcast.55, bf16[512,512]{1,0:T(8,128)(2,1)S(1)} %bitcast.60, ...), custom_call_target="tpu_custom_call" | custom-call | flops 2818572288 | bytes 6291456 | tf_op jit(solution)/shard_map/decoder_rest/pallas_call | solution.py:315
  97.3 6.2 %collective-permute-done.8 = bf16[768,512]{1,0:T(8,128)(2,1)S(1)} collective-permute-done((bf16[768,512]{1,0:T(8,128)(2,1)S(1)}, bf16[768,512]{1,0:T(8,128)(2,1)S(1)}, u32[]{:S(2)}, u32[]{:S(2)}) %collective-permute-start.8) | collective-permute-done | bytes 786464 | tf_op jit(solution)/shard_map/ppermute | solution.py:469
  105.8 4.4 %collective-permute-start.10 = (bf16[256,512]{1,0:T(8,128)(2,1)}, bf16[256,512]{1,0:T(8,128)(2,1)}, u32[]{:S(2)}, u32[]{:S(2)}) collective-permute-start(bf16[256,512]{1,0:T(8,128)(2,1)} %get-tuple-element.111), channel_id=1, source_target_pairs={{0,8},{8,16},{16,24},{24,32},{32,40},{40,48},{48,56},{56,64},{64,7... | collective-permute-start | bytes 786440 | tf_op jit(solution)/shard_map/ppermute | solution.py:474
  113.3 1.8 select_bitcast_fusion
  115.1 1.6 reshape.158.idx_row_ref
  120.3 3.4 %copy-done.2 = bf16[8192,512]{1,0:T(8,128)(2,1)S(1)} copy-done((bf16[8192,512]{1,0:T(8,128)(2,1)S(1)}, bf16[8192,512]{1,0:T(8,128)(2,1)}, u32[]{:S(2)}) %copy-start.2) | copy-done | bytes 8388632
  123.7 31.4 %enc_backward.1 = (bf16[256,512]{1,0:T(8,128)(2,1)}, bf16[1152,512]{1,0:T(8,128)(2,1)S(1)}, bf16[1536,512]{1,0:T(8,128)(2,1)S(1)}) custom-call(s32[8,1,1024]{2,1,0:T(1,128)S(1)} %copy-done.30, f32[256,32]{1,0:T(8,128)S(1)} %copy-done.29, bf16[256,512]{1,0:T(8,128)(2,1)S(1)} %bitcast.58, bf16[256,512]{1,0:T(8,128)(2,1)S(1)} %fusion.3.moved_cot_ref, ...), custom_call_target="tpu_custom_call" | custom-call | tf_op jit(solution)/shard_map/enc_backward/pallas_call | solution.py:432
  155.5 5.5 %collective-permute-start.12 = (bf16[1536,512]{1,0:T(8,128)(2,1)S(1)}, bf16[1536,512]{1,0:T(8,128)(2,1)S(1)}, u32[]{:S(2)}, u32[]{:S(2)}) collective-permute-start(bf16[1536,512]{1,0:T(8,128)(2,1)S(1)} %broadcast_select_fusion), channel_id=1, source_target_pairs={{0,1},{1,0},{2,3},{3,2},{4,5},{5,4},{6,7},{7,6},{8,9},{9,8},{10,11... | collective-permute-start | bytes 4718600 | tf_op jit(solution)/shard_map/ppermute | solution.py:478
  161.3 1.5 collective-permute-start.14
  164.1 1.8 add_convert_fusion
  165.8 15.8 %all-to-all-start = ((bf16[64,24,512]{2,1,0:T(8,128)(2,1)}), bf16[64,24,512]{2,1,0:T(8,128)(2,1)}, u32[]{:S(2)}, u32[]{:S(2)}) async-start(bf16[64,24,512]{2,1,0:T(8,128)(2,1)} %bitcast.62), calls=%async_computation | async-start | bytes 3145728 | tf_op jit(solution)/shard_map/all_to_all | solution.py:484
  182.5 2.9 %collective-permute-start.15 = (bf16[256,512]{1,0:T(8,128)(2,1)S(1)}, bf16[256,512]{1,0:T(8,128)(2,1)S(1)}, u32[]{:S(2)}, u32[]{:S(2)}) collective-permute-start(bf16[256,512]{1,0:T(8,128)(2,1)S(1)} %bitcast.67), channel_id=1, source_target_pairs={{0,8},{8,16},{16,24},{24,32},{32,40},{40,48},{48,56},{56,64},{64,7... | collective-permute-start | bytes 786440 | tf_op jit(solution)/shard_map/ppermute | solution.py:474
  186.7 17.3 %all-to-all-done = bf16[64,24,512]{2,1,0:T(8,128)(2,1)} async-done(((bf16[64,24,512]{2,1,0:T(8,128)(2,1)}), bf16[64,24,512]{2,1,0:T(8,128)(2,1)}, u32[]{:S(2)}, u32[]{:S(2)}) %all-to-all-start) | async-done | bytes 1572896 | tf_op jit(solution)/shard_map/all_to_all | solution.py:484
  204.0 1.7 reduce_sum.22
  205.8 30.0 %all_to_all.10 = bf16[64,24,512]{2,1,0:T(8,128)(2,1)S(1)} all-to-all(bf16[64,24,512]{2,1,0:T(8,128)(2,1)S(1)} %broadcast_in_dim.12), channel_id=1, replica_groups={{0,2,4,6,8,10,12,14,16,18,20,22,24,26,28,30,32,34,36,38,40,42,44,46,48,..., dimensions={0} | all-to-all | bytes 3145728 | tf_op jit(solution)/shard_map/all_to_all | solution.py:484
  235.8 3.5 %collective-permute-start.17 = (bf16[1536,512]{1,0:T(8,128)(2,1)S(1)}, bf16[1536,512]{1,0:T(8,128)(2,1)S(1)}, u32[]{:S(2)}, u32[]{:S(2)}) collective-permute-start(bf16[1536,512]{1,0:T(8,128)(2,1)S(1)} %bitcast.61), channel_id=1, source_target_pairs={{0,1},{1,0},{2,3},{3,2},{4,5},{5,4},{6,7},{7,6},{8,9},{9,8},{10,11... | collective-permute-start | bytes 4718600 | tf_op jit(solution)/shard_map/ppermute | solution.py:478
  242.8 2.7 %fusion.35 = (f32[512,512]{1,0:T(8,128)}, f32[512,512]{1,0:T(8,128)}, f32[512,512]{1,0:T(8,128)}, f32[512,512]{1,0:T(8,128)}, f32[512,512]{1,0:T(8,128)}, /*index=5*/f32[512,512]{1,0:T(8,128)}) fusion(f32[1536,512]{1,0:T(8,128)S(1)} %get-tuple-element.100, f32[1536,512]{1,0:T(8,128)S(1)} %get-tuple-element.101), kind=kLoop, calls=%fused_computation.92 | loop fusion | bytes 12582912 | tf_op jit(solution)/shard_map/slice | solution.py:609
  (116 shorter events, 31.2 us)
Async XLA Ops:
  0.6 12.6 %copy-start.6 = (bf16[8,64,512]{2,1,0:T(8,128)(2,1)S(1)}, bf16[8,64,512]{2,1,0:T(8,128)(2,1)}, u32[]{:S(2)}) copy-start(bf16[8,64,512]{2,1,0:T(8,128)(2,1)} %param.16) | copy-start | bytes 1572868
  2.6 9.7 %collective-permute-start = (bf16[256,512]{1,0:T(8,128)(2,1)}, bf16[256,512]{1,0:T(8,128)(2,1)S(1)}, u32[]{:S(2)}, u32[]{:S(2)}) collective-permute-start(bf16[256,512]{1,0:T(8,128)(2,1)} %bitcast.6), channel_id=1, source_target_pairs={{8,0},{16,8},{24,16},{32,24},{40,32},{48,40},{56,48},{64,56},{72,6... | collective-permute-start | bytes 786440 | tf_op jit(solution)/shard_map/ppermute | solution.py:474
  3.8 9.4 %collective-permute-start.1 = (bf16[256,512]{1,0:T(8,128)(2,1)}, bf16[256,512]{1,0:T(8,128)(2,1)S(1)}, u32[]{:S(2)}, u32[]{:S(2)}) collective-permute-start(bf16[256,512]{1,0:T(8,128)(2,1)} %bitcast.7), channel_id=1, source_target_pairs={{0,8},{8,16},{16,24},{24,32},{32,40},{40,48},{48,56},{56,64},{64,7... | collective-permute-start | bytes 786440 | tf_op jit(solution)/shard_map/ppermute | solution.py:474
  10.0 12.2 %copy-start.7 = (bf16[512,512]{1,0:T(8,128)(2,1)S(1)}, bf16[512,512]{1,0:T(8,128)(2,1)}, u32[]{:S(2)}) copy-start(bf16[512,512]{1,0:T(8,128)(2,1)} %out_ref.9) | copy-start | bytes 1572868
  10.0 12.2 %copy-start.10 = (bf16[512,512]{1,0:T(8,128)(2,1)S(1)}, bf16[512,512]{1,0:T(8,128)(2,1)}, u32[]{:S(2)}) copy-start(bf16[512,512]{1,0:T(8,128)(2,1)} %recv_ref.7) | copy-start | bytes 1572868
  10.0 12.2 %copy-start.11 = (bf16[512,512]{1,0:T(8,128)(2,1)S(1)}, bf16[512,512]{1,0:T(8,128)(2,1)}, u32[]{:S(2)}) copy-start(bf16[512,512]{1,0:T(8,128)(2,1)} %dec_send_ref.3) | copy-start | bytes 1572868
  10.0 12.2 %copy-start.14 = (bf16[512,512]{1,0:T(8,128)(2,1)S(1)}, bf16[512,512]{1,0:T(8,128)(2,1)}, u32[]{:S(2)}) copy-start(bf16[512,512]{1,0:T(8,128)(2,1)} %send_ref.1) | copy-start | bytes 1572868
  10.0 12.2 %copy-start.18 = (bf16[1,1,256,512]{3,2,1,0:T(8,128)(2,1)S(1)}, bf16[1,1,256,512]{3,2,1,0:T(8,128)(2,1)}, u32[]{:S(2)}) copy-start(bf16[1,1,256,512]{3,2,1,0:T(8,128)(2,1)} %param.17) | copy-start | bytes 786436
  14.0 6.9 %collective-permute-start.2 = (bf16[64,512]{1,0:T(8,128)(2,1)}, bf16[64,512]{1,0:T(8,128)(2,1)}, u32[]{:S(2)}, u32[]{:S(2)}) collective-permute-start(bf16[64,512]{1,0:T(8,128)(2,1)} %reshape.154), channel_id=1, source_target_pairs={{0,1},{1,2},{2,3},{3,4},{4,5},{5,6},{6,7},{7,0},{8,9},{9,10},{10,1... | collective-permute-start | bytes 196616 | tf_op jit(solution)/shard_map/ppermute | solution.py:469
  18.1 4.0 %collective-permute-start.3 = (bf16[64,512]{1,0:T(8,128)(2,1)}, bf16[64,512]{1,0:T(8,128)(2,1)}, u32[]{:S(2)}, u32[]{:S(2)}) collective-permute-start(bf16[64,512]{1,0:T(8,128)(2,1)} %reshape.155), channel_id=1, source_target_pairs={{0,7},{1,0},{2,1},{3,2},{4,3},{5,4},{6,5},{7,6},{8,15},{9,8},{10,9... | collective-permute-start | bytes 196616 | tf_op jit(solution)/shard_map/ppermute | solution.py:469
  50.0 12.5 %copy-start.8 = (bf16[8192,512]{1,0:T(8,128)(2,1)}, bf16[8192,512]{1,0:T(8,128)(2,1)S(1)}, u32[]{:S(2)}) copy-start(bf16[8192,512]{1,0:T(8,128)(2,1)S(1)} %get-tuple-element.81.slope_ref) | copy-start | bytes 25165828
  50.0 12.5 %copy-start.9 = (bf16[8192,512]{1,0:T(8,128)(2,1)}, bf16[8192,512]{1,0:T(8,128)(2,1)S(1)}, u32[]{:S(2)}) copy-start(bf16[8192,512]{1,0:T(8,128)(2,1)S(1)} %get-tuple-element.82.hidden_ref) | copy-start | bytes 25165828
  50.0 15.8 %collective-permute-start.4 = (bf16[256,512]{1,0:T(8,128)(2,1)S(1)}, bf16[256,512]{1,0:T(8,128)(2,1)S(1)}, u32[]{:S(2)}, u32[]{:S(2)}) collective-permute-start(bf16[256,512]{1,0:T(8,128)(2,1)S(1)} %get-tuple-element.64), channel_id=1, source_target_pairs={{8,0},{16,8},{24,16},{32,24},{40,32},{48,40},{56,48},{64,56},{72,6... | collective-permute-start | bytes 786440 | tf_op jit(solution)/shard_map/ppermute | solution.py:474
  51.3 14.5 %collective-permute-start.5 = (bf16[256,512]{1,0:T(8,128)(2,1)S(1)}, bf16[256,512]{1,0:T(8,128)(2,1)S(1)}, u32[]{:S(2)}, u32[]{:S(2)}) collective-permute-start(bf16[256,512]{1,0:T(8,128)(2,1)S(1)} %get-tuple-element.64), channel_id=1, source_target_pairs={{0,8},{8,16},{16,24},{24,32},{32,40},{40,48},{48,56},{56,64},{64,7... | collective-permute-start | bytes 786440 | tf_op jit(solution)/shard_map/ppermute | solution.py:474
  65.9 14.9 %collective-permute-start.6 = (bf16[768,512]{1,0:T(8,128)(2,1)S(1)}, bf16[768,512]{1,0:T(8,128)(2,1)}, u32[]{:S(2)}, u32[]{:S(2)}) collective-permute-start(bf16[768,512]{1,0:T(8,128)(2,1)S(1)} %pad_maximum_fusion.2.centre_ref), channel_id=1, source_target_pairs={{0,1},{1,2},{2,3},{3,4},{4,5},{5,6},{6,7},{7,0},{8,9},{9,10},{10,1... | collective-permute-start | bytes 2359304 | tf_op jit(solution)/shard_map/ppermute | solution.py:469
  66.7 14.1 %collective-permute-start.7 = (bf16[768,512]{1,0:T(8,128)(2,1)S(1)}, bf16[768,512]{1,0:T(8,128)(2,1)}, u32[]{:S(2)}, u32[]{:S(2)}) collective-permute-start(bf16[768,512]{1,0:T(8,128)(2,1)S(1)} %pad_maximum_fusion.2.centre_ref), channel_id=1, source_target_pairs={{0,7},{1,0},{2,1},{3,2},{4,3},{5,4},{6,5},{7,6},{8,15},{9,8},{10,9... | collective-permute-start | bytes 2359304 | tf_op jit(solution)/shard_map/ppermute | solution.py:469
  91.8 11.7 %collective-permute-start.8 = (bf16[768,512]{1,0:T(8,128)(2,1)S(1)}, bf16[768,512]{1,0:T(8,128)(2,1)S(1)}, u32[]{:S(2)}, u32[]{:S(2)}) collective-permute-start(bf16[768,512]{1,0:T(8,128)(2,1)S(1)} %get-tuple-element.78), channel_id=1, source_target_pairs={{0,7},{1,0},{2,1},{3,2},{4,3},{5,4},{6,5},{7,6},{8,15},{9,8},{10,9... | collective-permute-start | bytes 2359304 | tf_op jit(solution)/shard_map/ppermute | solution.py:469
  94.5 9.0 %collective-permute-start.9 = (bf16[768,512]{1,0:T(8,128)(2,1)S(1)}, bf16[768,512]{1,0:T(8,128)(2,1)S(1)}, u32[]{:S(2)}, u32[]{:S(2)}) collective-permute-start(bf16[768,512]{1,0:T(8,128)(2,1)S(1)} %get-tuple-element.79), channel_id=1, source_target_pairs={{0,1},{1,2},{2,3},{3,4},{4,5},{5,6},{6,7},{7,0},{8,9},{9,10},{10,1... | collective-permute-start | bytes 2359304 | tf_op jit(solution)/shard_map/ppermute | solution.py:469
  97.3 7.7 %copy-start.12 = (bf16[512,512]{1,0:T(8,128)(2,1)}, bf16[512,512]{1,0:T(8,128)(2,1)S(1)}, u32[]{:S(2)}) copy-start(bf16[512,512]{1,0:T(8,128)(2,1)S(1)} %get-tuple-element.86) | copy-start | bytes 1572868
  105.8 14.4 %copy-start.19 = (bf16[1,1,256,512]{3,2,1,0:T(8,128)(2,1)S(1)}, bf16[1,1,256,512]{3,2,1,0:T(8,128)(2,1)}, u32[]{:S(2)}) copy-start(bf16[1,1,256,512]{3,2,1,0:T(8,128)(2,1)} %param.17) | copy-start | bytes 786436
  105.8 14.5 %copy-start.29 = (f32[256,32]{1,0:T(8,128)S(1)}, f32[256,32]{1,0:T(8,128)}, u32[]{:S(2)}) copy-start(f32[256,32]{1,0:T(8,128)} %copy-done.28) | copy-start | bytes 98308
  105.8 10.9 %collective-permute-start.10 = (bf16[256,512]{1,0:T(8,128)(2,1)}, bf16[256,512]{1,0:T(8,128)(2,1)}, u32[]{:S(2)}, u32[]{:S(2)}) collective-permute-start(bf16[256,512]{1,0:T(8,128)(2,1)} %get-tuple-element.111), channel_id=1, source_target_pairs={{0,8},{8,16},{16,24},{24,32},{32,40},{40,48},{48,56},{56,64},{64,7... | collective-permute-start | bytes 786440 | tf_op jit(solution)/shard_map/ppermute | solution.py:474
  110.3 7.4 %collective-permute-start.11 = (bf16[256,512]{1,0:T(8,128)(2,1)}, bf16[256,512]{1,0:T(8,128)(2,1)}, u32[]{:S(2)}, u32[]{:S(2)}) collective-permute-start(bf16[256,512]{1,0:T(8,128)(2,1)} %get-tuple-element.112), channel_id=1, source_target_pairs={{8,0},{16,8},{24,16},{32,24},{40,32},{48,40},{56,48},{64,56},{72,6... | collective-permute-start | bytes 786440 | tf_op jit(solution)/shard_map/ppermute | solution.py:474
  123.7 31.4 %copy-start.13 = (bf16[512,512]{1,0:T(8,128)(2,1)S(1)}, bf16[512,512]{1,0:T(8,128)(2,1)}, u32[]{:S(2)}) copy-start(bf16[512,512]{1,0:T(8,128)(2,1)} %copy-done.12) | copy-start | bytes 1572868
  155.5 8.5 %collective-permute-start.12 = (bf16[1536,512]{1,0:T(8,128)(2,1)S(1)}, bf16[1536,512]{1,0:T(8,128)(2,1)S(1)}, u32[]{:S(2)}, u32[]{:S(2)}) collective-permute-start(bf16[1536,512]{1,0:T(8,128)(2,1)S(1)} %broadcast_select_fusion), channel_id=1, source_target_pairs={{0,1},{1,0},{2,3},{3,2},{4,5},{5,4},{6,7},{7,6},{8,9},{9,8},{10,11... | collective-permute-start | bytes 4718600 | tf_op jit(solution)/shard_map/ppermute | solution.py:478
  161.0 4.8 %collective-permute-start.13 = (bf16[64,512]{1,0:T(8,128)(2,1)S(1)}, bf16[64,512]{1,0:T(8,128)(2,1)S(1)}, u32[]{:S(2)}, u32[]{:S(2)}) collective-permute-start(bf16[64,512]{1,0:T(8,128)(2,1)S(1)} %get-tuple-element.106), channel_id=1, source_target_pairs={{0,7},{1,0},{2,1},{3,2},{4,3},{5,4},{6,5},{7,6},{8,15},{9,8},{10,9... | collective-permute-start | bytes 196616 | tf_op jit(solution)/shard_map/ppermute | solution.py:469
  161.3 4.6 %collective-permute-start.14 = (bf16[64,512]{1,0:T(8,128)(2,1)S(1)}, bf16[64,512]{1,0:T(8,128)(2,1)S(1)}, u32[]{:S(2)}, u32[]{:S(2)}) collective-permute-start(bf16[64,512]{1,0:T(8,128)(2,1)S(1)} %get-tuple-element.105), channel_id=1, source_target_pairs={{0,1},{1,2},{2,3},{3,4},{4,5},{5,6},{6,7},{7,0},{8,9},{9,10},{10,1... | collective-permute-start | bytes 196616 | tf_op jit(solution)/shard_map/ppermute | solution.py:469
  165.8 15.8 %copy-start.17 = (bf16[1152,512]{1,0:T(8,128)(2,1)S(1)}, bf16[1152,512]{1,0:T(8,128)(2,1)}, u32[]{:S(2)}) copy-start(bf16[1152,512]{1,0:T(8,128)(2,1)} %copy-done.16) | copy-start | bytes 3538948
  165.8 38.1 %all-to-all-start = ((bf16[64,24,512]{2,1,0:T(8,128)(2,1)}), bf16[64,24,512]{2,1,0:T(8,128)(2,1)}, u32[]{:S(2)}, u32[]{:S(2)}) async-start(bf16[64,24,512]{2,1,0:T(8,128)(2,1)} %bitcast.62), calls=%async_computation | async-start | bytes 3145728 | tf_op jit(solution)/shard_map/all_to_all | solution.py:484
  182.5 23.2 %collective-permute-start.15 = (bf16[256,512]{1,0:T(8,128)(2,1)S(1)}, bf16[256,512]{1,0:T(8,128)(2,1)S(1)}, u32[]{:S(2)}, u32[]{:S(2)}) collective-permute-start(bf16[256,512]{1,0:T(8,128)(2,1)S(1)} %bitcast.67), channel_id=1, source_target_pairs={{0,8},{8,16},{16,24},{24,32},{32,40},{40,48},{48,56},{56,64},{64,7... | collective-permute-start | bytes 786440 | tf_op jit(solution)/shard_map/ppermute | solution.py:474
  185.4 20.3 %collective-permute-start.16 = (bf16[256,512]{1,0:T(8,128)(2,1)S(1)}, bf16[256,512]{1,0:T(8,128)(2,1)S(1)}, u32[]{:S(2)}, u32[]{:S(2)}) collective-permute-start(bf16[256,512]{1,0:T(8,128)(2,1)S(1)} %bitcast.66), channel_id=1, source_target_pairs={{8,0},{16,8},{24,16},{32,24},{40,32},{48,40},{56,48},{64,56},{72,6... | collective-permute-start | bytes 786440 | tf_op jit(solution)/shard_map/ppermute | solution.py:474
  235.8 6.5 %collective-permute-start.17 = (bf16[1536,512]{1,0:T(8,128)(2,1)S(1)}, bf16[1536,512]{1,0:T(8,128)(2,1)S(1)}, u32[]{:S(2)}, u32[]{:S(2)}) collective-permute-start(bf16[1536,512]{1,0:T(8,128)(2,1)S(1)} %bitcast.61), channel_id=1, source_target_pairs={{0,1},{1,0},{2,3},{3,2},{4,5},{5,4},{6,7},{7,6},{8,9},{9,8},{10,11... | collective-permute-start | bytes 4718600 | tf_op jit(solution)/shard_map/ppermute | solution.py:478
  (19 other events, 68.0 us)

commit v2 on v1

--- a/solution.py
+++ b/solution.py
@@ -156,9 +156,9 @@
         out_shape=[
             jax.ShapeDtypeStruct((nodes, width), BF),
             jax.ShapeDtypeStruct((nodes, width), BF),
-            jax.ShapeDtypeStruct((nodes * degree, width), BF),
-            jax.ShapeDtypeStruct((nodes * degree, width), BF),
-            jax.ShapeDtypeStruct((nodes * degree, width), BF),
+            pltpu.HBM((nodes * degree, width), BF),
+            pltpu.HBM((nodes * degree, width), BF),
+            pltpu.HBM((nodes * degree, width), BF),
             jax.ShapeDtypeStruct((nodes, degree), F32),
         ],
         scratch_shapes=[
@@ -185,9 +185,9 @@
         grid=(count,),
         in_specs=[per_edge, whole((width, width))] + [pl.BlockSpec(memory_space=pl.ANY)] * len(kept),
         out_specs=per_edge,
-        out_shape=jax.ShapeDtypeStruct(normed.shape, BF),
+        out_shape=pltpu.HBM(normed.shape, BF),
         input_output_aliases={2: 0} if kept else {},
-        compiler_params=kernel_params(12),
+        compiler_params=kernel_params(56),
         cost_estimate=pl.CostEstimate(flops=2 * share * width, bytes_accessed=4 * share, transcendentals=0),
     )(normed, enc_out, *kept)
 
@@ -460,7 +460,7 @@
             pltpu.VMEM((nodes, width), F32),
             pltpu.VMEM((nodes, width), BF),
         ],
-        compiler_params=kernel_params(40),
+        compiler_params=kernel_params(56),
     )(idx_rows, scale, mesh_rows, moved_cot, normed, turned, slope, hidden, *pieces, dec_send, enc_recv, enc_out)
 
 

time: 247 us -> 245 us (level)
  local copies, waits for them, and re-layouts: 37.2 us -> 16.1 us
  Pallas kernels: 76.6 us -> 86.6 us
  other arithmetic: 11.9 us -> 17.7 us
    unnamed x65 -> x41, local copies, waits for them, and re-layouts: 25.1 us -> 4.2 us
    all_to_all x1, waiting for transfers between devices: 17.3 us -> 8.67 us  [across_chips(): lax.all_to_all(parts, ('lat', 'lon'), 0, 0, axis_index_groups=alike, tile...]
    pallas_call x2, Pallas kernels: 5.98 us -> 12.7 us  [enc_between(): pl.pallas_call(enc_between_kernel, name='enc_between', grid=(count,), in_...]
    ppermute x8, waiting for transfers between devices: 7.45 us -> 13.3 us  [to_lon(): lax.ppermute(shard, 'lon', [(i, (i + by) % count) for i in range(count)])]
    ppermute x8, waiting for transfers between devices: 4.15 us -> 8.93 us  [to_lat(): lax.ppermute(shard, 'lat', [(i, i + by) for i in range(count) if 0 <= i +...]
    all_to_all x1, starting transfers between devices: 15.8 us -> 19.7 us  [across_chips(): lax.all_to_all(parts, ('lat', 'lon'), 0, 0, axis_index_groups=alike, tile...]
    pallas_call x1, Pallas kernels: 31.4 us -> 33.9 us  [enc_backward(): pl.pallas_call(enc_backward_kernel, name='enc_backward', grid=(tiles + 1,...]
  transfers between devices with their start and end apart: 19 -> 19, of which waited for: 8 -> 12; matrix products, arithmetic and copies ran while one was open for 7% -> 9% of each run, Pallas kernels for 4% -> 6%
where the time goes in v2:
time: 245 us; the launch traced here: 244 us
  Pallas kernels  86.6 us (35%)
  starting transfers between devices  57.7 us (24%)
  waiting for transfers between devices  31.8 us (13%)
  blocking collectives  31.5 us (13%)
  other arithmetic  17.7 us (7%)
  local copies, waits for them, and re-layouts  16.1 us (7%)
    pallas_call x1, Pallas kernels, enc_backward(): pl.pallas_call(enc_backward_kernel, name='enc_backward', grid=(tiles + 1,...  33.9 us
    all_to_all x1, blocking collectives, across_chips(): lax.all_to_all(parts, ('lat', 'lon'), 0, 0, axis_index_groups=alike, tile...  31.5 us
    pallas_call x1, Pallas kernels, enc_forward(): pl.pallas_call(enc_forward_kernel, name='enc_forward', grid=(nodes // til...  26.5 us
    ppermute x8, starting transfers between devices, to_lat(): lax.ppermute(shard, 'lat', [(i, i + by) for i in range(count) if 0 <= i +...  22.3 us
    all_to_all x1, starting transfers between devices, across_chips(): lax.all_to_all(parts, ('lat', 'lon'), 0, 0, axis_index_groups=alike, tile...  19.7 us
    ppermute x8, waiting for transfers between devices, to_lon(): lax.ppermute(shard, 'lon', [(i, (i + by) % count) for i in range(count)])  13.3 us
    pallas_call x2, Pallas kernels, enc_between(): pl.pallas_call(enc_between_kernel, name='enc_between', grid=(count,), in_...  12.7 us
    pallas_call x1, Pallas kernels, decoder(): pl.pallas_call(decoder_kernel, name='decoder', out_shape=[node_shape, edg...  10.7 us
  transfers between devices with their start and end apart: 19, of which 12 were waited for; matrix products, arithmetic and copies ran while one was open for 9% of the time, Pallas kernels for 6%

profile of v2, /device:TPU:1, one launch (start us, length us, event | category | flops | bytes accessed | tf_op | source)
XLA Modules:
  0.0 243.8 jit_solution(12757527938610774297)
XLA Ops:
  0.7 1.9 fusion.41
  3.9 4.6 %collective-permute-start.1 = (bf16[256,512]{1,0:T(8,128)(2,1)}, bf16[256,512]{1,0:T(8,128)(2,1)S(1)}, u32[]{:S(2)}, u32[]{:S(2)}) collective-permute-start(bf16[256,512]{1,0:T(8,128)(2,1)} %bitcast.7), channel_id=1, source_target_pairs={{0,8},{8,16},{16,24},{24,32},{32,40},{40,48},{48,56},{56,64},{64,7... | collective-permute-start | bytes 786440 | tf_op jit(solution)/shard_map/ppermute | solution.py:474
  8.5 1.5 copy.28
  10.0 2.2 collective-permute-done.high_ref
  14.0 3.5 %collective-permute-start.2 = (bf16[64,512]{1,0:T(8,128)(2,1)}, bf16[64,512]{1,0:T(8,128)(2,1)}, u32[]{:S(2)}, u32[]{:S(2)}) collective-permute-start(bf16[64,512]{1,0:T(8,128)(2,1)} %reshape.154), channel_id=1, source_target_pairs={{0,1},{1,2},{2,3},{3,4},{4,5},{5,6},{6,7},{7,0},{8,9},{9,10},{10,1... | collective-permute-start | bytes 196616 | tf_op jit(solution)/shard_map/ppermute | solution.py:469
  23.1 26.5 %enc_forward.1 = (bf16[256,512]{1,0:T(8,128)(2,1)S(1)}, bf16[256,512]{1,0:T(8,128)(2,1)S(1)}, bf16[8192,512]{1,0:T(8,128)(2,1)}, bf16[8192,512]{1,0:T(8,128)(2,1...) custom-call(s32[256,32]{1,0:T(8,128)S(1)} %select_select_fusion.idx_ref, s32[256,1]{1,0:T(8,128)S(1)} %copy-done.11, ...), custom_call_target="tpu_custom_call" | custom-call | tf_op jit(solution)/shard_map/enc_forward/pallas_call | solution.py:145
  52.2 4.8 %collective-permute-start.5 = (bf16[256,512]{1,0:T(8,128)(2,1)S(1)}, bf16[256,512]{1,0:T(8,128)(2,1)S(1)}, u32[]{:S(2)}, u32[]{:S(2)}) collective-permute-start(bf16[256,512]{1,0:T(8,128)(2,1)S(1)} %get-tuple-element.64), channel_id=1, source_target_pairs={{0,8},{8,16},{16,24},{24,32},{32,40},{40,48},{48,56},{56,64},{64,7... | collective-permute-start | bytes 786440 | tf_op jit(solution)/shard_map/ppermute | solution.py:474
  57.1 6.3 %enc_between.2.refs_0_ = bf16[8192,512]{1,0:T(8,128)(2,1)} custom-call(bf16[8192,512]{1,0:T(8,128)(2,1)} %get-tuple-element.65.normed_ref, bf16[512,512]{1,0:T(8,128)(2,1)} %out_ref.9), custom_call_target="tpu_custom_call" | custom-call | flops 2147483648 | bytes 8388608 | tf_op jit(solution)/shard_map/enc_between/pallas_call | solution.py:182
  64.7 6.4 %enc_between.3.turned_ref = bf16[8192,512]{1,0:T(8,128)(2,1)} custom-call(bf16[8192,512]{1,0:T(8,128)(2,1)} %get-tuple-element.65.normed_ref, bf16[512,512]{1,0:T(8,128)(2,1)} %out_ref.9, bf16[8192,512]{1,0:T(8,128)(2,1)} %enc_between.2.refs_0_), custom_call_target="tpu_custom_call", output_to_operand_aliasing={{}: (2, {})} | custom-call | flops 2147483648 | bytes 8388608 | tf_op jit(solution)/shard_map/enc_between/pallas_call | solution.py:182
  71.1 2.1 collective-permute-done.6.left_ref
  73.2 2.8 %collective-permute-done.7.right_ref = bf16[768,512]{1,0:T(8,128)(2,1)} collective-permute-done((bf16[768,512]{1,0:T(8,128)(2,1)S(1)}, bf16[768,512]{1,0:T(8,128)(2,1)}, u32[]{:S(2)}, u32[]{:S(2)}) %collective-permute-start.7) | collective-permute-done | bytes 786464 | tf_op jit(solution)/shard_map/ppermute | solution.py:469
  76.0 10.7 %decoder.1 = (bf16[512,512]{1,0:T(8,128)(2,1)}, bf16[1536,512]{1,0:T(8,128)(2,1)S(1)}, bf16[1536,512]{1,0:T(8,128)(2,1)S(1)}, bf16[1536,512]{1,0:T(8,128)(2,1)S(...) custom-call(s32[512,3]{1,0:T(8,128)S(1)} %copy.30.idx_ref, ...), custom_call_target="tpu_custom_call" | custom-call | tf_op jit(solution)/shard_map/decoder/pallas_call | solution.py:277
  88.4 2.7 %decoder_rest.1 = (f32[512,512]{1,0:T(8,128)S(1)}, bf16[512,512]{1,0:T(8,128)(2,1)S(1)}, bf16[512,512]{1,0:T(8,128)(2,1)S(1)}, bf16[768,512]{1,0:T(8,128)(2,1)S(1)}) custom-call(s32[3,512]{1,0:T(4,128)S(1)} %fusion.30.idx_row_ref, bf16[512,512]{1,0:T(8,128)(2,1)S(1)} %bitcast.56, bf16[512,512]{1,0:T(8,128)(2,1)S(1)} %bitcast.60, ...), custom_call_target="tpu_custom_call" | custom-call | flops 2818572288 | bytes 6291456 | tf_op jit(solution)/shard_map/decoder_rest/pallas_call | solution.py:315
  91.2 7.2 %collective-permute-done.8 = bf16[768,512]{1,0:T(8,128)(2,1)S(1)} collective-permute-done((bf16[768,512]{1,0:T(8,128)(2,1)S(1)}, bf16[768,512]{1,0:T(8,128)(2,1)S(1)}, u32[]{:S(2)}, u32[]{:S(2)}) %collective-permute-start.8) | collective-permute-done | bytes 786464 | tf_op jit(solution)/shard_map/ppermute | solution.py:469
  98.4 1.5 fusion.34
  100.8 3.9 %collective-permute-start.10 = (bf16[256,512]{1,0:T(8,128)(2,1)}, bf16[256,512]{1,0:T(8,128)(2,1)S(1)}, u32[]{:S(2)}, u32[]{:S(2)}) collective-permute-start(bf16[256,512]{1,0:T(8,128)(2,1)} %get-tuple-element.111), channel_id=1, source_target_pairs={{0,8},{8,16},{16,24},{24,32},{32,40},{40,48},{48,56},{56,64},{64,7... | collective-permute-start | bytes 786440 | tf_op jit(solution)/shard_map/ppermute | solution.py:474
  108.3 4.2 %collective-permute-done.11 = bf16[256,512]{1,0:T(8,128)(2,1)} collective-permute-done((bf16[256,512]{1,0:T(8,128)(2,1)}, bf16[256,512]{1,0:T(8,128)(2,1)}, u32[]{:S(2)}, u32[]{:S(2)}) %collective-permute-start.11) | collective-permute-done | bytes 262176 | tf_op jit(solution)/shard_map/ppermute | solution.py:474
  114.4 33.9 %enc_backward.1 = (bf16[256,512]{1,0:T(8,128)(2,1)}, bf16[1152,512]{1,0:T(8,128)(2,1)}, bf16[1536,512]{1,0:T(8,128)(2,1)}) custom-call(s32[8,1,1024]{2,1,0:T(1,128)} %reshape.158.idx_row_ref, f32[256,32]{1,0:T(8,128)} %copy-done.14, bf16[256,512]{1,0:T(8,128)(2,1)} %bitcast.57, bf16[256,512]{1,0:T(8,128)(2,1)} %copy-done.17, ...), custom_call_target="tpu_custom_call" | custom-call | tf_op jit(solution)/shard_map/enc_backward/pallas_call | solution.py:432
  148.4 2.0 broadcast_select_fusion
  150.3 4.4 %collective-permute-start.12 = (bf16[1536,512]{1,0:T(8,128)(2,1)S(1)}, bf16[1536,512]{1,0:T(8,128)(2,1)S(1)}, u32[]{:S(2)}, u32[]{:S(2)}) collective-permute-start(bf16[1536,512]{1,0:T(8,128)(2,1)S(1)} %broadcast_select_fusion), channel_id=1, source_target_pairs={{0,1},{1,0},{2,3},{3,2},{4,5},{5,4},{6,7},{7,6},{8,9},{9,8},{10,11... | collective-permute-start | bytes 4718600 | tf_op jit(solution)/shard_map/ppermute | solution.py:478
  155.6 1.7 collective-permute-start.14
  157.7 1.8 add_convert_fusion
  159.5 19.7 %all-to-all-start = ((bf16[64,24,512]{2,1,0:T(8,128)(2,1)}), bf16[64,24,512]{2,1,0:T(8,128)(2,1)S(1)}, u32[]{:S(2)}, u32[]{:S(2)}) async-start(bf16[64,24,512]{2,1,0:T(8,128)(2,1)} %bitcast.62), calls=%async_computation | async-start | bytes 3145728 | tf_op jit(solution)/shard_map/all_to_all | solution.py:484
  180.6 1.6 convert.22
  182.3 1.7 fusion.17
  184.0 1.7 fusion.16
  185.6 1.7 convert.19
  188.1 3.6 %collective-permute-start.15 = (bf16[256,512]{1,0:T(8,128)(2,1)}, bf16[256,512]{1,0:T(8,128)(2,1)}, u32[]{:S(2)}, u32[]{:S(2)}) collective-permute-start(bf16[256,512]{1,0:T(8,128)(2,1)} %bitcast.15), channel_id=1, source_target_pairs={{0,8},{8,16},{16,24},{24,32},{32,40},{40,48},{48,56},{56,64},{64,7... | collective-permute-start | bytes 786440 | tf_op jit(solution)/shard_map/ppermute | solution.py:474
  193.0 8.7 %all-to-all-done = bf16[64,24,512]{2,1,0:T(8,128)(2,1)S(1)} async-done(((bf16[64,24,512]{2,1,0:T(8,128)(2,1)}), bf16[64,24,512]{2,1,0:T(8,128)(2,1)S(1)}, u32[]{:S(2)}, u32[]{:S(2)}) %all-to-all-start) | async-done | bytes 1572896 | tf_op jit(solution)/shard_map/all_to_all | solution.py:484
  202.6 31.5 %all_to_all.10 = bf16[64,24,512]{2,1,0:T(8,128)(2,1)S(1)} all-to-all(bf16[64,24,512]{2,1,0:T(8,128)(2,1)S(1)} %broadcast_in_dim.12), channel_id=1, replica_groups={{0,2,4,6,8,10,12,14,16,18,20,22,24,26,28,30,32,34,36,38,40,42,44,46,48,..., dimensions={0} | all-to-all | bytes 3145728 | tf_op jit(solution)/shard_map/all_to_all | solution.py:484
  234.1 3.5 %collective-permute-start.17 = (bf16[1536,512]{1,0:T(8,128)(2,1)S(1)}, bf16[1536,512]{1,0:T(8,128)(2,1)S(1)}, u32[]{:S(2)}, u32[]{:S(2)}) collective-permute-start(bf16[1536,512]{1,0:T(8,128)(2,1)S(1)} %bitcast.61), channel_id=1, source_target_pairs={{0,1},{1,0},{2,3},{3,2},{4,5},{5,4},{6,7},{7,6},{8,9},{9,8},{10,11... | collective-permute-start | bytes 4718600 | tf_op jit(solution)/shard_map/ppermute | solution.py:478
  241.1 2.7 %fusion.35 = (f32[512,512]{1,0:T(8,128)}, f32[512,512]{1,0:T(8,128)}, f32[512,512]{1,0:T(8,128)}, f32[512,512]{1,0:T(8,128)}, f32[512,512]{1,0:T(8,128)}, /*index=5*/f32[512,512]{1,0:T(8,128)}) fusion(f32[1536,512]{1,0:T(8,128)S(1)} %get-tuple-element.100, f32[1536,512]{1,0:T(8,128)S(1)} %get-tuple-element.101), kind=kLoop, calls=%fused_computation.92 | loop fusion | bytes 12582912 | tf_op jit(solution)/shard_map/slice | solution.py:609
  (92 shorter events, 29.7 us)
Async XLA Ops:
  0.6 12.6 %copy-start = (bf16[8,64,512]{2,1,0:T(8,128)(2,1)S(1)}, bf16[8,64,512]{2,1,0:T(8,128)(2,1)}, u32[]{:S(2)}) copy-start(bf16[8,64,512]{2,1,0:T(8,128)(2,1)} %param.16) | copy-start | bytes 1572868
  2.6 9.7 %collective-permute-start = (bf16[256,512]{1,0:T(8,128)(2,1)}, bf16[256,512]{1,0:T(8,128)(2,1)S(1)}, u32[]{:S(2)}, u32[]{:S(2)}) collective-permute-start(bf16[256,512]{1,0:T(8,128)(2,1)} %bitcast.6), channel_id=1, source_target_pairs={{8,0},{16,8},{24,16},{32,24},{40,32},{48,40},{56,48},{64,56},{72,6... | collective-permute-start | bytes 786440 | tf_op jit(solution)/shard_map/ppermute | solution.py:474
  3.9 9.4 %collective-permute-start.1 = (bf16[256,512]{1,0:T(8,128)(2,1)}, bf16[256,512]{1,0:T(8,128)(2,1)S(1)}, u32[]{:S(2)}, u32[]{:S(2)}) collective-permute-start(bf16[256,512]{1,0:T(8,128)(2,1)} %bitcast.7), channel_id=1, source_target_pairs={{0,8},{8,16},{16,24},{24,32},{32,40},{40,48},{48,56},{56,64},{64,7... | collective-permute-start | bytes 786440 | tf_op jit(solution)/shard_map/ppermute | solution.py:474
  10.0 12.2 %copy-start.1 = (bf16[512,512]{1,0:T(8,128)(2,1)S(1)}, bf16[512,512]{1,0:T(8,128)(2,1)}, u32[]{:S(2)}) copy-start(bf16[512,512]{1,0:T(8,128)(2,1)} %out_ref.9) | copy-start | bytes 1572868
  10.0 12.2 %copy-start.4 = (bf16[512,512]{1,0:T(8,128)(2,1)S(1)}, bf16[512,512]{1,0:T(8,128)(2,1)}, u32[]{:S(2)}) copy-start(bf16[512,512]{1,0:T(8,128)(2,1)} %recv_ref.7) | copy-start | bytes 1572868
  10.0 12.2 %copy-start.5 = (bf16[512,512]{1,0:T(8,128)(2,1)S(1)}, bf16[512,512]{1,0:T(8,128)(2,1)}, u32[]{:S(2)}) copy-start(bf16[512,512]{1,0:T(8,128)(2,1)} %dec_send_ref.3) | copy-start | bytes 1572868
  10.0 12.2 %copy-start.6 = (bf16[512,512]{1,0:T(8,128)(2,1)S(1)}, bf16[512,512]{1,0:T(8,128)(2,1)}, u32[]{:S(2)}) copy-start(bf16[512,512]{1,0:T(8,128)(2,1)} %send_ref.1) | copy-start | bytes 1572868
  10.0 12.2 %copy-start.7 = (bf16[1,1,256,512]{3,2,1,0:T(8,128)(2,1)S(1)}, bf16[1,1,256,512]{3,2,1,0:T(8,128)(2,1)}, u32[]{:S(2)}) copy-start(bf16[1,1,256,512]{3,2,1,0:T(8,128)(2,1)} %param.17) | copy-start | bytes 786436
  12.2 37.3 %copy-start.2 = (bf16[256,512]{1,0:T(8,128)(2,1)}, bf16[256,512]{1,0:T(8,128)(2,1)S(1)}, u32[]{:S(2)}) copy-start(bf16[256,512]{1,0:T(8,128)(2,1)S(1)} %collective-permute-done.high_ref) | copy-start | bytes 786436
  13.2 36.4 %copy-start.3 = (bf16[256,512]{1,0:T(8,128)(2,1)}, bf16[256,512]{1,0:T(8,128)(2,1)S(1)}, u32[]{:S(2)}) copy-start(bf16[256,512]{1,0:T(8,128)(2,1)S(1)} %collective-permute-done.1.low_ref) | copy-start | bytes 786436
  14.0 6.9 %collective-permute-start.2 = (bf16[64,512]{1,0:T(8,128)(2,1)}, bf16[64,512]{1,0:T(8,128)(2,1)}, u32[]{:S(2)}, u32[]{:S(2)}) collective-permute-start(bf16[64,512]{1,0:T(8,128)(2,1)} %reshape.154), channel_id=1, source_target_pairs={{0,1},{1,2},{2,3},{3,4},{4,5},{5,6},{6,7},{7,0},{8,9},{9,10},{10,1... | collective-permute-start | bytes 196616 | tf_op jit(solution)/shard_map/ppermute | solution.py:469
  18.1 4.0 %collective-permute-start.3 = (bf16[64,512]{1,0:T(8,128)(2,1)}, bf16[64,512]{1,0:T(8,128)(2,1)}, u32[]{:S(2)}, u32[]{:S(2)}) collective-permute-start(bf16[64,512]{1,0:T(8,128)(2,1)} %reshape.155), channel_id=1, source_target_pairs={{0,7},{1,0},{2,1},{3,2},{4,3},{5,4},{6,5},{7,6},{8,15},{9,8},{10,9... | collective-permute-start | bytes 196616 | tf_op jit(solution)/shard_map/ppermute | solution.py:469
  50.9 12.4 %collective-permute-start.4 = (bf16[256,512]{1,0:T(8,128)(2,1)S(1)}, bf16[256,512]{1,0:T(8,128)(2,1)S(1)}, u32[]{:S(2)}, u32[]{:S(2)}) collective-permute-start(bf16[256,512]{1,0:T(8,128)(2,1)S(1)} %get-tuple-element.64), channel_id=1, source_target_pairs={{8,0},{16,8},{24,16},{32,24},{40,32},{48,40},{56,48},{64,56},{72,6... | collective-permute-start | bytes 786440 | tf_op jit(solution)/shard_map/ppermute | solution.py:474
  52.2 11.1 %collective-permute-start.5 = (bf16[256,512]{1,0:T(8,128)(2,1)S(1)}, bf16[256,512]{1,0:T(8,128)(2,1)S(1)}, u32[]{:S(2)}, u32[]{:S(2)}) collective-permute-start(bf16[256,512]{1,0:T(8,128)(2,1)S(1)} %get-tuple-element.64), channel_id=1, source_target_pairs={{0,8},{8,16},{16,24},{24,32},{32,40},{40,48},{48,56},{56,64},{64,7... | collective-permute-start | bytes 786440 | tf_op jit(solution)/shard_map/ppermute | solution.py:474
  63.4 9.8 %collective-permute-start.6 = (bf16[768,512]{1,0:T(8,128)(2,1)S(1)}, bf16[768,512]{1,0:T(8,128)(2,1)S(1)}, u32[]{:S(2)}, u32[]{:S(2)}) collective-permute-start(bf16[768,512]{1,0:T(8,128)(2,1)S(1)} %pad_maximum_fusion.2.centre_ref), channel_id=1, source_target_pairs={{0,1},{1,2},{2,3},{3,4},{4,5},{5,6},{6,7},{7,0},{8,9},{9,10},{10,1... | collective-permute-start | bytes 2359304 | tf_op jit(solution)/shard_map/ppermute | solution.py:469
  64.3 11.7 %collective-permute-start.7 = (bf16[768,512]{1,0:T(8,128)(2,1)S(1)}, bf16[768,512]{1,0:T(8,128)(2,1)}, u32[]{:S(2)}, u32[]{:S(2)}) collective-permute-start(bf16[768,512]{1,0:T(8,128)(2,1)S(1)} %pad_maximum_fusion.2.centre_ref), channel_id=1, source_target_pairs={{0,7},{1,0},{2,1},{3,2},{4,3},{5,4},{6,5},{7,6},{8,15},{9,8},{10,9... | collective-permute-start | bytes 2359304 | tf_op jit(solution)/shard_map/ppermute | solution.py:469
  64.6 11.3 %copy-start.8 = (bf16[512,512]{1,0:T(8,128)(2,1)S(1)}, bf16[512,512]{1,0:T(8,128)(2,1)}, u32[]{:S(2)}) copy-start(bf16[512,512]{1,0:T(8,128)(2,1)} %out_ref.8) | copy-start | bytes 1572868
  64.7 11.3 %copy-start.9 = (bf16[8,64,512]{2,1,0:T(8,128)(2,1)S(1)}, bf16[8,64,512]{2,1,0:T(8,128)(2,1)}, u32[]{:S(2)}) copy-start(bf16[8,64,512]{2,1,0:T(8,128)(2,1)} %param.18) | copy-start | bytes 1572868
  64.7 11.3 %copy-start.10 = (bf16[512,512]{1,0:T(8,128)(2,1)S(1)}, bf16[512,512]{1,0:T(8,128)(2,1)}, u32[]{:S(2)}) copy-start(bf16[512,512]{1,0:T(8,128)(2,1)} %recv_ref.6) | copy-start | bytes 1572868
  86.7 11.7 %collective-permute-start.8 = (bf16[768,512]{1,0:T(8,128)(2,1)S(1)}, bf16[768,512]{1,0:T(8,128)(2,1)S(1)}, u32[]{:S(2)}, u32[]{:S(2)}) collective-permute-start(bf16[768,512]{1,0:T(8,128)(2,1)S(1)} %get-tuple-element.78), channel_id=1, source_target_pairs={{0,7},{1,0},{2,1},{3,2},{4,3},{5,4},{6,5},{7,6},{8,15},{9,8},{10,9... | collective-permute-start | bytes 2359304 | tf_op jit(solution)/shard_map/ppermute | solution.py:469
  87.4 11.0 %collective-permute-start.9 = (bf16[768,512]{1,0:T(8,128)(2,1)S(1)}, bf16[768,512]{1,0:T(8,128)(2,1)S(1)}, u32[]{:S(2)}, u32[]{:S(2)}) collective-permute-start(bf16[768,512]{1,0:T(8,128)(2,1)S(1)} %get-tuple-element.79), channel_id=1, source_target_pairs={{0,1},{1,2},{2,3},{3,4},{4,5},{5,6},{6,7},{7,0},{8,9},{9,10},{10,1... | collective-permute-start | bytes 2359304 | tf_op jit(solution)/shard_map/ppermute | solution.py:469
  99.9 13.8 %copy-start.13 = (bf16[256,512]{1,0:T(8,128)(2,1)S(1)}, bf16[256,512]{1,0:T(8,128)(2,1)}, u32[]{:S(2)}) copy-start(bf16[256,512]{1,0:T(8,128)(2,1)} %copy-done.12) | copy-start | bytes 786436
  100.8 7.5 %collective-permute-start.10 = (bf16[256,512]{1,0:T(8,128)(2,1)}, bf16[256,512]{1,0:T(8,128)(2,1)S(1)}, u32[]{:S(2)}, u32[]{:S(2)}) collective-permute-start(bf16[256,512]{1,0:T(8,128)(2,1)} %get-tuple-element.111), channel_id=1, source_target_pairs={{0,8},{8,16},{16,24},{24,32},{32,40},{40,48},{48,56},{56,64},{64,7... | collective-permute-start | bytes 786440 | tf_op jit(solution)/shard_map/ppermute | solution.py:474
  104.7 7.8 %collective-permute-start.11 = (bf16[256,512]{1,0:T(8,128)(2,1)}, bf16[256,512]{1,0:T(8,128)(2,1)}, u32[]{:S(2)}, u32[]{:S(2)}) collective-permute-start(bf16[256,512]{1,0:T(8,128)(2,1)} %get-tuple-element.112), channel_id=1, source_target_pairs={{8,0},{16,8},{24,16},{32,24},{40,32},{48,40},{56,48},{64,56},{72,6... | collective-permute-start | bytes 786440 | tf_op jit(solution)/shard_map/ppermute | solution.py:474
  150.3 7.4 %collective-permute-start.12 = (bf16[1536,512]{1,0:T(8,128)(2,1)S(1)}, bf16[1536,512]{1,0:T(8,128)(2,1)S(1)}, u32[]{:S(2)}, u32[]{:S(2)}) collective-permute-start(bf16[1536,512]{1,0:T(8,128)(2,1)S(1)} %broadcast_select_fusion), channel_id=1, source_target_pairs={{0,1},{1,0},{2,3},{3,2},{4,5},{5,4},{6,7},{7,6},{8,9},{9,8},{10,11... | collective-permute-start | bytes 4718600 | tf_op jit(solution)/shard_map/ppermute | solution.py:478
  155.6 4.0 %collective-permute-start.13 = (bf16[64,512]{1,0:T(8,128)(2,1)S(1)}, bf16[64,512]{1,0:T(8,128)(2,1)S(1)}, u32[]{:S(2)}, u32[]{:S(2)}) collective-permute-start(bf16[64,512]{1,0:T(8,128)(2,1)S(1)} %get-tuple-element.106), channel_id=1, source_target_pairs={{0,7},{1,0},{2,1},{3,2},{4,3},{5,4},{6,5},{7,6},{8,15},{9,8},{10,9... | collective-permute-start | bytes 196616 | tf_op jit(solution)/shard_map/ppermute | solution.py:469
  155.6 4.0 %collective-permute-start.14 = (bf16[64,512]{1,0:T(8,128)(2,1)S(1)}, bf16[64,512]{1,0:T(8,128)(2,1)S(1)}, u32[]{:S(2)}, u32[]{:S(2)}) collective-permute-start(bf16[64,512]{1,0:T(8,128)(2,1)S(1)} %get-tuple-element.105), channel_id=1, source_target_pairs={{0,1},{1,2},{2,3},{3,4},{4,5},{5,6},{6,7},{7,0},{8,9},{9,10},{10,1... | collective-permute-start | bytes 196616 | tf_op jit(solution)/shard_map/ppermute | solution.py:469
  159.5 42.1 %all-to-all-start = ((bf16[64,24,512]{2,1,0:T(8,128)(2,1)}), bf16[64,24,512]{2,1,0:T(8,128)(2,1)S(1)}, u32[]{:S(2)}, u32[]{:S(2)}) async-start(bf16[64,24,512]{2,1,0:T(8,128)(2,1)} %bitcast.62), calls=%async_computation | async-start | bytes 3145728 | tf_op jit(solution)/shard_map/all_to_all | solution.py:484
  188.1 13.8 %collective-permute-start.15 = (bf16[256,512]{1,0:T(8,128)(2,1)}, bf16[256,512]{1,0:T(8,128)(2,1)}, u32[]{:S(2)}, u32[]{:S(2)}) collective-permute-start(bf16[256,512]{1,0:T(8,128)(2,1)} %bitcast.15), channel_id=1, source_target_pairs={{0,8},{8,16},{16,24},{24,32},{32,40},{40,48},{48,56},{56,64},{64,7... | collective-permute-start | bytes 786440 | tf_op jit(solution)/shard_map/ppermute | solution.py:474
  191.7 10.7 %collective-permute-start.16 = (bf16[256,512]{1,0:T(8,128)(2,1)S(1)}, bf16[256,512]{1,0:T(8,128)(2,1)}, u32[]{:S(2)}, u32[]{:S(2)}) collective-permute-start(bf16[256,512]{1,0:T(8,128)(2,1)S(1)} %bitcast.66), channel_id=1, source_target_pairs={{8,0},{16,8},{24,16},{32,24},{40,32},{48,40},{56,48},{64,56},{72,6... | collective-permute-start | bytes 786440 | tf_op jit(solution)/shard_map/ppermute | solution.py:474
  202.6 35.0 %copy-start.15 = (f32[16,64,512]{2,1,0:T(8,128)S(1)}, f32[16,64,512]{2,1,0:T(8,128)}, u32[]{:S(2)}) copy-start(f32[16,64,512]{2,1,0:T(8,128)} %fusion.16) | copy-start | bytes 6291460
  234.1 6.5 %collective-permute-start.17 = (bf16[1536,512]{1,0:T(8,128)(2,1)S(1)}, bf16[1536,512]{1,0:T(8,128)(2,1)S(1)}, u32[]{:S(2)}, u32[]{:S(2)}) collective-permute-start(bf16[1536,512]{1,0:T(8,128)(2,1)S(1)} %bitcast.61), channel_id=1, source_target_pairs={{0,1},{1,0},{2,3},{3,2},{4,5},{5,4},{6,7},{7,6},{8,9},{9,8},{10,11... | collective-permute-start | bytes 4718600 | tf_op jit(solution)/shard_map/ppermute | solution.py:478
  (7 other events, 21.1 us)

commit v3 on v1

--- a/solution.py
+++ b/solution.py
@@ -53,7 +53,7 @@
                 stages[d](i - d)
 
 
-def kernel_params(mib):
+def kernel_params(mib=56):
     return pltpu.CompilerParams(vmem_limit_bytes=mib * MIB)
 
 
@@ -166,7 +166,7 @@
             pltpu.VMEM((edges, band_rows), BF),
             pltpu.VMEM((nodes, width), F32),
         ],
-        compiler_params=kernel_params(26),
+        compiler_params=kernel_params(56),
     )(idx, counts, mesh_rows, *pieces, enc_send, enc_recv, enc_out, dec_send)
 
 
@@ -187,7 +187,7 @@
         out_specs=per_edge,
         out_shape=jax.ShapeDtypeStruct(normed.shape, BF),
         input_output_aliases={2: 0} if kept else {},
-        compiler_params=kernel_params(12),
+        compiler_params=kernel_params(56),
         cost_estimate=pl.CostEstimate(flops=2 * share * width, bytes_accessed=4 * share, transcendentals=0),
     )(normed, enc_out, *kept)
 
@@ -359,25 +359,22 @@
         turned_level[...] = dot_nt(level.astype(BF), out_ref[...])
         out_acc[...] = jnp.zeros_like(out_acc)
 
-    def scatter(slot, n):
-        half = width // 2
-        at = slice(n * half, (n + 1) * half)
-        totals[:, at] += dot(onehots[slot][...], cots[slot][:, at])
+    def scatter(slot):
+        totals[...] += dot(onehots[slot][...], cots[slot][...])
 
     def edge_part(slot, beside):
         strips = tile // STRIP
         total = [jnp.zeros((STRIP, width), F32)] * strips
         scales = scale_ref[...]
         for n in range(2):
-            if beside is not None:
-                scatter(beside, n)
+            if beside is not None and n == 0:
+                scatter(beside)
             for k in range(n * degree // 2, (n + 1) * degree // 2):
                 for i in range(strips):
                     at = slice(k * tile + i * STRIP, k * tile + (i + 1) * STRIP)
                     mine = pl.ds(pl.multiple_of(step * tile + i * STRIP, STRIP), STRIP)
-                    spread = scaling * node_cot[mine, :]
                     normed = normed_ref[at, :].astype(F32)
-                    along = jnp.mean(spread * normed, axis=-1, keepdims=True)
+                    along = scaling * jnp.mean(node_cot[mine, :] * normed, axis=-1, keepdims=True)
                     scale = scales[i * STRIP : (i + 1) * STRIP, k : k + 1]
                     message_cot[at, :] = (scale * (levels[mine, :] - along * normed)).astype(BF)
                     turned = scale * (turned_level[mine, :] - along * turned_ref[at, :].astype(F32))
@@ -402,8 +399,7 @@
 
     @pl.when(step == tiles)
     def _():
-        scatter(1, 0)
-        scatter(1, 1)
+        scatter(1)
         grads_ref[width : 2 * width, :] = dot_tn(mesh_ref[...], received_cot[...]).astype(BF)
         grads_ref[2 * width :, :] = out_acc[...].astype(BF)
         mesh_grad_ref[...] = (node_cot[...] + dot_nt(received_cot[...], recv_ref[...])).astype(BF)
@@ -460,7 +456,7 @@
             pltpu.VMEM((nodes, width), F32),
             pltpu.VMEM((nodes, width), BF),
         ],
-        compiler_params=kernel_params(40),
+        compiler_params=kernel_params(56),
     )(idx_rows, scale, mesh_rows, moved_cot, normed, turned, slope, hidden, *pieces, dec_send, enc_recv, enc_out)
 
 
@@ -557,10 +553,12 @@
         dec_idx_rows, grid_rows, cot_rows, dec_hidden, dec_message_cot, dec_before_cot, dec_received_cot,
         dec_recv, 3 * slots,
     )
-    column = centre_tot.astype(F32) + from_east.astype(F32) + from_west.astype(F32)
-    from_below = to_lat(column[slots : 2 * slots].astype(BF), 1)
-    from_above = to_lat(column[2 * slots :].astype(BF), -1)
-    moved_cot = column[:slots] + from_below.astype(F32) + from_above.astype(F32)
+    def met(at):
+        return centre_tot[at].astype(F32) + from_east[at].astype(F32) + from_west[at].astype(F32)
+
+    from_below = to_lat(met(slice(slots, 2 * slots)).astype(BF), 1)
+    from_above = to_lat(met(slice(2 * slots, 3 * slots)).astype(BF), -1)
+    moved_cot = met(slice(0, slots)) + from_below.astype(F32) + from_above.astype(F32)
     moved_cot = moved_cot.astype(BF)
     dec_send_grad = dot_tn(mesh_new, moved_cot).astype(BF)
 
@@ -578,14 +576,20 @@
     swapped = core_swap(jnp.where(leads, dec_stack, enc_stack))
     kept = jnp.where(leads, enc_stack, dec_stack).astype(F32) + swapped.astype(F32)
     kept = kept.astype(BF).reshape(chips, 3 * width // chips, width)
-    kept, from_right, from_left = lax.optimization_barrier((kept, from_right, from_left))
-
-    inner_cot = band_cot[:inner_rows].astype(F32).reshape(tall, lon_cells, width)
-    inner_cot = inner_cot.at[:, lon_cells - REACH :].add(from_right.astype(F32).reshape(tall, REACH, width))
-    inner_cot = inner_cot.at[:, :REACH].add(from_left.astype(F32).reshape(tall, REACH, width))
-    inner_cot = inner_cot.reshape(inner_rows, width)
-    from_low = to_lat(inner_cot[cells : cells + edge_rows].astype(BF), 1)
-    from_high = to_lat(inner_cot[cells + edge_rows :].astype(BF), -1)
+
+    def met_cells(first, count):
+        rows = band_cot[first * lon_cells : (first + count) * lon_cells].astype(F32).reshape(count, lon_cells, width)
+        at = slice(first * REACH, (first + count) * REACH)
+        gap = jnp.zeros((count, lon_cells - 2 * REACH, width), F32)
+        east = from_right[at].astype(F32).reshape(count, REACH, width)
+        west = from_left[at].astype(F32).reshape(count, REACH, width)
+        return (rows + jnp.concatenate([west, gap, east], axis=1)).reshape(count * lon_cells, width)
+
+    to_upper = met_cells(lat_cells, REACH).astype(BF)
+    to_lower = met_cells(lat_cells + REACH, REACH).astype(BF)
+    kept, to_upper, to_lower = lax.optimization_barrier((kept, to_upper, to_lower))
+    from_low = to_lat(to_upper, 1)
+    from_high = to_lat(to_lower, -1)
 
     mine = jnp.sum(across_chips(kept).astype(F32), axis=0).astype(BF)
     mine, from_low, from_high = lax.optimization_barrier((mine, from_low, from_high))
@@ -594,7 +598,7 @@
     enc_grads = jnp.where(leads, ours, theirs).astype(F32)
     dec_grads = jnp.where(leads, theirs, ours).astype(F32)
 
-    sent_cot = inner_cot[:cells] + jnp.concatenate([from_low, from_high], axis=0).astype(F32)
+    sent_cot = met_cells(0, lat_cells) + jnp.concatenate([from_low, from_high], axis=0).astype(F32)
     grid_grad = (grid_part + dot_nt(sent_cot.astype(BF), enc_send)).astype(BF)
 
     return (

time: 247 us -> 244 us (0.988)
  local copies, waits for them, and re-layouts: 37.2 us -> 9.86 us
  waiting for transfers between devices: 30.5 us -> 45.5 us
  Pallas kernels: 76.6 us -> 83.8 us
  other arithmetic: 11.9 us -> 15.8 us
  starting transfers between devices: 55.6 us -> 53 us
    unnamed x65 -> x43, local copies, waits for them, and re-layouts: 25.1 us -> 2.89 us
    ppermute x8, waiting for transfers between devices: 7.45 us -> 17.2 us  [to_lon(): lax.ppermute(shard, 'lon', [(i, (i + by) % count) for i in range(count)])]
    pallas_call x2, Pallas kernels: 5.98 us -> 12.8 us  [enc_between(): pl.pallas_call(enc_between_kernel, name='enc_between', grid=(count,), in_...]
    ppermute x8, waiting for transfers between devices: 4.15 us -> 8.38 us  [to_lat(): lax.ppermute(shard, 'lat', [(i, i + by) for i in range(count) if 0 <= i +...]
    ppermute x2, starting transfers between devices: 8.93 us -> 5.45 us  [core_swap(): lax.ppermute(array, 'lon', [(i, i ^ 1) for i in range(lax.axis_size('lon'...]
    all_to_all x1, starting transfers between devices: 15.8 us -> 18.9 us  [across_chips(): lax.all_to_all(parts, ('lat', 'lon'), 0, 0, axis_index_groups=alike, tile...]
    convert_element_type x0 -> x2, other arithmetic: none -> 2.99 us  [the longest x1 2 us: on_device(): to_lower = met_cells(lat_cells + REACH, REACH).astype(BF)]
    select_n x1, other arithmetic: 0.44 us -> 3 us  [on_device(): swapped = core_swap(jnp.where(leads, dec_stack, enc_stack))]
  transfers between devices with their start and end apart: 19 -> 19, of which waited for: 8 -> 12; matrix products, arithmetic and copies ran while one was open for 7% -> 4% of each run, Pallas kernels for 4% -> 6%
where the time goes in v3:
time: 244 us; the launch traced here: 243 us
  Pallas kernels  83.8 us (34%)
  starting transfers between devices  53 us (22%)
  waiting for transfers between devices  45.5 us (19%)
  blocking collectives  32.2 us (13%)
  other arithmetic  15.8 us (6%)
  local copies, waits for them, and re-layouts  9.86 us (4%)
    all_to_all x1, blocking collectives, across_chips(): lax.all_to_all(parts, ('lat', 'lon'), 0, 0, axis_index_groups=alike, tile...  32.2 us
    pallas_call x1, Pallas kernels, enc_backward(): pl.pallas_call(enc_backward_kernel, name='enc_backward', grid=(tiles + 1,...  30.8 us
    pallas_call x1, Pallas kernels, enc_forward(): pl.pallas_call(enc_forward_kernel, name='enc_forward', grid=(nodes // til...  28 us
    ppermute x8, starting transfers between devices, to_lat(): lax.ppermute(shard, 'lat', [(i, i + by) for i in range(count) if 0 <= i +...  22.3 us
    all_to_all x1, waiting for transfers between devices, across_chips(): lax.all_to_all(parts, ('lat', 'lon'), 0, 0, axis_index_groups=alike, tile...  19.7 us
    all_to_all x1, starting transfers between devices, across_chips(): lax.all_to_all(parts, ('lat', 'lon'), 0, 0, axis_index_groups=alike, tile...  18.9 us
    ppermute x8, waiting for transfers between devices, to_lon(): lax.ppermute(shard, 'lon', [(i, (i + by) % count) for i in range(count)])  17.2 us
    pallas_call x2, Pallas kernels, enc_between(): pl.pallas_call(enc_between_kernel, name='enc_between', grid=(count,), in_...  12.8 us
  transfers between devices with their start and end apart: 19, of which 12 were waited for; matrix products, arithmetic and copies ran while one was open for 4% of the time, Pallas kernels for 6%

profile of v3, /device:TPU:1, one launch (start us, length us, event | category | flops | bytes accessed | tf_op | source)
XLA Modules:
  0.0 242.9 jit_solution(7325091972550426389)
XLA Ops:
  1.8 1.3 collective-permute-start
  3.1 4.6 %collective-permute-start.1 = (bf16[256,512]{1,0:T(8,128)(2,1)S(1)}, bf16[256,512]{1,0:T(8,128)(2,1)S(1)}, u32[]{:S(2)}, u32[]{:S(2)}) collective-permute-start(bf16[256,512]{1,0:T(8,128)(2,1)S(1)} %bitcast.71), channel_id=1, source_target_pairs={{0,8},{8,16},{16,24},{24,32},{32,40},{40,48},{48,56},{56,64},{64,7... | collective-permute-start | bytes 786440 | tf_op jit(solution)/shard_map/ppermute | solution.py:470
  8.6 2.7 %collective-permute-done.high_ref = bf16[256,512]{1,0:T(8,128)(2,1)S(1)} collective-permute-done((bf16[256,512]{1,0:T(8,128)(2,1)S(1)}, bf16[256,512]{1,0:T(8,128)(2,1)S(1)}, u32[]{:S(2)}, u32[]{:S(2)}) %collective-permute-start) | collective-permute-done | bytes 262176 | tf_op jit(solution)/shard_map/ppermute | solution.py:470
  12.3 3.5 %collective-permute-start.2 = (bf16[64,512]{1,0:T(8,128)(2,1)S(1)}, bf16[64,512]{1,0:T(8,128)(2,1)S(1)}, u32[]{:S(2)}, u32[]{:S(2)}) collective-permute-start(bf16[64,512]{1,0:T(8,128)(2,1)S(1)} %reshape.119), channel_id=1, source_target_pairs={{0,1},{1,2},{2,3},{3,4},{4,5},{5,6},{6,7},{7,0},{8,9},{9,10},{10,1... | collective-permute-start | bytes 196616 | tf_op jit(solution)/shard_map/ppermute | solution.py:465
  17.6 1.9 collective-permute-done.3.right_ref
  20.1 28.0 %enc_forward.1 = (bf16[256,512]{1,0:T(8,128)(2,1)}, bf16[256,512]{1,0:T(8,128)(2,1)}, bf16[8192,512]{1,0:T(8,128)(2,1)}, bf16[8192,512]{1,0:T(8,128)(2,1)}, bf16...) custom-call(s32[256,32]{1,0:T(8,128)} %select_select_fusion.idx_ref, s32[256,1]{1,0:T(8,128)} %copy.29.count_ref, ...), custom_call_target="tpu_custom_call" | custom-call | tf_op jit(solution)/shard_map/enc_forward/pallas_call | solution.py:145
  49.4 4.9 %collective-permute-start.5 = (bf16[256,512]{1,0:T(8,128)(2,1)}, bf16[256,512]{1,0:T(8,128)(2,1)S(1)}, u32[]{:S(2)}, u32[]{:S(2)}) collective-permute-start(bf16[256,512]{1,0:T(8,128)(2,1)} %get-tuple-element.40), channel_id=1, source_target_pairs={{0,8},{8,16},{16,24},{24,32},{32,40},{40,48},{48,56},{56,64},{64,7... | collective-permute-start | bytes 786440 | tf_op jit(solution)/shard_map/ppermute | solution.py:470
  54.4 6.4 %enc_between.2.refs_0_ = bf16[8192,512]{1,0:T(8,128)(2,1)} custom-call(bf16[8192,512]{1,0:T(8,128)(2,1)} %get-tuple-element.41.normed_ref, bf16[512,512]{1,0:T(8,128)(2,1)} %out_ref.9), custom_call_target="tpu_custom_call" | custom-call | flops 2147483648 | bytes 8388608 | tf_op jit(solution)/shard_map/enc_between/pallas_call | solution.py:182
  61.9 6.4 %enc_between.3.turned_ref = bf16[8192,512]{1,0:T(8,128)(2,1)} custom-call(bf16[8192,512]{1,0:T(8,128)(2,1)} %get-tuple-element.41.normed_ref, bf16[512,512]{1,0:T(8,128)(2,1)} %out_ref.9, bf16[8192,512]{1,0:T(8,128)(2,1)} %enc_between.2.refs_0_), custom_call_target="tpu_custom_call", output_to_operand_aliasing={{}: (2, {})} | custom-call | flops 2147483648 | bytes 8388608 | tf_op jit(solution)/shard_map/enc_between/pallas_call | solution.py:182
  68.3 1.7 collective-permute-done.6.left_ref
  70.0 2.8 %collective-permute-done.7.right_ref = bf16[768,512]{1,0:T(8,128)(2,1)S(1)} collective-permute-done((bf16[768,512]{1,0:T(8,128)(2,1)S(1)}, bf16[768,512]{1,0:T(8,128)(2,1)S(1)}, u32[]{:S(2)}, u32[]{:S(2)}) %collective-permute-start.7) | collective-permute-done | bytes 786464 | tf_op jit(solution)/shard_map/ppermute | solution.py:465
  72.8 9.5 %decoder.1 = (bf16[512,512]{1,0:T(8,128)(2,1)}, bf16[1536,512]{1,0:T(8,128)(2,1)S(1)}, bf16[1536,512]{1,0:T(8,128)(2,1)S(1)}, bf16[1536,512]{1,0:T(8,128)(2,1)S(...) custom-call(s32[512,3]{1,0:T(8,128)S(1)} %copy.30.idx_ref, ...), custom_call_target="tpu_custom_call" | custom-call | tf_op jit(solution)/shard_map/decoder/pallas_call | solution.py:277
  84.1 2.7 %decoder_rest.1 = (f32[512,512]{1,0:T(8,128)S(1)}, bf16[512,512]{1,0:T(8,128)(2,1)S(1)}, bf16[512,512]{1,0:T(8,128)(2,1)S(1)}, bf16[768,512]{1,0:T(8,128)(2,1)S(1)}) custom-call(s32[3,512]{1,0:T(4,128)S(1)} %fusion.29.idx_row_ref, bf16[512,512]{1,0:T(8,128)(2,1)S(1)} %bitcast.62, bf16[512,512]{1,0:T(8,128)(2,1)S(1)} %bitcast.64, ...), custom_call_target="tpu_custom_call" | custom-call | flops 2818572288 | bytes 6291456 | tf_op jit(solution)/shard_map/decoder_rest/pallas_call | solution.py:315
  86.9 7.2 %collective-permute-done.8 = bf16[768,512]{1,0:T(8,128)(2,1)S(1)} collective-permute-done((bf16[768,512]{1,0:T(8,128)(2,1)S(1)}, bf16[768,512]{1,0:T(8,128)(2,1)S(1)}, u32[]{:S(2)}, u32[]{:S(2)}) %collective-permute-start.8) | collective-permute-done | bytes 786464 | tf_op jit(solution)/shard_map/ppermute | solution.py:465
  96.0 4.5 %collective-permute-start.10 = (bf16[256,512]{1,0:T(8,128)(2,1)}, bf16[256,512]{1,0:T(8,128)(2,1)}, u32[]{:S(2)}, u32[]{:S(2)}) collective-permute-start(bf16[256,512]{1,0:T(8,128)(2,1)} %get-tuple-element.79), channel_id=1, source_target_pairs={{0,8},{8,16},{16,24},{24,32},{32,40},{40,48},{48,56},{56,64},{64,7... | collective-permute-start | bytes 786440 | tf_op jit(solution)/shard_map/ppermute | solution.py:470
  100.5 1.5 collective-permute-start.11
  103.4 4.5 %collective-permute-done.11 = bf16[256,512]{1,0:T(8,128)(2,1)} collective-permute-done((bf16[256,512]{1,0:T(8,128)(2,1)}, bf16[256,512]{1,0:T(8,128)(2,1)}, u32[]{:S(2)}, u32[]{:S(2)}) %collective-permute-start.11) | collective-permute-done | bytes 262176 | tf_op jit(solution)/shard_map/ppermute | solution.py:470
  107.9 1.4 add_convert_fusion.1.moved_cot_ref
  110.0 30.8 %enc_backward.1 = (bf16[256,512]{1,0:T(8,128)(2,1)}, bf16[1152,512]{1,0:T(8,128)(2,1)}, bf16[1536,512]{1,0:T(8,128)(2,1)}) custom-call(s32[8,1,1024]{2,1,0:T(1,128)} %reshape.123.idx_row_ref, f32[256,32]{1,0:T(8,128)} %get-tuple-element.52.scale_ref, bf16[256,512]{1,0:T(8,128)(2,1)} %bitcast.69, bf16[256,512]{1,0:T(8,128)(2,1)} %copy-done.6, ...), custom_call_target="tpu_custom_call" | custom-call | tf_op jit(solution)/shard_map/enc_backward/pallas_call | solution.py:428
  140.8 3.0 %broadcast_select_fusion = bf16[1536,512]{1,0:T(8,128)(2,1)} fusion(bf16[1536,512]{1,0:T(8,128)(2,1)} %get-tuple-element.60, pred[]{:T(512)S(6)} %eq.19, bf16[512,512]{1,0:T(8,128)(2,1)S(1)} %get-tuple-element.63, bf16[512,512]{1,0:T(8,128)(2,1)S(1)} %get-tuple-element.62, bf16[512,512]{1,0:T(8,128)(2,1)S(1)} %convolution_convert_fusion), kind=kLoop, calls=%fused_computation.4 | loop fusion | flops 5505024 | bytes 4718593 | tf_op jit(solution)/shard_map/jit(_where)/select_n | solution.py:576
  143.8 4.2 %collective-permute-start.14 = (bf16[1536,512]{1,0:T(8,128)(2,1)}, bf16[1536,512]{1,0:T(8,128)(2,1)}, u32[]{:S(2)}, u32[]{:S(2)}) collective-permute-start(bf16[1536,512]{1,0:T(8,128)(2,1)} %broadcast_select_fusion), channel_id=1, source_target_pairs={{0,1},{1,0},{2,3},{3,2},{4,5},{5,4},{6,7},{7,6},{8,9},{9,8},{10,11... | collective-permute-start | bytes 4718600 | tf_op jit(solution)/shard_map/ppermute | solution.py:474
  149.5 1.5 collective-permute-done.12
  151.0 2.0 collective-permute-done.13
  153.3 2.0 fusion.3
  155.3 3.2 %add_convert_fusion = bf16[1536,512]{1,0:T(8,128)(2,1)} fusion(bf16[1536,512]{1,0:T(8,128)(2,1)} %collective-permute-done.14, bf16[1536,512]{1,0:T(8,128)(2,1)S(1)} %copy-done.5, pred[]{:T(512)S(6)} %eq.19, bf16[512,512]{1,0:T(8,128)(2,1)S(1)} %get-tuple-element.63, bf16[512,512]{1,0:T(8,128)(2,1)S(1)} %get-tuple-element.62, ...), kind=kLoop, calls=%fused_computation | loop fusion | flops 8650752 | bytes 6291457 | tf_op jit(solution)/shard_map/convert_element_type | solution.py:578
  158.6 18.9 %all-to-all-start = ((bf16[64,24,512]{2,1,0:T(8,128)(2,1)}), bf16[64,24,512]{2,1,0:T(8,128)(2,1)S(1)}, u32[]{:S(2)}, u32[]{:S(2)}) async-start(bf16[64,24,512]{2,1,0:T(8,128)(2,1)} %bitcast.66), calls=%async_computation | async-start | bytes 3145728 | tf_op jit(solution)/shard_map/all_to_all | solution.py:480
  177.5 2.9 %collective-permute-start.15 = (bf16[256,512]{1,0:T(8,128)(2,1)}, bf16[256,512]{1,0:T(8,128)(2,1)S(1)}, u32[]{:S(2)}, u32[]{:S(2)}) collective-permute-start(bf16[256,512]{1,0:T(8,128)(2,1)} %get-tuple-element.65), channel_id=1, source_target_pairs={{0,8},{8,16},{16,24},{24,32},{32,40},{40,48},{48,56},{56,64},{64,7... | collective-permute-start | bytes 786440 | tf_op jit(solution)/shard_map/ppermute | solution.py:470
  181.7 19.7 %all-to-all-done = bf16[64,24,512]{2,1,0:T(8,128)(2,1)S(1)} async-done(((bf16[64,24,512]{2,1,0:T(8,128)(2,1)}), bf16[64,24,512]{2,1,0:T(8,128)(2,1)S(1)}, u32[]{:S(2)}, u32[]{:S(2)}) %all-to-all-start) | async-done | bytes 1572896 | tf_op jit(solution)/shard_map/all_to_all | solution.py:480
  201.8 32.2 %all_to_all.10 = bf16[64,24,512]{2,1,0:T(8,128)(2,1)S(1)} all-to-all(bf16[64,24,512]{2,1,0:T(8,128)(2,1)S(1)} %broadcast_in_dim.16), channel_id=1, replica_groups={{0,2,4,6,8,10,12,14,16,18,20,22,24,26,28,30,32,34,36,38,40,42,44,46,48,..., dimensions={0} | all-to-all | bytes 3145728 | tf_op jit(solution)/shard_map/all_to_all | solution.py:480
  235.5 1.3 fusion.2
  238.4 1.8 select_convert_fusion
  240.2 2.7 %fusion.33 = (f32[512,512]{1,0:T(8,128)}, f32[512,512]{1,0:T(8,128)}, f32[512,512]{1,0:T(8,128)}, f32[512,512]{1,0:T(8,128)}, f32[512,512]{1,0:T(8,128)}, /*index=5*/f32[512,512]{1,0:T(8,128)}) fusion(f32[1536,512]{1,0:T(8,128)S(1)} %get-tuple-element.74, f32[1536,512]{1,0:T(8,128)S(1)} %get-tuple-element.75), kind=kLoop, calls=%fused_computation.100 | loop fusion | bytes 12582912 | tf_op jit(solution)/shard_map/slice | solution.py:613
  (99 shorter events, 19.9 us)
Async XLA Ops:
  0.6 11.5 %copy-start = (bf16[8,64,512]{2,1,0:T(8,128)(2,1)S(1)}, bf16[8,64,512]{2,1,0:T(8,128)(2,1)}, u32[]{:S(2)}) copy-start(bf16[8,64,512]{2,1,0:T(8,128)(2,1)} %param.12) | copy-start | bytes 1572868
  1.8 15.0 %copy-start.19 = (s32[1,1,256,32]{2,3,1,0:T(8,128)S(1)}, s32[1,1,256,32]{2,3,1,0:T(8,128)}, u32[]{:S(2)}) copy-start(s32[1,1,256,32]{2,3,1,0:T(8,128)} %param.22) | copy-start | bytes 98308
  1.8 9.5 %collective-permute-start = (bf16[256,512]{1,0:T(8,128)(2,1)S(1)}, bf16[256,512]{1,0:T(8,128)(2,1)S(1)}, u32[]{:S(2)}, u32[]{:S(2)}) collective-permute-start(bf16[256,512]{1,0:T(8,128)(2,1)S(1)} %bitcast.72), channel_id=1, source_target_pairs={{8,0},{16,8},{24,16},{32,24},{40,32},{48,40},{56,48},{64,56},{72,6... | collective-permute-start | bytes 786440 | tf_op jit(solution)/shard_map/ppermute | solution.py:470
  3.1 9.0 %collective-permute-start.1 = (bf16[256,512]{1,0:T(8,128)(2,1)S(1)}, bf16[256,512]{1,0:T(8,128)(2,1)S(1)}, u32[]{:S(2)}, u32[]{:S(2)}) collective-permute-start(bf16[256,512]{1,0:T(8,128)(2,1)S(1)} %bitcast.71), channel_id=1, source_target_pairs={{0,8},{8,16},{16,24},{24,32},{32,40},{40,48},{48,56},{56,64},{64,7... | collective-permute-start | bytes 786440 | tf_op jit(solution)/shard_map/ppermute | solution.py:470
  11.3 8.2 %copy-start.7 = (bf16[256,512]{1,0:T(8,128)(2,1)}, bf16[256,512]{1,0:T(8,128)(2,1)S(1)}, u32[]{:S(2)}) copy-start(bf16[256,512]{1,0:T(8,128)(2,1)S(1)} %collective-permute-done.high_ref) | copy-start | bytes 786436
  12.1 7.4 %copy-start.8 = (bf16[256,512]{1,0:T(8,128)(2,1)}, bf16[256,512]{1,0:T(8,128)(2,1)S(1)}, u32[]{:S(2)}) copy-start(bf16[256,512]{1,0:T(8,128)(2,1)S(1)} %collective-permute-done.1.low_ref) | copy-start | bytes 786436
  12.3 5.3 %collective-permute-start.2 = (bf16[64,512]{1,0:T(8,128)(2,1)S(1)}, bf16[64,512]{1,0:T(8,128)(2,1)S(1)}, u32[]{:S(2)}, u32[]{:S(2)}) collective-permute-start(bf16[64,512]{1,0:T(8,128)(2,1)S(1)} %reshape.119), channel_id=1, source_target_pairs={{0,1},{1,2},{2,3},{3,4},{4,5},{5,6},{6,7},{7,0},{8,9},{9,10},{10,1... | collective-permute-start | bytes 196616 | tf_op jit(solution)/shard_map/ppermute | solution.py:465
  15.8 3.7 %collective-permute-start.3 = (bf16[64,512]{1,0:T(8,128)(2,1)S(1)}, bf16[64,512]{1,0:T(8,128)(2,1)S(1)}, u32[]{:S(2)}, u32[]{:S(2)}) collective-permute-start(bf16[64,512]{1,0:T(8,128)(2,1)S(1)} %reshape.120), channel_id=1, source_target_pairs={{0,7},{1,0},{2,1},{3,2},{4,3},{5,4},{6,5},{7,6},{8,15},{9,8},{10,9... | collective-permute-start | bytes 196616 | tf_op jit(solution)/shard_map/ppermute | solution.py:465
  48.1 12.6 %collective-permute-start.4 = (bf16[256,512]{1,0:T(8,128)(2,1)}, bf16[256,512]{1,0:T(8,128)(2,1)S(1)}, u32[]{:S(2)}, u32[]{:S(2)}) collective-permute-start(bf16[256,512]{1,0:T(8,128)(2,1)} %get-tuple-element.40), channel_id=1, source_target_pairs={{8,0},{16,8},{24,16},{32,24},{40,32},{48,40},{56,48},{64,56},{72,6... | collective-permute-start | bytes 786440 | tf_op jit(solution)/shard_map/ppermute | solution.py:470
  49.4 11.3 %collective-permute-start.5 = (bf16[256,512]{1,0:T(8,128)(2,1)}, bf16[256,512]{1,0:T(8,128)(2,1)S(1)}, u32[]{:S(2)}, u32[]{:S(2)}) collective-permute-start(bf16[256,512]{1,0:T(8,128)(2,1)} %get-tuple-element.40), channel_id=1, source_target_pairs={{0,8},{8,16},{16,24},{24,32},{32,40},{40,48},{48,56},{56,64},{64,7... | collective-permute-start | bytes 786440 | tf_op jit(solution)/shard_map/ppermute | solution.py:470
  54.4 6.4 %copy-start.15 = (bf16[256,512]{1,0:T(8,128)(2,1)S(1)}, bf16[256,512]{1,0:T(8,128)(2,1)}, u32[]{:S(2)}) copy-start(bf16[256,512]{1,0:T(8,128)(2,1)} %get-tuple-element.40) | copy-start | bytes 786436
  60.8 9.2 %collective-permute-start.6 = (bf16[768,512]{1,0:T(8,128)(2,1)S(1)}, bf16[768,512]{1,0:T(8,128)(2,1)S(1)}, u32[]{:S(2)}, u32[]{:S(2)}) collective-permute-start(bf16[768,512]{1,0:T(8,128)(2,1)S(1)} %pad_maximum_fusion.3.centre_ref), channel_id=1, source_target_pairs={{0,1},{1,2},{2,3},{3,4},{4,5},{5,6},{6,7},{7,0},{8,9},{9,10},{10,1... | collective-permute-start | bytes 2359304 | tf_op jit(solution)/shard_map/ppermute | solution.py:465
  61.1 11.7 %collective-permute-start.7 = (bf16[768,512]{1,0:T(8,128)(2,1)S(1)}, bf16[768,512]{1,0:T(8,128)(2,1)S(1)}, u32[]{:S(2)}, u32[]{:S(2)}) collective-permute-start(bf16[768,512]{1,0:T(8,128)(2,1)S(1)} %pad_maximum_fusion.3.centre_ref), channel_id=1, source_target_pairs={{0,7},{1,0},{2,1},{3,2},{4,3},{5,4},{6,5},{7,6},{8,15},{9,8},{10,9... | collective-permute-start | bytes 2359304 | tf_op jit(solution)/shard_map/ppermute | solution.py:465
  61.8 11.0 %copy-start.1 = (bf16[8,64,512]{2,1,0:T(8,128)(2,1)S(1)}, bf16[8,64,512]{2,1,0:T(8,128)(2,1)}, u32[]{:S(2)}) copy-start(bf16[8,64,512]{2,1,0:T(8,128)(2,1)} %param.12) | copy-start | bytes 1572868
  61.8 11.0 %copy-start.2 = (bf16[512,512]{1,0:T(8,128)(2,1)S(1)}, bf16[512,512]{1,0:T(8,128)(2,1)}, u32[]{:S(2)}) copy-start(bf16[512,512]{1,0:T(8,128)(2,1)} %out_ref.8) | copy-start | bytes 1572868
  61.8 11.0 %copy-start.3 = (bf16[8,64,512]{2,1,0:T(8,128)(2,1)S(1)}, bf16[8,64,512]{2,1,0:T(8,128)(2,1)}, u32[]{:S(2)}) copy-start(bf16[8,64,512]{2,1,0:T(8,128)(2,1)} %param.14) | copy-start | bytes 1572868
  61.8 11.0 %copy-start.4 = (bf16[512,512]{1,0:T(8,128)(2,1)S(1)}, bf16[512,512]{1,0:T(8,128)(2,1)}, u32[]{:S(2)}) copy-start(bf16[512,512]{1,0:T(8,128)(2,1)} %recv_ref.6) | copy-start | bytes 1572868
  82.4 11.7 %collective-permute-start.8 = (bf16[768,512]{1,0:T(8,128)(2,1)S(1)}, bf16[768,512]{1,0:T(8,128)(2,1)S(1)}, u32[]{:S(2)}, u32[]{:S(2)}) collective-permute-start(bf16[768,512]{1,0:T(8,128)(2,1)S(1)} %get-tuple-element.54), channel_id=1, source_target_pairs={{0,7},{1,0},{2,1},{3,2},{4,3},{5,4},{6,5},{7,6},{8,15},{9,8},{10,9... | collective-permute-start | bytes 2359304 | tf_op jit(solution)/shard_map/ppermute | solution.py:465
  83.3 10.8 %collective-permute-start.9 = (bf16[768,512]{1,0:T(8,128)(2,1)S(1)}, bf16[768,512]{1,0:T(8,128)(2,1)S(1)}, u32[]{:S(2)}, u32[]{:S(2)}) collective-permute-start(bf16[768,512]{1,0:T(8,128)(2,1)S(1)} %get-tuple-element.55), channel_id=1, source_target_pairs={{0,1},{1,2},{2,3},{3,4},{4,5},{5,6},{6,7},{7,0},{8,9},{9,10},{10,1... | collective-permute-start | bytes 2359304 | tf_op jit(solution)/shard_map/ppermute | solution.py:465
  86.9 15.1 %copy-start.16 = (s32[1,1,256,32]{2,3,1,0:T(8,128)S(1)}, s32[1,1,256,32]{2,3,1,0:T(8,128)}, u32[]{:S(2)}) copy-start(s32[1,1,256,32]{2,3,1,0:T(8,128)} %param.21) | copy-start | bytes 98308
  96.0 13.3 %copy-start.14 = (bf16[256,512]{1,0:T(8,128)(2,1)S(1)}, bf16[256,512]{1,0:T(8,128)(2,1)}, u32[]{:S(2)}) copy-start(bf16[256,512]{1,0:T(8,128)(2,1)} %get-tuple-element.61) | copy-start | bytes 786436
  96.0 7.4 %collective-permute-start.10 = (bf16[256,512]{1,0:T(8,128)(2,1)}, bf16[256,512]{1,0:T(8,128)(2,1)}, u32[]{:S(2)}, u32[]{:S(2)}) collective-permute-start(bf16[256,512]{1,0:T(8,128)(2,1)} %get-tuple-element.79), channel_id=1, source_target_pairs={{0,8},{8,16},{16,24},{24,32},{32,40},{40,48},{48,56},{56,64},{64,7... | collective-permute-start | bytes 786440 | tf_op jit(solution)/shard_map/ppermute | solution.py:470
  100.5 7.4 %collective-permute-start.11 = (bf16[256,512]{1,0:T(8,128)(2,1)}, bf16[256,512]{1,0:T(8,128)(2,1)}, u32[]{:S(2)}, u32[]{:S(2)}) collective-permute-start(bf16[256,512]{1,0:T(8,128)(2,1)} %get-tuple-element.80), channel_id=1, source_target_pairs={{8,0},{16,8},{24,16},{32,24},{40,32},{48,40},{56,48},{64,56},{72,6... | collective-permute-start | bytes 786440 | tf_op jit(solution)/shard_map/ppermute | solution.py:470
  143.8 11.6 %collective-permute-start.14 = (bf16[1536,512]{1,0:T(8,128)(2,1)}, bf16[1536,512]{1,0:T(8,128)(2,1)}, u32[]{:S(2)}, u32[]{:S(2)}) collective-permute-start(bf16[1536,512]{1,0:T(8,128)(2,1)} %broadcast_select_fusion), channel_id=1, source_target_pairs={{0,1},{1,0},{2,3},{3,2},{4,5},{5,4},{6,7},{7,6},{8,9},{9,8},{10,11... | collective-permute-start | bytes 4718600 | tf_op jit(solution)/shard_map/ppermute | solution.py:474
  148.9 2.1 collective-permute-start.12
  149.1 4.0 %collective-permute-start.13 = (bf16[64,512]{1,0:T(8,128)(2,1)S(1)}, bf16[64,512]{1,0:T(8,128)(2,1)S(1)}, u32[]{:S(2)}, u32[]{:S(2)}) collective-permute-start(bf16[64,512]{1,0:T(8,128)(2,1)S(1)} %get-tuple-element.84), channel_id=1, source_target_pairs={{0,7},{1,0},{2,1},{3,2},{4,3},{5,4},{6,5},{7,6},{8,15},{9,8},{10,9... | collective-permute-start | bytes 196616 | tf_op jit(solution)/shard_map/ppermute | solution.py:465
  153.1 2.3 copy-start.17
  158.6 42.9 %all-to-all-start = ((bf16[64,24,512]{2,1,0:T(8,128)(2,1)}), bf16[64,24,512]{2,1,0:T(8,128)(2,1)S(1)}, u32[]{:S(2)}, u32[]{:S(2)}) async-start(bf16[64,24,512]{2,1,0:T(8,128)(2,1)} %bitcast.66), calls=%async_computation | async-start | bytes 3145728 | tf_op jit(solution)/shard_map/all_to_all | solution.py:480
  177.5 24.2 %collective-permute-start.15 = (bf16[256,512]{1,0:T(8,128)(2,1)}, bf16[256,512]{1,0:T(8,128)(2,1)S(1)}, u32[]{:S(2)}, u32[]{:S(2)}) collective-permute-start(bf16[256,512]{1,0:T(8,128)(2,1)} %get-tuple-element.65), channel_id=1, source_target_pairs={{0,8},{8,16},{16,24},{24,32},{32,40},{40,48},{48,56},{56,64},{64,7... | collective-permute-start | bytes 786440 | tf_op jit(solution)/shard_map/ppermute | solution.py:470
  180.4 21.2 %collective-permute-start.16 = (bf16[256,512]{1,0:T(8,128)(2,1)S(1)}, bf16[256,512]{1,0:T(8,128)(2,1)S(1)}, u32[]{:S(2)}, u32[]{:S(2)}) collective-permute-start(bf16[256,512]{1,0:T(8,128)(2,1)S(1)} %get-tuple-element.66), channel_id=1, source_target_pairs={{8,0},{16,8},{24,16},{32,24},{40,32},{48,40},{56,48},{64,56},{72,6... | collective-permute-start | bytes 786440 | tf_op jit(solution)/shard_map/ppermute | solution.py:470
  201.8 33.5 %copy-start.18 = (bf16[64,512]{1,0:T(8,128)(2,1)S(1)}, bf16[64,512]{1,0:T(8,128)(2,1)}, u32[]{:S(2)}) copy-start(bf16[64,512]{1,0:T(8,128)(2,1)} %copy-done.17) | copy-start | bytes 196612
  234.0 4.4 %collective-permute-start.17 = (bf16[1536,512]{1,0:T(8,128)(2,1)S(1)}, bf16[1536,512]{1,0:T(8,128)(2,1)}, u32[]{:S(2)}, u32[]{:S(2)}) collective-permute-start(bf16[1536,512]{1,0:T(8,128)(2,1)S(1)} %bitcast.65), channel_id=1, source_target_pairs={{0,1},{1,0},{2,3},{3,2},{4,5},{5,4},{6,7},{7,6},{8,9},{9,8},{10,11... | collective-permute-start | bytes 4718600 | tf_op jit(solution)/shard_map/ppermute | solution.py:474
  (8 other events, 10.2 us)

commit v4 on v3

--- a/solution.py
+++ b/solution.py
@@ -576,20 +576,14 @@
     swapped = core_swap(jnp.where(leads, dec_stack, enc_stack))
     kept = jnp.where(leads, enc_stack, dec_stack).astype(F32) + swapped.astype(F32)
     kept = kept.astype(BF).reshape(chips, 3 * width // chips, width)
-
-    def met_cells(first, count):
-        rows = band_cot[first * lon_cells : (first + count) * lon_cells].astype(F32).reshape(count, lon_cells, width)
-        at = slice(first * REACH, (first + count) * REACH)
-        gap = jnp.zeros((count, lon_cells - 2 * REACH, width), F32)
-        east = from_right[at].astype(F32).reshape(count, REACH, width)
-        west = from_left[at].astype(F32).reshape(count, REACH, width)
-        return (rows + jnp.concatenate([west, gap, east], axis=1)).reshape(count * lon_cells, width)
-
-    to_upper = met_cells(lat_cells, REACH).astype(BF)
-    to_lower = met_cells(lat_cells + REACH, REACH).astype(BF)
-    kept, to_upper, to_lower = lax.optimization_barrier((kept, to_upper, to_lower))
-    from_low = to_lat(to_upper, 1)
-    from_high = to_lat(to_lower, -1)
+    kept, from_right, from_left = lax.optimization_barrier((kept, from_right, from_left))
+
+    inner_cot = band_cot[:inner_rows].astype(F32).reshape(tall, lon_cells, width)
+    inner_cot = inner_cot.at[:, lon_cells - REACH :].add(from_right.astype(F32).reshape(tall, REACH, width))
+    inner_cot = inner_cot.at[:, :REACH].add(from_left.astype(F32).reshape(tall, REACH, width))
+    inner_cot = inner_cot.reshape(inner_rows, width)
+    from_low = to_lat(inner_cot[cells : cells + edge_rows].astype(BF), 1)
+    from_high = to_lat(inner_cot[cells + edge_rows :].astype(BF), -1)
 
     mine = jnp.sum(across_chips(kept).astype(F32), axis=0).astype(BF)
     mine, from_low, from_high = lax.optimization_barrier((mine, from_low, from_high))
@@ -598,7 +592,7 @@
     enc_grads = jnp.where(leads, ours, theirs).astype(F32)
     dec_grads = jnp.where(leads, theirs, ours).astype(F32)
 
-    sent_cot = met_cells(0, lat_cells) + jnp.concatenate([from_low, from_high], axis=0).astype(F32)
+    sent_cot = inner_cot[:cells] + jnp.concatenate([from_low, from_high], axis=0).astype(F32)
     grid_grad = (grid_part + dot_nt(sent_cot.astype(BF), enc_send)).astype(BF)
 
     return (

time: 244 us -> 236 us (0.967)
  waiting for transfers between devices: 45.5 us -> 40.1 us
  other arithmetic: 15.8 us -> 12.7 us
  starting transfers between devices: 53 us -> 55.6 us
    ppermute x8, waiting for transfers between devices: 17.2 us -> 13.7 us  [to_lon(): lax.ppermute(shard, 'lon', [(i, (i + by) % count) for i in range(count)])]
    all_to_all x1, waiting for transfers between devices: 19.7 us -> 16.3 us  [across_chips(): lax.all_to_all(parts, ('lat', 'lon'), 0, 0, axis_index_groups=alike, tile...]
  transfers between devices with their start and end apart: 19 -> 19, of which waited for: 12 -> 11; matrix products, arithmetic and copies ran while one was open for 4% -> 5% of each run, Pallas kernels for 6% -> 7%
where the time goes in v4:
time: 236 us; the launch traced here: 235 us
  Pallas kernels  83.9 us (36%)
  starting transfers between devices  55.6 us (24%)
  waiting for transfers between devices  40.1 us (17%)
  blocking collectives  30.2 us (13%)
  other arithmetic  12.7 us (5%)
  local copies, waits for them, and re-layouts  9.61 us (4%)
    pallas_call x1, Pallas kernels, enc_backward(): pl.pallas_call(enc_backward_kernel, name='enc_backward', grid=(tiles + 1,...  30.8 us
    all_to_all x1, blocking collectives, across_chips(): lax.all_to_all(parts, ('lat', 'lon'), 0, 0, axis_index_groups=alike, tile...  30.2 us
    pallas_call x1, Pallas kernels, enc_forward(): pl.pallas_call(enc_forward_kernel, name='enc_forward', grid=(nodes // til...  28 us
    ppermute x8, starting transfers between devices, to_lat(): lax.ppermute(shard, 'lat', [(i, i + by) for i in range(count) if 0 <= i +...  22.8 us
    all_to_all x1, starting transfers between devices, across_chips(): lax.all_to_all(parts, ('lat', 'lon'), 0, 0, axis_index_groups=alike, tile...  17.7 us
    all_to_all x1, waiting for transfers between devices, across_chips(): lax.all_to_all(parts, ('lat', 'lon'), 0, 0, axis_index_groups=alike, tile...  16.3 us
    ppermute x8, waiting for transfers between devices, to_lon(): lax.ppermute(shard, 'lon', [(i, (i + by) % count) for i in range(count)])  13.7 us
    pallas_call x2, Pallas kernels, enc_between(): pl.pallas_call(enc_between_kernel, name='enc_between', grid=(count,), in_...  12.8 us
  transfers between devices with their start and end apart: 19, of which 11 were waited for; matrix products, arithmetic and copies ran while one was open for 5% of the time, Pallas kernels for 7%

profile of v4, /device:TPU:1, one launch (start us, length us, event | category | flops | bytes accessed | tf_op | source)
XLA Modules:
  0.0 234.8 jit_solution(15776316594861236373)
XLA Ops:
  1.7 1.3 collective-permute-start
  3.0 4.6 %collective-permute-start.1 = (bf16[256,512]{1,0:T(8,128)(2,1)S(1)}, bf16[256,512]{1,0:T(8,128)(2,1)S(1)}, u32[]{:S(2)}, u32[]{:S(2)}) collective-permute-start(bf16[256,512]{1,0:T(8,128)(2,1)S(1)} %bitcast.66), channel_id=1, source_target_pairs={{0,8},{8,16},{16,24},{24,32},{32,40},{40,48},{48,56},{56,64},{64,7... | collective-permute-start | bytes 786440 | tf_op jit(solution)/shard_map/ppermute | solution.py:470
  8.5 2.7 %collective-permute-done.high_ref = bf16[256,512]{1,0:T(8,128)(2,1)S(1)} collective-permute-done((bf16[256,512]{1,0:T(8,128)(2,1)S(1)}, bf16[256,512]{1,0:T(8,128)(2,1)S(1)}, u32[]{:S(2)}, u32[]{:S(2)}) %collective-permute-start) | collective-permute-done | bytes 262176 | tf_op jit(solution)/shard_map/ppermute | solution.py:470
  13.4 3.5 %collective-permute-start.2 = (bf16[64,512]{1,0:T(8,128)(2,1)S(1)}, bf16[64,512]{1,0:T(8,128)(2,1)S(1)}, u32[]{:S(2)}, u32[]{:S(2)}) collective-permute-start(bf16[64,512]{1,0:T(8,128)(2,1)S(1)} %reshape.154), channel_id=1, source_target_pairs={{0,1},{1,2},{2,3},{3,4},{4,5},{5,6},{6,7},{7,0},{8,9},{9,10},{10,1... | collective-permute-start | bytes 196616 | tf_op jit(solution)/shard_map/ppermute | solution.py:465
  18.7 1.9 collective-permute-done.3.right_ref
  21.2 28.0 %enc_forward.1 = (bf16[256,512]{1,0:T(8,128)(2,1)}, bf16[256,512]{1,0:T(8,128)(2,1)}, bf16[8192,512]{1,0:T(8,128)(2,1)}, bf16[8192,512]{1,0:T(8,128)(2,1)}, bf16...) custom-call(s32[256,32]{1,0:T(8,128)} %select_select_fusion.idx_ref, s32[256,1]{1,0:T(8,128)} %copy.29.count_ref, ...), custom_call_target="tpu_custom_call" | custom-call | tf_op jit(solution)/shard_map/enc_forward/pallas_call | solution.py:145
  49.2 1.3 collective-permute-start.4
  50.5 4.9 %collective-permute-start.5 = (bf16[256,512]{1,0:T(8,128)(2,1)}, bf16[256,512]{1,0:T(8,128)(2,1)S(1)}, u32[]{:S(2)}, u32[]{:S(2)}) collective-permute-start(bf16[256,512]{1,0:T(8,128)(2,1)} %get-tuple-element.64), channel_id=1, source_target_pairs={{0,8},{8,16},{16,24},{24,32},{32,40},{40,48},{48,56},{56,64},{64,7... | collective-permute-start | bytes 786440 | tf_op jit(solution)/shard_map/ppermute | solution.py:470
  55.5 6.3 %enc_between.2.refs_0_ = bf16[8192,512]{1,0:T(8,128)(2,1)} custom-call(bf16[8192,512]{1,0:T(8,128)(2,1)} %get-tuple-element.65.normed_ref, bf16[512,512]{1,0:T(8,128)(2,1)} %out_ref.9), custom_call_target="tpu_custom_call" | custom-call | flops 2147483648 | bytes 8388608 | tf_op jit(solution)/shard_map/enc_between/pallas_call | solution.py:182
  62.8 6.4 %enc_between.3.turned_ref = bf16[8192,512]{1,0:T(8,128)(2,1)} custom-call(bf16[8192,512]{1,0:T(8,128)(2,1)} %get-tuple-element.65.normed_ref, bf16[512,512]{1,0:T(8,128)(2,1)} %out_ref.9, bf16[8192,512]{1,0:T(8,128)(2,1)} %enc_between.2.refs_0_), custom_call_target="tpu_custom_call", output_to_operand_aliasing={{}: (2, {})} | custom-call | flops 2147483648 | bytes 8388608 | tf_op jit(solution)/shard_map/enc_between/pallas_call | solution.py:182
  69.3 1.8 collective-permute-done.6.left_ref
  71.1 2.8 %collective-permute-done.7.right_ref = bf16[768,512]{1,0:T(8,128)(2,1)S(1)} collective-permute-done((bf16[768,512]{1,0:T(8,128)(2,1)S(1)}, bf16[768,512]{1,0:T(8,128)(2,1)S(1)}, u32[]{:S(2)}, u32[]{:S(2)}) %collective-permute-start.7) | collective-permute-done | bytes 786464 | tf_op jit(solution)/shard_map/ppermute | solution.py:465
  73.9 9.5 %decoder.1 = (bf16[512,512]{1,0:T(8,128)(2,1)}, bf16[1536,512]{1,0:T(8,128)(2,1)S(1)}, bf16[1536,512]{1,0:T(8,128)(2,1)S(1)}, bf16[1536,512]{1,0:T(8,128)(2,1)S(...) custom-call(s32[512,3]{1,0:T(8,128)S(1)} %copy.30.idx_ref, ...), custom_call_target="tpu_custom_call" | custom-call | tf_op jit(solution)/shard_map/decoder/pallas_call | solution.py:277
  85.2 2.7 %decoder_rest.1 = (f32[512,512]{1,0:T(8,128)S(1)}, bf16[512,512]{1,0:T(8,128)(2,1)S(1)}, bf16[512,512]{1,0:T(8,128)(2,1)S(1)}, bf16[768,512]{1,0:T(8,128)(2,1)S(1)}) custom-call(s32[3,512]{1,0:T(4,128)S(1)} %fusion.28.idx_row_ref, bf16[512,512]{1,0:T(8,128)(2,1)S(1)} %bitcast.56, bf16[512,512]{1,0:T(8,128)(2,1)S(1)} %bitcast.58, ...), custom_call_target="tpu_custom_call" | custom-call | flops 2818572288 | bytes 6291456 | tf_op jit(solution)/shard_map/decoder_rest/pallas_call | solution.py:315
  88.0 7.2 %collective-permute-done.8 = bf16[768,512]{1,0:T(8,128)(2,1)S(1)} collective-permute-done((bf16[768,512]{1,0:T(8,128)(2,1)S(1)}, bf16[768,512]{1,0:T(8,128)(2,1)S(1)}, u32[]{:S(2)}, u32[]{:S(2)}) %collective-permute-start.8) | collective-permute-done | bytes 786464 | tf_op jit(solution)/shard_map/ppermute | solution.py:465
  97.0 4.4 %collective-permute-start.10 = (bf16[256,512]{1,0:T(8,128)(2,1)}, bf16[256,512]{1,0:T(8,128)(2,1)}, u32[]{:S(2)}, u32[]{:S(2)}) collective-permute-start(bf16[256,512]{1,0:T(8,128)(2,1)} %get-tuple-element.103), channel_id=1, source_target_pairs={{0,8},{8,16},{16,24},{24,32},{32,40},{40,48},{48,56},{56,64},{64,7... | collective-permute-start | bytes 786440 | tf_op jit(solution)/shard_map/ppermute | solution.py:470
  101.5 1.5 collective-permute-start.11
  104.4 4.5 %collective-permute-done.11 = bf16[256,512]{1,0:T(8,128)(2,1)} collective-permute-done((bf16[256,512]{1,0:T(8,128)(2,1)}, bf16[256,512]{1,0:T(8,128)(2,1)}, u32[]{:S(2)}, u32[]{:S(2)}) %collective-permute-start.11) | collective-permute-done | bytes 262176 | tf_op jit(solution)/shard_map/ppermute | solution.py:470
  108.9 1.4 add_convert_fusion.1.moved_cot_ref
  110.9 30.8 %enc_backward.1 = (bf16[256,512]{1,0:T(8,128)(2,1)}, bf16[1152,512]{1,0:T(8,128)(2,1)}, bf16[1536,512]{1,0:T(8,128)(2,1)}) custom-call(s32[8,1,1024]{2,1,0:T(1,128)} %reshape.158.idx_row_ref, f32[256,32]{1,0:T(8,128)} %get-tuple-element.76.scale_ref, bf16[256,512]{1,0:T(8,128)(2,1)} %bitcast.64, bf16[256,512]{1,0:T(8,128)(2,1)} %copy-done.5, ...), custom_call_target="tpu_custom_call" | custom-call | tf_op jit(solution)/shard_map/enc_backward/pallas_call | solution.py:428
  141.8 2.0 broadcast_select_fusion
  143.8 4.2 %collective-permute-start.12 = (bf16[1536,512]{1,0:T(8,128)(2,1)S(1)}, bf16[1536,512]{1,0:T(8,128)(2,1)S(1)}, u32[]{:S(2)}, u32[]{:S(2)}) collective-permute-start(bf16[1536,512]{1,0:T(8,128)(2,1)S(1)} %broadcast_select_fusion), channel_id=1, source_target_pairs={{0,1},{1,0},{2,3},{3,2},{4,5},{5,4},{6,7},{7,6},{8,9},{9,8},{10,11... | collective-permute-start | bytes 4718600 | tf_op jit(solution)/shard_map/ppermute | solution.py:474
  151.0 1.8 add_convert_fusion
  152.8 17.7 %all-to-all-start = ((bf16[64,24,512]{2,1,0:T(8,128)(2,1)}), bf16[64,24,512]{2,1,0:T(8,128)(2,1)}, u32[]{:S(2)}, u32[]{:S(2)}) async-start(bf16[64,24,512]{2,1,0:T(8,128)(2,1)} %bitcast.60), calls=%async_computation | async-start | bytes 3145728 | tf_op jit(solution)/shard_map/all_to_all | solution.py:480
  172.0 3.5 %collective-permute-start.15 = (bf16[256,512]{1,0:T(8,128)(2,1)}, bf16[256,512]{1,0:T(8,128)(2,1)}, u32[]{:S(2)}, u32[]{:S(2)}) collective-permute-start(bf16[256,512]{1,0:T(8,128)(2,1)} %bitcast.15), channel_id=1, source_target_pairs={{0,8},{8,16},{16,24},{24,32},{32,40},{40,48},{48,56},{56,64},{64,7... | collective-permute-start | bytes 786440 | tf_op jit(solution)/shard_map/ppermute | solution.py:470
  175.5 1.3 collective-permute-start.16
  176.8 16.3 %all-to-all-done = bf16[64,24,512]{2,1,0:T(8,128)(2,1)} async-done(((bf16[64,24,512]{2,1,0:T(8,128)(2,1)}), bf16[64,24,512]{2,1,0:T(8,128)(2,1)}, u32[]{:S(2)}, u32[]{:S(2)}) %all-to-all-start) | async-done | bytes 1572896 | tf_op jit(solution)/shard_map/all_to_all | solution.py:480
  193.1 1.7 reduce_sum.22
  194.9 30.2 %all_to_all.10 = bf16[64,24,512]{2,1,0:T(8,128)(2,1)S(1)} all-to-all(bf16[64,24,512]{2,1,0:T(8,128)(2,1)S(1)} %broadcast_in_dim.12), channel_id=1, replica_groups={{0,2,4,6,8,10,12,14,16,18,20,22,24,26,28,30,32,34,36,38,40,42,44,46,48,..., dimensions={0} | all-to-all | bytes 3145728 | tf_op jit(solution)/shard_map/all_to_all | solution.py:480
  225.0 3.4 %collective-permute-start.17 = (bf16[1536,512]{1,0:T(8,128)(2,1)S(1)}, bf16[1536,512]{1,0:T(8,128)(2,1)S(1)}, u32[]{:S(2)}, u32[]{:S(2)}) collective-permute-start(bf16[1536,512]{1,0:T(8,128)(2,1)S(1)} %bitcast.59), channel_id=1, source_target_pairs={{0,1},{1,0},{2,3},{3,2},{4,5},{5,4},{6,7},{7,6},{8,9},{9,8},{10,11... | collective-permute-start | bytes 4718600 | tf_op jit(solution)/shard_map/ppermute | solution.py:474
  229.8 1.3 fusion
  232.0 2.7 %fusion.32 = (f32[512,512]{1,0:T(8,128)}, f32[512,512]{1,0:T(8,128)}, f32[512,512]{1,0:T(8,128)}, f32[512,512]{1,0:T(8,128)}, f32[512,512]{1,0:T(8,128)}, /*index=5*/f32[512,512]{1,0:T(8,128)}) fusion(f32[1536,512]{1,0:T(8,128)S(1)} %get-tuple-element.98, f32[1536,512]{1,0:T(8,128)S(1)} %get-tuple-element.99), kind=kLoop, calls=%fused_computation.90 | loop fusion | bytes 12582912 | tf_op jit(solution)/shard_map/slice | solution.py:607
  (89 shorter events, 20.0 us)
Async XLA Ops:
  0.6 17.2 %copy-start.17 = (s32[1,1,256,32]{2,3,1,0:T(8,128)S(1)}, s32[1,1,256,32]{2,3,1,0:T(8,128)}, u32[]{:S(2)}) copy-start(s32[1,1,256,32]{2,3,1,0:T(8,128)} %param.26) | copy-start | bytes 98308
  1.7 9.5 %collective-permute-start = (bf16[256,512]{1,0:T(8,128)(2,1)S(1)}, bf16[256,512]{1,0:T(8,128)(2,1)S(1)}, u32[]{:S(2)}, u32[]{:S(2)}) collective-permute-start(bf16[256,512]{1,0:T(8,128)(2,1)S(1)} %bitcast.67), channel_id=1, source_target_pairs={{8,0},{16,8},{24,16},{32,24},{40,32},{48,40},{56,48},{64,56},{72,6... | collective-permute-start | bytes 786440 | tf_op jit(solution)/shard_map/ppermute | solution.py:470
  3.0 9.0 %collective-permute-start.1 = (bf16[256,512]{1,0:T(8,128)(2,1)S(1)}, bf16[256,512]{1,0:T(8,128)(2,1)S(1)}, u32[]{:S(2)}, u32[]{:S(2)}) collective-permute-start(bf16[256,512]{1,0:T(8,128)(2,1)S(1)} %bitcast.66), channel_id=1, source_target_pairs={{0,8},{8,16},{16,24},{24,32},{32,40},{40,48},{48,56},{56,64},{64,7... | collective-permute-start | bytes 786440 | tf_op jit(solution)/shard_map/ppermute | solution.py:470
  11.2 9.4 %copy-start.6 = (bf16[256,512]{1,0:T(8,128)(2,1)}, bf16[256,512]{1,0:T(8,128)(2,1)S(1)}, u32[]{:S(2)}) copy-start(bf16[256,512]{1,0:T(8,128)(2,1)S(1)} %collective-permute-done.high_ref) | copy-start | bytes 786436
  12.1 8.5 %copy-start.7 = (bf16[256,512]{1,0:T(8,128)(2,1)}, bf16[256,512]{1,0:T(8,128)(2,1)S(1)}, u32[]{:S(2)}) copy-start(bf16[256,512]{1,0:T(8,128)(2,1)S(1)} %collective-permute-done.1.low_ref) | copy-start | bytes 786436
  13.4 5.3 %collective-permute-start.2 = (bf16[64,512]{1,0:T(8,128)(2,1)S(1)}, bf16[64,512]{1,0:T(8,128)(2,1)S(1)}, u32[]{:S(2)}, u32[]{:S(2)}) collective-permute-start(bf16[64,512]{1,0:T(8,128)(2,1)S(1)} %reshape.154), channel_id=1, source_target_pairs={{0,1},{1,2},{2,3},{3,4},{4,5},{5,6},{6,7},{7,0},{8,9},{9,10},{10,1... | collective-permute-start | bytes 196616 | tf_op jit(solution)/shard_map/ppermute | solution.py:465
  16.9 3.7 %collective-permute-start.3 = (bf16[64,512]{1,0:T(8,128)(2,1)S(1)}, bf16[64,512]{1,0:T(8,128)(2,1)S(1)}, u32[]{:S(2)}, u32[]{:S(2)}) collective-permute-start(bf16[64,512]{1,0:T(8,128)(2,1)S(1)} %reshape.155), channel_id=1, source_target_pairs={{0,7},{1,0},{2,1},{3,2},{4,3},{5,4},{6,5},{7,6},{8,15},{9,8},{10,9... | collective-permute-start | bytes 196616 | tf_op jit(solution)/shard_map/ppermute | solution.py:465
  49.2 12.6 %collective-permute-start.4 = (bf16[256,512]{1,0:T(8,128)(2,1)}, bf16[256,512]{1,0:T(8,128)(2,1)S(1)}, u32[]{:S(2)}, u32[]{:S(2)}) collective-permute-start(bf16[256,512]{1,0:T(8,128)(2,1)} %get-tuple-element.64), channel_id=1, source_target_pairs={{8,0},{16,8},{24,16},{32,24},{40,32},{48,40},{56,48},{64,56},{72,6... | collective-permute-start | bytes 786440 | tf_op jit(solution)/shard_map/ppermute | solution.py:470
  50.5 11.3 %collective-permute-start.5 = (bf16[256,512]{1,0:T(8,128)(2,1)}, bf16[256,512]{1,0:T(8,128)(2,1)S(1)}, u32[]{:S(2)}, u32[]{:S(2)}) collective-permute-start(bf16[256,512]{1,0:T(8,128)(2,1)} %get-tuple-element.64), channel_id=1, source_target_pairs={{0,8},{8,16},{16,24},{24,32},{32,40},{40,48},{48,56},{56,64},{64,7... | collective-permute-start | bytes 786440 | tf_op jit(solution)/shard_map/ppermute | solution.py:470
  55.4 6.4 %copy-start.15 = (bf16[256,512]{1,0:T(8,128)(2,1)S(1)}, bf16[256,512]{1,0:T(8,128)(2,1)}, u32[]{:S(2)}) copy-start(bf16[256,512]{1,0:T(8,128)(2,1)} %get-tuple-element.64) | copy-start | bytes 786436
  55.4 7.0 %copy-start.18 = (s32[3,8,64]{2,1,0:T(8,128)S(1)}, s32[3,8,64]{2,1,0:T(8,128)}, u32[]{:S(2)}) copy-start(s32[3,8,64]{2,1,0:T(8,128)} %param.27) | copy-start | bytes 18436
  61.9 9.2 %collective-permute-start.6 = (bf16[768,512]{1,0:T(8,128)(2,1)S(1)}, bf16[768,512]{1,0:T(8,128)(2,1)S(1)}, u32[]{:S(2)}, u32[]{:S(2)}) collective-permute-start(bf16[768,512]{1,0:T(8,128)(2,1)S(1)} %pad_maximum_fusion.2.centre_ref), channel_id=1, source_target_pairs={{0,1},{1,2},{2,3},{3,4},{4,5},{5,6},{6,7},{7,0},{8,9},{9,10},{10,1... | collective-permute-start | bytes 2359304 | tf_op jit(solution)/shard_map/ppermute | solution.py:465
  62.2 11.7 %collective-permute-start.7 = (bf16[768,512]{1,0:T(8,128)(2,1)S(1)}, bf16[768,512]{1,0:T(8,128)(2,1)S(1)}, u32[]{:S(2)}, u32[]{:S(2)}) collective-permute-start(bf16[768,512]{1,0:T(8,128)(2,1)S(1)} %pad_maximum_fusion.2.centre_ref), channel_id=1, source_target_pairs={{0,7},{1,0},{2,1},{3,2},{4,3},{5,4},{6,5},{7,6},{8,15},{9,8},{10,9... | collective-permute-start | bytes 2359304 | tf_op jit(solution)/shard_map/ppermute | solution.py:465
  62.8 11.1 %copy-start = (bf16[8,64,512]{2,1,0:T(8,128)(2,1)S(1)}, bf16[8,64,512]{2,1,0:T(8,128)(2,1)}, u32[]{:S(2)}) copy-start(bf16[8,64,512]{2,1,0:T(8,128)(2,1)} %param.16) | copy-start | bytes 1572868
  62.8 11.1 %copy-start.1 = (bf16[512,512]{1,0:T(8,128)(2,1)S(1)}, bf16[512,512]{1,0:T(8,128)(2,1)}, u32[]{:S(2)}) copy-start(bf16[512,512]{1,0:T(8,128)(2,1)} %out_ref.8) | copy-start | bytes 1572868
  62.8 11.1 %copy-start.2 = (bf16[8,64,512]{2,1,0:T(8,128)(2,1)S(1)}, bf16[8,64,512]{2,1,0:T(8,128)(2,1)}, u32[]{:S(2)}) copy-start(bf16[8,64,512]{2,1,0:T(8,128)(2,1)} %param.18) | copy-start | bytes 1572868
  62.8 11.1 %copy-start.3 = (bf16[512,512]{1,0:T(8,128)(2,1)S(1)}, bf16[512,512]{1,0:T(8,128)(2,1)}, u32[]{:S(2)}) copy-start(bf16[512,512]{1,0:T(8,128)(2,1)} %recv_ref.6) | copy-start | bytes 1572868
  83.4 11.7 %collective-permute-start.8 = (bf16[768,512]{1,0:T(8,128)(2,1)S(1)}, bf16[768,512]{1,0:T(8,128)(2,1)S(1)}, u32[]{:S(2)}, u32[]{:S(2)}) collective-permute-start(bf16[768,512]{1,0:T(8,128)(2,1)S(1)} %get-tuple-element.78), channel_id=1, source_target_pairs={{0,7},{1,0},{2,1},{3,2},{4,3},{5,4},{6,5},{7,6},{8,15},{9,8},{10,9... | collective-permute-start | bytes 2359304 | tf_op jit(solution)/shard_map/ppermute | solution.py:465
  84.3 10.8 %collective-permute-start.9 = (bf16[768,512]{1,0:T(8,128)(2,1)S(1)}, bf16[768,512]{1,0:T(8,128)(2,1)S(1)}, u32[]{:S(2)}, u32[]{:S(2)}) collective-permute-start(bf16[768,512]{1,0:T(8,128)(2,1)S(1)} %get-tuple-element.79), channel_id=1, source_target_pairs={{0,1},{1,2},{2,3},{3,4},{4,5},{5,6},{6,7},{7,0},{8,9},{9,10},{10,1... | collective-permute-start | bytes 2359304 | tf_op jit(solution)/shard_map/ppermute | solution.py:465
  87.9 15.0 %copy-start.16 = (s32[1,1,256,32]{2,3,1,0:T(8,128)S(1)}, s32[1,1,256,32]{2,3,1,0:T(8,128)}, u32[]{:S(2)}) copy-start(s32[1,1,256,32]{2,3,1,0:T(8,128)} %param.25) | copy-start | bytes 98308
  96.0 14.2 %copy-start.14 = (bf16[256,512]{1,0:T(8,128)(2,1)S(1)}, bf16[256,512]{1,0:T(8,128)(2,1)}, u32[]{:S(2)}) copy-start(bf16[256,512]{1,0:T(8,128)(2,1)} %get-tuple-element.85) | copy-start | bytes 786436
  97.0 7.3 %collective-permute-start.10 = (bf16[256,512]{1,0:T(8,128)(2,1)}, bf16[256,512]{1,0:T(8,128)(2,1)}, u32[]{:S(2)}, u32[]{:S(2)}) collective-permute-start(bf16[256,512]{1,0:T(8,128)(2,1)} %get-tuple-element.103), channel_id=1, source_target_pairs={{0,8},{8,16},{16,24},{24,32},{32,40},{40,48},{48,56},{56,64},{64,7... | collective-permute-start | bytes 786440 | tf_op jit(solution)/shard_map/ppermute | solution.py:470
  101.5 7.4 %collective-permute-start.11 = (bf16[256,512]{1,0:T(8,128)(2,1)}, bf16[256,512]{1,0:T(8,128)(2,1)}, u32[]{:S(2)}, u32[]{:S(2)}) collective-permute-start(bf16[256,512]{1,0:T(8,128)(2,1)} %get-tuple-element.104), channel_id=1, source_target_pairs={{8,0},{16,8},{24,16},{32,24},{40,32},{48,40},{56,48},{64,56},{72,6... | collective-permute-start | bytes 786440 | tf_op jit(solution)/shard_map/ppermute | solution.py:470
  141.8 6.2 %copy-start.9 = (bf16[1152,512]{1,0:T(8,128)(2,1)S(1)}, bf16[1152,512]{1,0:T(8,128)(2,1)}, u32[]{:S(2)}) copy-start(bf16[1152,512]{1,0:T(8,128)(2,1)} %get-tuple-element.83) | copy-start | bytes 3538948
  141.8 9.2 %copy-start.4 = (bf16[1536,512]{1,0:T(8,128)(2,1)S(1)}, bf16[1536,512]{1,0:T(8,128)(2,1)}, u32[]{:S(2)}) copy-start(bf16[1536,512]{1,0:T(8,128)(2,1)} %get-tuple-element.84) | copy-start | bytes 4718596
  143.8 7.2 %collective-permute-start.12 = (bf16[1536,512]{1,0:T(8,128)(2,1)S(1)}, bf16[1536,512]{1,0:T(8,128)(2,1)S(1)}, u32[]{:S(2)}, u32[]{:S(2)}) collective-permute-start(bf16[1536,512]{1,0:T(8,128)(2,1)S(1)} %broadcast_select_fusion), channel_id=1, source_target_pairs={{0,1},{1,0},{2,3},{3,2},{4,5},{5,4},{6,7},{7,6},{8,9},{9,8},{10,11... | collective-permute-start | bytes 4718600 | tf_op jit(solution)/shard_map/ppermute | solution.py:474
  148.0 4.8 %collective-permute-start.13 = (bf16[64,512]{1,0:T(8,128)(2,1)S(1)}, bf16[64,512]{1,0:T(8,128)(2,1)S(1)}, u32[]{:S(2)}, u32[]{:S(2)}) collective-permute-start(bf16[64,512]{1,0:T(8,128)(2,1)S(1)} %get-tuple-element.106), channel_id=1, source_target_pairs={{0,7},{1,0},{2,1},{3,2},{4,3},{5,4},{6,5},{7,6},{8,15},{9,8},{10,9... | collective-permute-start | bytes 196616 | tf_op jit(solution)/shard_map/ppermute | solution.py:465
  148.7 4.1 %collective-permute-start.14 = (bf16[64,512]{1,0:T(8,128)(2,1)S(1)}, bf16[64,512]{1,0:T(8,128)(2,1)S(1)}, u32[]{:S(2)}, u32[]{:S(2)}) collective-permute-start(bf16[64,512]{1,0:T(8,128)(2,1)S(1)} %get-tuple-element.105), channel_id=1, source_target_pairs={{0,1},{1,2},{2,3},{3,4},{4,5},{5,6},{6,7},{7,0},{8,9},{9,10},{10,1... | collective-permute-start | bytes 196616 | tf_op jit(solution)/shard_map/ppermute | solution.py:465
  152.8 40.3 %all-to-all-start = ((bf16[64,24,512]{2,1,0:T(8,128)(2,1)}), bf16[64,24,512]{2,1,0:T(8,128)(2,1)}, u32[]{:S(2)}, u32[]{:S(2)}) async-start(bf16[64,24,512]{2,1,0:T(8,128)(2,1)} %bitcast.60), calls=%async_computation | async-start | bytes 3145728 | tf_op jit(solution)/shard_map/all_to_all | solution.py:480
  172.0 22.8 %collective-permute-start.15 = (bf16[256,512]{1,0:T(8,128)(2,1)}, bf16[256,512]{1,0:T(8,128)(2,1)}, u32[]{:S(2)}, u32[]{:S(2)}) collective-permute-start(bf16[256,512]{1,0:T(8,128)(2,1)} %bitcast.15), channel_id=1, source_target_pairs={{0,8},{8,16},{16,24},{24,32},{32,40},{40,48},{48,56},{56,64},{64,7... | collective-permute-start | bytes 786440 | tf_op jit(solution)/shard_map/ppermute | solution.py:470
  175.5 19.3 %collective-permute-start.16 = (bf16[256,512]{1,0:T(8,128)(2,1)S(1)}, bf16[256,512]{1,0:T(8,128)(2,1)}, u32[]{:S(2)}, u32[]{:S(2)}) collective-permute-start(bf16[256,512]{1,0:T(8,128)(2,1)S(1)} %bitcast.68), channel_id=1, source_target_pairs={{8,0},{16,8},{24,16},{32,24},{40,32},{48,40},{56,48},{64,56},{72,6... | collective-permute-start | bytes 786440 | tf_op jit(solution)/shard_map/ppermute | solution.py:470
  225.0 6.5 %collective-permute-start.17 = (bf16[1536,512]{1,0:T(8,128)(2,1)S(1)}, bf16[1536,512]{1,0:T(8,128)(2,1)S(1)}, u32[]{:S(2)}, u32[]{:S(2)}) collective-permute-start(bf16[1536,512]{1,0:T(8,128)(2,1)S(1)} %bitcast.59), channel_id=1, source_target_pairs={{0,1},{1,0},{2,3},{3,2},{4,5},{5,4},{6,7},{7,6},{8,9},{9,8},{10,11... | collective-permute-start | bytes 4718600 | tf_op jit(solution)/shard_map/ppermute | solution.py:474
  (6 other events, 10.7 us)

commit v5 on v4

--- a/solution.py
+++ b/solution.py
@@ -193,14 +193,17 @@
 
 
 def decoder_kernel(
-    idx_ref, idx_row_ref, grid_ref, cot_ref, centre_ref, left_ref, right_ref,
+    idx_ref, idx_row_ref, grid_ref, cot_ref, b0_ref, b1_ref, b2_ref, b3_ref, b4_ref, b5_ref,
     recv_ref, out_ref,
-    new_ref, hidden_ref, message_cot_ref, before_cot_ref, received_cot_ref, left_tot_ref, right_tot_ref,
+    new_ref, hidden_ref, message_cot_ref, before_cot_ref, received_cot_ref,
+    left_own_ref, left_ref, right_own_ref, right_ref,
     onehot, onehot_t, received_all, new_all, received_cot_all,
 ):
     nodes, width = grid_ref.shape
     degree = idx_ref.shape[1]
-    third = centre_ref.shape[0]
+    blocks = (b0_ref, b1_ref, b2_ref, b3_ref, b4_ref, b5_ref)
+    third = b0_ref.shape[0] + b1_ref.shape[0]
+    slots = b0_ref.shape[0]
     tile = DEC_TILE
     parts = nodes // tile
     index = idx_ref[...].astype(jnp.int16)
@@ -219,9 +222,12 @@
 
     def gather(i):
         j, at, edges = spot(i)
-        gathered = dot(onehot[edges, :third], centre_ref[...])
-        gathered = gathered + dot(onehot[edges, third : 2 * third], left_ref[...])
-        held["gathered", i] = gathered + dot(onehot[edges, 2 * third :], right_ref[...])
+        gathered, first = 0.0, 0
+        for block in blocks:
+            last = first + block.shape[0]
+            gathered = gathered + dot(onehot[edges, first:last], block[...])
+            first = last
+        held["gathered", i] = gathered
 
     def activate(i):
         j, at, edges = spot(i)
@@ -261,23 +267,28 @@
         onehot_t[:, edges] = one_hot(picks, rows.astype(jnp.int16))
 
     staggered([place, gather, activate, norm, back], degree * parts)
-    left_tot_ref[...] = dot(onehot_t[:third, :], before_cot_ref[...]).astype(BF)
+    left_tot = dot(onehot_t[:third, :], before_cot_ref[...]).astype(BF)
+    left_own_ref[...] = left_tot[:slots, :]
+    left_ref[...] = left_tot[slots:, :]
     new_ref[...] = new_all[...].astype(BF)
-    right_tot_ref[...] = dot(onehot_t[third:, :], before_cot_ref[...]).astype(BF)
+    right_tot = dot(onehot_t[third:, :], before_cot_ref[...]).astype(BF)
+    right_own_ref[...] = right_tot[:slots, :]
+    right_ref[...] = right_tot[slots:, :]
     received_cot_ref[...] = received_cot_all[...].astype(BF)
 
 
-def decoder(idx, idx_rows, grid_rows, cot_rows, centre, left, right, dec_recv, dec_out):
+def decoder(idx, idx_rows, grid_rows, cot_rows, blocks, dec_recv, dec_out):
     nodes, width = grid_rows.shape
     degree = idx.shape[1]
-    third = centre.shape[0]
+    third = blocks[0].shape[0] + blocks[1].shape[0]
     edge_shape = jax.ShapeDtypeStruct((degree * nodes, width), BF)
     node_shape = jax.ShapeDtypeStruct((nodes, width), BF)
-    side_shape = jax.ShapeDtypeStruct((third, width), BF)
+    own_shape = jax.ShapeDtypeStruct(blocks[0].shape, BF)
+    side_shape = jax.ShapeDtypeStruct(blocks[1].shape, BF)
     return pl.pallas_call(
         decoder_kernel,
         name="decoder",
-        out_shape=[node_shape, edge_shape, edge_shape, edge_shape, node_shape, side_shape, side_shape],
+        out_shape=[node_shape, edge_shape, edge_shape, edge_shape, node_shape, own_shape, side_shape, own_shape, side_shape],
         scratch_shapes=[
             pltpu.VMEM((degree * nodes, 3 * third), BF),
             pltpu.VMEM((2 * third, degree * nodes), BF),
@@ -286,7 +297,7 @@
             pltpu.VMEM((nodes, width), F32),
         ],
         compiler_params=kernel_params(36),
-    )(idx, idx_rows, grid_rows, cot_rows, centre, left, right, dec_recv, dec_out)
+    )(idx, idx_rows, grid_rows, cot_rows, *blocks, dec_recv, dec_out)
 
 
 def decoder_rest_kernel(
@@ -537,15 +548,20 @@
     half = slots * degree // 2
     block = half // 4
     part = enc_between(normed, enc_out, 0, 4, block)
-    centre = jnp.concatenate([moved, above, below], axis=0)
-    centre, part = lax.optimization_barrier((centre, part))
-    west = to_lon(centre, 1)
-    east = to_lon(centre, -1)
+    own_west = to_lon(moved, 1)
+    own_east = to_lon(moved, -1)
+    sides = jnp.concatenate([above, below], axis=0)
+    sides, part = lax.optimization_barrier((sides, part))
+    west = to_lon(sides, 1)
+    east = to_lon(sides, -1)
     turned = enc_between(normed, enc_out, 4, 4, block, part)
     west, east, turned = lax.optimization_barrier((west, east, turned))
     cot_rows = grid_cot.reshape(cells, width)
-    grid_new, dec_hidden, dec_message_cot, dec_before_cot, dec_received_cot, west_tot, east_tot = decoder(
-        dec_idx_rows.T, dec_idx_rows, grid_rows, cot_rows, centre, west, east, dec_recv, dec_out
+    (
+        grid_new, dec_hidden, dec_message_cot, dec_before_cot, dec_received_cot, west_own, west_tot, east_own, east_tot,
+    ) = decoder(
+        dec_idx_rows.T, dec_idx_rows, grid_rows, cot_rows, (moved, sides, own_west, west, own_east, east),
+        dec_recv, dec_out,
     )
     from_east = to_lon(west_tot, -1)
     from_west = to_lon(east_tot, 1)
@@ -553,12 +569,17 @@
         dec_idx_rows, grid_rows, cot_rows, dec_hidden, dec_message_cot, dec_before_cot, dec_received_cot,
         dec_recv, 3 * slots,
     )
-    def met(at):
-        return centre_tot[at].astype(F32) + from_east[at].astype(F32) + from_west[at].astype(F32)
-
-    from_below = to_lat(met(slice(slots, 2 * slots)).astype(BF), 1)
-    from_above = to_lat(met(slice(2 * slots, 3 * slots)).astype(BF), -1)
-    moved_cot = met(slice(0, slots)) + from_below.astype(F32) + from_above.astype(F32)
+    from_east, from_west, west_own, east_own = lax.optimization_barrier((from_east, from_west, west_own, east_own))
+
+    def met(first):
+        at = slice(first, first + slots)
+        other = centre_tot[slots + first : 2 * slots + first].astype(F32)
+        return (other + from_east[at].astype(F32) + from_west[at].astype(F32)).astype(BF)
+
+    from_below = to_lat(met(0), 1)
+    from_above = to_lat(met(slots), -1)
+    own_cot = to_lon(west_own, -1).astype(F32) + to_lon(east_own, 1).astype(F32)
+    moved_cot = centre_tot[:slots].astype(F32) + own_cot + from_below.astype(F32) + from_above.astype(F32)
     moved_cot = moved_cot.astype(BF)
     dec_send_grad = dot_tn(mesh_new, moved_cot).astype(BF)
 

time: 236 us -> 233 us (0.987)
  waiting for transfers between devices: 40.1 us -> 32.3 us
  starting transfers between devices: 55.6 us -> 61.3 us
    ppermute x8 -> x12, starting transfers between devices: 7.53 us -> 15.5 us  [to_lon(): lax.ppermute(shard, 'lon', [(i, (i + by) % count) for i in range(count)])]
    ppermute x8, waiting for transfers between devices: 8.37 us -> 3.6 us  [to_lat(): lax.ppermute(shard, 'lat', [(i, i + by) for i in range(count) if 0 <= i +...]
    ppermute x8 -> x12, waiting for transfers between devices: 13.7 us -> 10.8 us  [to_lon(): lax.ppermute(shard, 'lon', [(i, (i + by) % count) for i in range(count)])]
  transfers between devices with their start and end apart: 19 -> 23, of which waited for: 11 -> 10; matrix products, arithmetic and copies ran while one was open for 5% -> 5% of each run, Pallas kernels for 7% -> 7%
where the time goes in v5:
time: 233 us; the launch traced here: 232 us
  Pallas kernels  84.4 us (36%)
  starting transfers between devices  61.3 us (26%)
  waiting for transfers between devices  32.3 us (14%)
  blocking collectives  30.2 us (13%)
  other arithmetic  13.6 us (6%)
  local copies, waits for them, and re-layouts  8.73 us (4%)
    pallas_call x1, Pallas kernels, enc_backward(): pl.pallas_call(enc_backward_kernel, name='enc_backward', grid=(tiles + 1,...  30.8 us
    all_to_all x1, blocking collectives, across_chips(): lax.all_to_all(parts, ('lat', 'lon'), 0, 0, axis_index_groups=alike, tile...  30.2 us
    pallas_call x1, Pallas kernels, enc_forward(): pl.pallas_call(enc_forward_kernel, name='enc_forward', grid=(nodes // til...  28 us
    ppermute x8, starting transfers between devices, to_lat(): lax.ppermute(shard, 'lat', [(i, i + by) for i in range(count) if 0 <= i +...  22.8 us
    all_to_all x1, starting transfers between devices, across_chips(): lax.all_to_all(parts, ('lat', 'lon'), 0, 0, axis_index_groups=alike, tile...  17.4 us
    all_to_all x1, waiting for transfers between devices, across_chips(): lax.all_to_all(parts, ('lat', 'lon'), 0, 0, axis_index_groups=alike, tile...  16.3 us
    ppermute x12, starting transfers between devices, to_lon(): lax.ppermute(shard, 'lon', [(i, (i + by) % count) for i in range(count)])  15.5 us
    pallas_call x2, Pallas kernels, enc_between(): pl.pallas_call(enc_between_kernel, name='enc_between', grid=(count,), in_...  12.8 us
  transfers between devices with their start and end apart: 23, of which 10 were waited for; matrix products, arithmetic and copies ran while one was open for 5% of the time, Pallas kernels for 7%

profile of v5, /device:TPU:1, one launch (start us, length us, event | category | flops | bytes accessed | tf_op | source)
XLA Modules:
  0.0 232.4 jit_solution(4652671182920089431)
XLA Ops:
  1.7 1.3 collective-permute-start
  3.0 4.6 %collective-permute-start.1 = (bf16[256,512]{1,0:T(8,128)(2,1)S(1)}, bf16[256,512]{1,0:T(8,128)(2,1)S(1)}, u32[]{:S(2)}, u32[]{:S(2)}) collective-permute-start(bf16[256,512]{1,0:T(8,128)(2,1)S(1)} %bitcast.66), channel_id=1, source_target_pairs={{0,8},{8,16},{16,24},{24,32},{32,40},{40,48},{48,56},{56,64},{64,7... | collective-permute-start | bytes 786440 | tf_op jit(solution)/shard_map/ppermute | solution.py:481
  8.5 2.7 %collective-permute-done.high_ref = bf16[256,512]{1,0:T(8,128)(2,1)S(1)} collective-permute-done((bf16[256,512]{1,0:T(8,128)(2,1)S(1)}, bf16[256,512]{1,0:T(8,128)(2,1)S(1)}, u32[]{:S(2)}, u32[]{:S(2)}) %collective-permute-start) | collective-permute-done | bytes 262176 | tf_op jit(solution)/shard_map/ppermute | solution.py:481
  13.4 3.5 %collective-permute-start.2 = (bf16[64,512]{1,0:T(8,128)(2,1)S(1)}, bf16[64,512]{1,0:T(8,128)(2,1)S(1)}, u32[]{:S(2)}, u32[]{:S(2)}) collective-permute-start(bf16[64,512]{1,0:T(8,128)(2,1)S(1)} %reshape.154), channel_id=1, source_target_pairs={{0,1},{1,2},{2,3},{3,4},{4,5},{5,6},{6,7},{7,0},{8,9},{9,10},{10,1... | collective-permute-start | bytes 196616 | tf_op jit(solution)/shard_map/ppermute | solution.py:476
  18.7 1.9 collective-permute-done.3.right_ref
  21.2 28.0 %enc_forward.1 = (bf16[256,512]{1,0:T(8,128)(2,1)}, bf16[256,512]{1,0:T(8,128)(2,1)}, bf16[8192,512]{1,0:T(8,128)(2,1)}, bf16[8192,512]{1,0:T(8,128)(2,1)}, bf16...) custom-call(s32[256,32]{1,0:T(8,128)} %select_select_fusion.idx_ref, s32[256,1]{1,0:T(8,128)} %copy.29.count_ref, ...), custom_call_target="tpu_custom_call" | custom-call | tf_op jit(solution)/shard_map/enc_forward/pallas_call | solution.py:145
  49.2 1.3 collective-permute-start.4
  50.5 4.9 %collective-permute-start.5 = (bf16[256,512]{1,0:T(8,128)(2,1)}, bf16[256,512]{1,0:T(8,128)(2,1)S(1)}, u32[]{:S(2)}, u32[]{:S(2)}) collective-permute-start(bf16[256,512]{1,0:T(8,128)(2,1)} %get-tuple-element.70.b0_ref), channel_id=1, source_target_pairs={{0,8},{8,16},{16,24},{24,32},{32,40},{40,48},{48,56},{56,64},{64,7... | collective-permute-start | bytes 786440 | tf_op jit(solution)/shard_map/ppermute | solution.py:481
  55.5 6.3 %enc_between.2.refs_0_ = bf16[8192,512]{1,0:T(8,128)(2,1)} custom-call(bf16[8192,512]{1,0:T(8,128)(2,1)} %get-tuple-element.71.normed_ref, bf16[512,512]{1,0:T(8,128)(2,1)} %out_ref.9), custom_call_target="tpu_custom_call" | custom-call | flops 2147483648 | bytes 8388608 | tf_op jit(solution)/shard_map/enc_between/pallas_call | solution.py:182
  62.5 1.5 collective-permute-start.6
  65.4 6.5 %enc_between.3.turned_ref = bf16[8192,512]{1,0:T(8,128)(2,1)} custom-call(bf16[8192,512]{1,0:T(8,128)(2,1)} %get-tuple-element.71.normed_ref, bf16[512,512]{1,0:T(8,128)(2,1)} %out_ref.9, bf16[8192,512]{1,0:T(8,128)(2,1)} %enc_between.2.refs_0_), custom_call_target="tpu_custom_call", output_to_operand_aliasing={{}: (2, {})} | custom-call | flops 2147483648 | bytes 8388608 | tf_op jit(solution)/shard_map/enc_between/pallas_call | solution.py:182
  71.9 2.0 collective-permute-done.9.b4_ref
  73.9 10.1 %decoder.1 = (bf16[512,512]{1,0:T(8,128)(2,1)}, bf16[1536,512]{1,0:T(8,128)(2,1)S(1)}, bf16[1536,512]{1,0:T(8,128)(2,1)S(1)}, bf16[1536,512]{1,0:T(8,128)(2,1)S(...) custom-call(s32[512,3]{1,0:T(8,128)S(1)} %copy.30.idx_ref, ...), custom_call_target="tpu_custom_call" | custom-call | tf_op jit(solution)/shard_map/decoder/pallas_call | solution.py:288
  85.7 2.7 %decoder_rest.1 = (f32[512,512]{1,0:T(8,128)S(1)}, bf16[512,512]{1,0:T(8,128)(2,1)S(1)}, bf16[512,512]{1,0:T(8,128)(2,1)S(1)}, bf16[768,512]{1,0:T(8,128)(2,1)S(1)}) custom-call(s32[3,512]{1,0:T(4,128)S(1)} %fusion.27.idx_row_ref, bf16[512,512]{1,0:T(8,128)(2,1)S(1)} %bitcast.56, bf16[512,512]{1,0:T(8,128)(2,1)S(1)} %bitcast.58, ...), custom_call_target="tpu_custom_call" | custom-call | flops 2818572288 | bytes 6291456 | tf_op jit(solution)/shard_map/decoder_rest/pallas_call | solution.py:326
  88.5 4.4 %collective-permute-done.10 = bf16[512,512]{1,0:T(8,128)(2,1)S(1)} collective-permute-done((bf16[512,512]{1,0:T(8,128)(2,1)S(1)}, bf16[512,512]{1,0:T(8,128)(2,1)S(1)}, u32[]{:S(2)}, u32[]{:S(2)}) %collective-permute-start.10) | collective-permute-done | bytes 524320 | tf_op jit(solution)/shard_map/ppermute | solution.py:476
  93.9 4.3 %collective-permute-start.14 = (bf16[256,512]{1,0:T(8,128)(2,1)}, bf16[256,512]{1,0:T(8,128)(2,1)}, u32[]{:S(2)}, u32[]{:S(2)}) collective-permute-start(bf16[256,512]{1,0:T(8,128)(2,1)} %get-tuple-element.115), channel_id=1, source_target_pairs={{0,8},{8,16},{16,24},{24,32},{32,40},{40,48},{48,56},{56,64},{64,7... | collective-permute-start | bytes 786440 | tf_op jit(solution)/shard_map/ppermute | solution.py:481
  98.2 1.5 collective-permute-start.15
  99.7 5.3 %collective-permute-start.12 = (bf16[256,512]{1,0:T(8,128)(2,1)}, bf16[256,512]{1,0:T(8,128)(2,1)}, u32[]{:S(2)}, u32[]{:S(2)}) collective-permute-start(bf16[256,512]{1,0:T(8,128)(2,1)} %get-tuple-element.88), channel_id=1, source_target_pairs={{0,7},{1,0},{2,1},{3,2},{4,3},{5,4},{6,5},{7,6},{8,15},{9,8},{10,9... | collective-permute-start | bytes 786440 | tf_op jit(solution)/shard_map/ppermute | solution.py:476
  106.6 2.1 collective-permute-done.13
  108.7 1.4 add_convert_fusion.2.moved_cot_ref
  110.8 30.8 %enc_backward.1 = (bf16[256,512]{1,0:T(8,128)(2,1)}, bf16[1152,512]{1,0:T(8,128)(2,1)}, bf16[1536,512]{1,0:T(8,128)(2,1)}) custom-call(s32[8,1,1024]{2,1,0:T(1,128)} %reshape.158.idx_row_ref, f32[256,32]{1,0:T(8,128)} %get-tuple-element.82.scale_ref, bf16[256,512]{1,0:T(8,128)(2,1)} %bitcast.64, bf16[256,512]{1,0:T(8,128)(2,1)} %copy-done.6, ...), custom_call_target="tpu_custom_call" | custom-call | tf_op jit(solution)/shard_map/enc_backward/pallas_call | solution.py:439
  141.6 2.0 broadcast_select_fusion
  143.6 2.2 collective-permute-start.16
  148.9 1.8 add_convert_fusion
  150.7 17.4 %all-to-all-start = ((bf16[64,24,512]{2,1,0:T(8,128)(2,1)}), bf16[64,24,512]{2,1,0:T(8,128)(2,1)}, u32[]{:S(2)}, u32[]{:S(2)}) async-start(bf16[64,24,512]{2,1,0:T(8,128)(2,1)} %bitcast.60), calls=%async_computation | async-start | bytes 3145728 | tf_op jit(solution)/shard_map/all_to_all | solution.py:491
  169.6 3.5 %collective-permute-start.19 = (bf16[256,512]{1,0:T(8,128)(2,1)}, bf16[256,512]{1,0:T(8,128)(2,1)}, u32[]{:S(2)}, u32[]{:S(2)}) collective-permute-start(bf16[256,512]{1,0:T(8,128)(2,1)} %bitcast.15), channel_id=1, source_target_pairs={{0,8},{8,16},{16,24},{24,32},{32,40},{40,48},{48,56},{56,64},{64,7... | collective-permute-start | bytes 786440 | tf_op jit(solution)/shard_map/ppermute | solution.py:481
  173.1 1.3 collective-permute-start.20
  174.4 16.3 %all-to-all-done = bf16[64,24,512]{2,1,0:T(8,128)(2,1)} async-done(((bf16[64,24,512]{2,1,0:T(8,128)(2,1)}), bf16[64,24,512]{2,1,0:T(8,128)(2,1)}, u32[]{:S(2)}, u32[]{:S(2)}) %all-to-all-start) | async-done | bytes 1572896 | tf_op jit(solution)/shard_map/all_to_all | solution.py:491
  190.7 1.7 reduce_sum.22
  192.5 30.2 %all_to_all.10 = bf16[64,24,512]{2,1,0:T(8,128)(2,1)S(1)} all-to-all(bf16[64,24,512]{2,1,0:T(8,128)(2,1)S(1)} %broadcast_in_dim.12), channel_id=1, replica_groups={{0,2,4,6,8,10,12,14,16,18,20,22,24,26,28,30,32,34,36,38,40,42,44,46,48,..., dimensions={0} | all-to-all | bytes 3145728 | tf_op jit(solution)/shard_map/all_to_all | solution.py:491
  222.7 3.4 %collective-permute-start.21 = (bf16[1536,512]{1,0:T(8,128)(2,1)S(1)}, bf16[1536,512]{1,0:T(8,128)(2,1)S(1)}, u32[]{:S(2)}, u32[]{:S(2)}) collective-permute-start(bf16[1536,512]{1,0:T(8,128)(2,1)S(1)} %bitcast.59), channel_id=1, source_target_pairs={{0,1},{1,0},{2,3},{3,2},{4,5},{5,4},{6,7},{7,6},{8,9},{9,8},{10,11... | collective-permute-start | bytes 4718600 | tf_op jit(solution)/shard_map/ppermute | solution.py:485
  229.6 2.7 %fusion.31 = (f32[512,512]{1,0:T(8,128)}, f32[512,512]{1,0:T(8,128)}, f32[512,512]{1,0:T(8,128)}, f32[512,512]{1,0:T(8,128)}, f32[512,512]{1,0:T(8,128)}, /*index=5*/f32[512,512]{1,0:T(8,128)}) fusion(f32[1536,512]{1,0:T(8,128)S(1)} %get-tuple-element.110, f32[1536,512]{1,0:T(8,128)S(1)} %get-tuple-element.111), kind=kLoop, calls=%fused_computation.89 | loop fusion | bytes 12582912 | tf_op jit(solution)/shard_map/slice | solution.py:628
  (94 shorter events, 21.6 us)
Async XLA Ops:
  0.6 17.2 %copy-start.15 = (s32[1,1,256,32]{2,3,1,0:T(8,128)S(1)}, s32[1,1,256,32]{2,3,1,0:T(8,128)}, u32[]{:S(2)}) copy-start(s32[1,1,256,32]{2,3,1,0:T(8,128)} %param.26) | copy-start | bytes 98308
  1.7 9.5 %collective-permute-start = (bf16[256,512]{1,0:T(8,128)(2,1)S(1)}, bf16[256,512]{1,0:T(8,128)(2,1)S(1)}, u32[]{:S(2)}, u32[]{:S(2)}) collective-permute-start(bf16[256,512]{1,0:T(8,128)(2,1)S(1)} %bitcast.67), channel_id=1, source_target_pairs={{8,0},{16,8},{24,16},{32,24},{40,32},{48,40},{56,48},{64,56},{72,6... | collective-permute-start | bytes 786440 | tf_op jit(solution)/shard_map/ppermute | solution.py:481
  3.0 9.0 %collective-permute-start.1 = (bf16[256,512]{1,0:T(8,128)(2,1)S(1)}, bf16[256,512]{1,0:T(8,128)(2,1)S(1)}, u32[]{:S(2)}, u32[]{:S(2)}) collective-permute-start(bf16[256,512]{1,0:T(8,128)(2,1)S(1)} %bitcast.66), channel_id=1, source_target_pairs={{0,8},{8,16},{16,24},{24,32},{32,40},{40,48},{48,56},{56,64},{64,7... | collective-permute-start | bytes 786440 | tf_op jit(solution)/shard_map/ppermute | solution.py:481
  11.2 9.4 %copy-start.7 = (bf16[256,512]{1,0:T(8,128)(2,1)}, bf16[256,512]{1,0:T(8,128)(2,1)S(1)}, u32[]{:S(2)}) copy-start(bf16[256,512]{1,0:T(8,128)(2,1)S(1)} %collective-permute-done.high_ref) | copy-start | bytes 786436
  12.1 8.5 %copy-start.8 = (bf16[256,512]{1,0:T(8,128)(2,1)}, bf16[256,512]{1,0:T(8,128)(2,1)S(1)}, u32[]{:S(2)}) copy-start(bf16[256,512]{1,0:T(8,128)(2,1)S(1)} %collective-permute-done.1.low_ref) | copy-start | bytes 786436
  13.4 5.3 %collective-permute-start.2 = (bf16[64,512]{1,0:T(8,128)(2,1)S(1)}, bf16[64,512]{1,0:T(8,128)(2,1)S(1)}, u32[]{:S(2)}, u32[]{:S(2)}) collective-permute-start(bf16[64,512]{1,0:T(8,128)(2,1)S(1)} %reshape.154), channel_id=1, source_target_pairs={{0,1},{1,2},{2,3},{3,4},{4,5},{5,6},{6,7},{7,0},{8,9},{9,10},{10,1... | collective-permute-start | bytes 196616 | tf_op jit(solution)/shard_map/ppermute | solution.py:476
  16.9 38.6 %copy-start.16 = (s32[3,8,64]{2,1,0:T(8,128)S(1)}, s32[3,8,64]{2,1,0:T(8,128)}, u32[]{:S(2)}) copy-start(s32[3,8,64]{2,1,0:T(8,128)} %param.27) | copy-start | bytes 18436
  16.9 3.7 %collective-permute-start.3 = (bf16[64,512]{1,0:T(8,128)(2,1)S(1)}, bf16[64,512]{1,0:T(8,128)(2,1)S(1)}, u32[]{:S(2)}, u32[]{:S(2)}) collective-permute-start(bf16[64,512]{1,0:T(8,128)(2,1)S(1)} %reshape.155), channel_id=1, source_target_pairs={{0,7},{1,0},{2,1},{3,2},{4,3},{5,4},{6,5},{7,6},{8,15},{9,8},{10,9... | collective-permute-start | bytes 196616 | tf_op jit(solution)/shard_map/ppermute | solution.py:476
  49.2 12.7 %collective-permute-start.4 = (bf16[256,512]{1,0:T(8,128)(2,1)}, bf16[256,512]{1,0:T(8,128)(2,1)S(1)}, u32[]{:S(2)}, u32[]{:S(2)}) collective-permute-start(bf16[256,512]{1,0:T(8,128)(2,1)} %get-tuple-element.70.b0_ref), channel_id=1, source_target_pairs={{8,0},{16,8},{24,16},{32,24},{40,32},{48,40},{56,48},{64,56},{72,6... | collective-permute-start | bytes 786440 | tf_op jit(solution)/shard_map/ppermute | solution.py:481
  50.5 11.4 %collective-permute-start.5 = (bf16[256,512]{1,0:T(8,128)(2,1)}, bf16[256,512]{1,0:T(8,128)(2,1)S(1)}, u32[]{:S(2)}, u32[]{:S(2)}) collective-permute-start(bf16[256,512]{1,0:T(8,128)(2,1)} %get-tuple-element.70.b0_ref), channel_id=1, source_target_pairs={{0,8},{8,16},{16,24},{24,32},{32,40},{40,48},{48,56},{56,64},{64,7... | collective-permute-start | bytes 786440 | tf_op jit(solution)/shard_map/ppermute | solution.py:481
  61.9 10.0 %collective-permute-start.7 = (bf16[512,512]{1,0:T(8,128)(2,1)S(1)}, bf16[512,512]{1,0:T(8,128)(2,1)S(1)}, u32[]{:S(2)}, u32[]{:S(2)}) collective-permute-start(bf16[512,512]{1,0:T(8,128)(2,1)S(1)} %pad_maximum_fusion.2.b1_ref), channel_id=1, source_target_pairs={{0,1},{1,2},{2,3},{3,4},{4,5},{5,6},{6,7},{7,0},{8,9},{9,10},{10,1... | collective-permute-start | bytes 1572872 | tf_op jit(solution)/shard_map/ppermute | solution.py:476
  62.2 9.7 %collective-permute-start.8 = (bf16[512,512]{1,0:T(8,128)(2,1)S(1)}, bf16[512,512]{1,0:T(8,128)(2,1)S(1)}, u32[]{:S(2)}, u32[]{:S(2)}) collective-permute-start(bf16[512,512]{1,0:T(8,128)(2,1)S(1)} %pad_maximum_fusion.2.b1_ref), channel_id=1, source_target_pairs={{0,7},{1,0},{2,1},{3,2},{4,3},{5,4},{6,5},{7,6},{8,15},{9,8},{10,9... | collective-permute-start | bytes 1572872 | tf_op jit(solution)/shard_map/ppermute | solution.py:476
  62.5 9.4 %collective-permute-start.6 = (bf16[256,512]{1,0:T(8,128)(2,1)S(1)}, bf16[256,512]{1,0:T(8,128)(2,1)S(1)}, u32[]{:S(2)}, u32[]{:S(2)}) collective-permute-start(bf16[256,512]{1,0:T(8,128)(2,1)S(1)} %copy-done.4), channel_id=1, source_target_pairs={{0,1},{1,2},{2,3},{3,4},{4,5},{5,6},{6,7},{7,0},{8,9},{9,10},{10,1... | collective-permute-start | bytes 786440 | tf_op jit(solution)/shard_map/ppermute | solution.py:476
  64.0 9.9 %collective-permute-start.9 = (bf16[256,512]{1,0:T(8,128)(2,1)S(1)}, bf16[256,512]{1,0:T(8,128)(2,1)S(1)}, u32[]{:S(2)}, u32[]{:S(2)}) collective-permute-start(bf16[256,512]{1,0:T(8,128)(2,1)S(1)} %copy-done.4), channel_id=1, source_target_pairs={{0,7},{1,0},{2,1},{3,2},{4,3},{5,4},{6,5},{7,6},{8,15},{9,8},{10,9... | collective-permute-start | bytes 786440 | tf_op jit(solution)/shard_map/ppermute | solution.py:476
  65.4 8.5 %copy-start = (bf16[8,64,512]{2,1,0:T(8,128)(2,1)S(1)}, bf16[8,64,512]{2,1,0:T(8,128)(2,1)}, u32[]{:S(2)}) copy-start(bf16[8,64,512]{2,1,0:T(8,128)(2,1)} %param.16) | copy-start | bytes 1572868
  65.4 8.5 %copy-start.1 = (bf16[512,512]{1,0:T(8,128)(2,1)S(1)}, bf16[512,512]{1,0:T(8,128)(2,1)}, u32[]{:S(2)}) copy-start(bf16[512,512]{1,0:T(8,128)(2,1)} %out_ref.8) | copy-start | bytes 1572868
  65.4 8.5 %copy-start.2 = (bf16[8,64,512]{2,1,0:T(8,128)(2,1)S(1)}, bf16[8,64,512]{2,1,0:T(8,128)(2,1)}, u32[]{:S(2)}) copy-start(bf16[8,64,512]{2,1,0:T(8,128)(2,1)} %param.18) | copy-start | bytes 1572868
  84.0 8.9 %collective-permute-start.10 = (bf16[512,512]{1,0:T(8,128)(2,1)S(1)}, bf16[512,512]{1,0:T(8,128)(2,1)S(1)}, u32[]{:S(2)}, u32[]{:S(2)}) collective-permute-start(bf16[512,512]{1,0:T(8,128)(2,1)S(1)} %get-tuple-element.84), channel_id=1, source_target_pairs={{0,7},{1,0},{2,1},{3,2},{4,3},{5,4},{6,5},{7,6},{8,15},{9,8},{10,9... | collective-permute-start | bytes 1572872 | tf_op jit(solution)/shard_map/ppermute | solution.py:476
  84.9 8.0 %collective-permute-start.11 = (bf16[512,512]{1,0:T(8,128)(2,1)S(1)}, bf16[512,512]{1,0:T(8,128)(2,1)S(1)}, u32[]{:S(2)}, u32[]{:S(2)}) collective-permute-start(bf16[512,512]{1,0:T(8,128)(2,1)S(1)} %get-tuple-element.85), channel_id=1, source_target_pairs={{0,1},{1,2},{2,3},{3,4},{4,5},{5,6},{6,7},{7,0},{8,9},{9,10},{10,1... | collective-permute-start | bytes 1572872 | tf_op jit(solution)/shard_map/ppermute | solution.py:476
  88.5 16.6 %copy-start.14 = (s32[1,1,256,32]{2,3,1,0:T(8,128)S(1)}, s32[1,1,256,32]{2,3,1,0:T(8,128)}, u32[]{:S(2)}) copy-start(s32[1,1,256,32]{2,3,1,0:T(8,128)} %param.25) | copy-start | bytes 98308
  92.9 17.2 %copy-start.13 = (bf16[256,512]{1,0:T(8,128)(2,1)S(1)}, bf16[256,512]{1,0:T(8,128)(2,1)}, u32[]{:S(2)}) copy-start(bf16[256,512]{1,0:T(8,128)(2,1)} %get-tuple-element.97) | copy-start | bytes 786436
  93.9 12.3 %collective-permute-start.14 = (bf16[256,512]{1,0:T(8,128)(2,1)}, bf16[256,512]{1,0:T(8,128)(2,1)}, u32[]{:S(2)}, u32[]{:S(2)}) collective-permute-start(bf16[256,512]{1,0:T(8,128)(2,1)} %get-tuple-element.115), channel_id=1, source_target_pairs={{0,8},{8,16},{16,24},{24,32},{32,40},{40,48},{48,56},{56,64},{64,7... | collective-permute-start | bytes 786440 | tf_op jit(solution)/shard_map/ppermute | solution.py:481
  98.2 8.0 %collective-permute-start.15 = (bf16[256,512]{1,0:T(8,128)(2,1)}, bf16[256,512]{1,0:T(8,128)(2,1)}, u32[]{:S(2)}, u32[]{:S(2)}) collective-permute-start(bf16[256,512]{1,0:T(8,128)(2,1)} %get-tuple-element.116), channel_id=1, source_target_pairs={{8,0},{16,8},{24,16},{32,24},{40,32},{48,40},{56,48},{64,56},{72,6... | collective-permute-start | bytes 786440 | tf_op jit(solution)/shard_map/ppermute | solution.py:481
  99.7 6.9 %collective-permute-start.12 = (bf16[256,512]{1,0:T(8,128)(2,1)}, bf16[256,512]{1,0:T(8,128)(2,1)}, u32[]{:S(2)}, u32[]{:S(2)}) collective-permute-start(bf16[256,512]{1,0:T(8,128)(2,1)} %get-tuple-element.88), channel_id=1, source_target_pairs={{0,7},{1,0},{2,1},{3,2},{4,3},{5,4},{6,5},{7,6},{8,15},{9,8},{10,9... | collective-permute-start | bytes 786440 | tf_op jit(solution)/shard_map/ppermute | solution.py:476
  105.1 3.6 %collective-permute-start.13 = (bf16[256,512]{1,0:T(8,128)(2,1)}, bf16[256,512]{1,0:T(8,128)(2,1)}, u32[]{:S(2)}, u32[]{:S(2)}) collective-permute-start(bf16[256,512]{1,0:T(8,128)(2,1)} %get-tuple-element.89), channel_id=1, source_target_pairs={{0,1},{1,2},{2,3},{3,4},{4,5},{5,6},{6,7},{7,0},{8,9},{9,10},{10,1... | collective-permute-start | bytes 786440 | tf_op jit(solution)/shard_map/ppermute | solution.py:476
  143.6 5.3 %collective-permute-start.16 = (bf16[1536,512]{1,0:T(8,128)(2,1)S(1)}, bf16[1536,512]{1,0:T(8,128)(2,1)S(1)}, u32[]{:S(2)}, u32[]{:S(2)}) collective-permute-start(bf16[1536,512]{1,0:T(8,128)(2,1)S(1)} %broadcast_select_fusion), channel_id=1, source_target_pairs={{0,1},{1,0},{2,3},{3,2},{4,5},{5,4},{6,7},{7,6},{8,9},{9,8},{10,11... | collective-permute-start | bytes 4718600 | tf_op jit(solution)/shard_map/ppermute | solution.py:485
  145.9 4.8 %collective-permute-start.17 = (bf16[64,512]{1,0:T(8,128)(2,1)S(1)}, bf16[64,512]{1,0:T(8,128)(2,1)S(1)}, u32[]{:S(2)}, u32[]{:S(2)}) collective-permute-start(bf16[64,512]{1,0:T(8,128)(2,1)S(1)} %get-tuple-element.118), channel_id=1, source_target_pairs={{0,7},{1,0},{2,1},{3,2},{4,3},{5,4},{6,5},{7,6},{8,15},{9,8},{10,9... | collective-permute-start | bytes 196616 | tf_op jit(solution)/shard_map/ppermute | solution.py:476
  146.6 4.1 %collective-permute-start.18 = (bf16[64,512]{1,0:T(8,128)(2,1)S(1)}, bf16[64,512]{1,0:T(8,128)(2,1)S(1)}, u32[]{:S(2)}, u32[]{:S(2)}) collective-permute-start(bf16[64,512]{1,0:T(8,128)(2,1)S(1)} %get-tuple-element.117), channel_id=1, source_target_pairs={{0,1},{1,2},{2,3},{3,4},{4,5},{5,6},{6,7},{7,0},{8,9},{9,10},{10,1... | collective-permute-start | bytes 196616 | tf_op jit(solution)/shard_map/ppermute | solution.py:476
  150.7 40.0 %all-to-all-start = ((bf16[64,24,512]{2,1,0:T(8,128)(2,1)}), bf16[64,24,512]{2,1,0:T(8,128)(2,1)}, u32[]{:S(2)}, u32[]{:S(2)}) async-start(bf16[64,24,512]{2,1,0:T(8,128)(2,1)} %bitcast.60), calls=%async_computation | async-start | bytes 3145728 | tf_op jit(solution)/shard_map/all_to_all | solution.py:491
  169.6 22.8 %collective-permute-start.19 = (bf16[256,512]{1,0:T(8,128)(2,1)}, bf16[256,512]{1,0:T(8,128)(2,1)}, u32[]{:S(2)}, u32[]{:S(2)}) collective-permute-start(bf16[256,512]{1,0:T(8,128)(2,1)} %bitcast.15), channel_id=1, source_target_pairs={{0,8},{8,16},{16,24},{24,32},{32,40},{40,48},{48,56},{56,64},{64,7... | collective-permute-start | bytes 786440 | tf_op jit(solution)/shard_map/ppermute | solution.py:481
  173.1 19.3 %collective-permute-start.20 = (bf16[256,512]{1,0:T(8,128)(2,1)S(1)}, bf16[256,512]{1,0:T(8,128)(2,1)}, u32[]{:S(2)}, u32[]{:S(2)}) collective-permute-start(bf16[256,512]{1,0:T(8,128)(2,1)S(1)} %bitcast.68), channel_id=1, source_target_pairs={{8,0},{16,8},{24,16},{32,24},{40,32},{48,40},{56,48},{64,56},{72,6... | collective-permute-start | bytes 786440 | tf_op jit(solution)/shard_map/ppermute | solution.py:481
  222.7 6.5 %collective-permute-start.21 = (bf16[1536,512]{1,0:T(8,128)(2,1)S(1)}, bf16[1536,512]{1,0:T(8,128)(2,1)S(1)}, u32[]{:S(2)}, u32[]{:S(2)}) collective-permute-start(bf16[1536,512]{1,0:T(8,128)(2,1)S(1)} %bitcast.59), channel_id=1, source_target_pairs={{0,1},{1,0},{2,3},{3,2},{4,5},{5,4},{6,7},{7,6},{8,9},{9,8},{10,11... | collective-permute-start | bytes 4718600 | tf_op jit(solution)/shard_map/ppermute | solution.py:485
  (8 other events, 35.0 us)
